TPU v7x, 256 devices: a whole 4x4x8 slice. The times are simulated.
256 devices in a mesh: row: 32 (over x, y, z_lo), ma: 8 (over z_hi, core).
Axes of the slice: x: 4, y: 4, z: 8 (z_hi: 4, z_lo: 2; z = z_hi * 2 + z_lo), core: 2. Of those that a mesh axis runs over, the one named last changes fastest.
Arguments:
- coeffs: bfloat16 [64, 12, 136, 4096], P('row', None, 'ma'), may hold values from -6 to 6
- legendre: bfloat16 [136, 64, 2048], P('ma'), may hold values from -0.1875 to 0.1875
- lat_weights: float32 [32], replicated, may hold values from 4 to 16
- m_blocks: int32 [16], replicated, may hold values from 0 to 15, as said below
Outputs:
- nonlinear: bfloat16 [64, 8, 136, 4096], P('row', None, 'ma')
- radial_slope: bfloat16 [64, 8, 136, 4096], P('row', None, 'ma')
Inputs may be any that keep to these rules, and one draw needn't show every extreme that they name: `m_blocks`: each of the 16 order blocks appears once; entries 2p and 2p + 1 always sum to 15.
All inputs are finite; a program needn't handle non-finite values.
Results may differ from a plain program's by a relative error of at most 0.017.
Values may be sent and summed in bfloat16 or wider, within the bound.
No kernel may reach another device: no remote copies, remote signals or barrier semaphores. Data moves between devices by JAX's collectives and lax.ppermute only.
A program may use at most 128 MiB of HBM per device.

v0:
```python
import math

import jax
import jax.numpy as jnp
from jax import lax
from jax.sharding import PartitionSpec as P

PHI_POINTS = 3072


def with_halo(block, sides, width):
    for axis, dim in sides:
        count = lax.axis_size(axis)
        forward = [(i, i + 1) for i in range(count - 1)]
        backward = [(target, source) for source, target in forward]
        low = lax.ppermute(
            lax.slice_in_dim(block, block.shape[dim] - width, None, axis=dim), axis, forward
        )
        high = lax.ppermute(lax.slice_in_dim(block, 0, width, axis=dim), axis, backward)
        block = jnp.concatenate([low, block, high], axis=dim)
    return block


def block_lookup(blocks, wanted):
    indices = jnp.arange(blocks.shape[0], dtype=jnp.int32)
    return jnp.sum(jnp.where(indices[None, :] == wanted[:, None], blocks[None, :], 0), axis=1)


def slot_positions(listed, slot_total, span):
    slot_ids = jnp.arange(slot_total, dtype=jnp.int32)
    pair_index = slot_ids // span
    offsets = slot_ids % span
    leading = block_lookup(listed, 2 * pair_index)
    return 2 * pair_index + (offsets >= span - 1 - leading).astype(jnp.int32)


def azimuth_pair(blocks, block, points):
    columns = jnp.arange(blocks.shape[0] * block, dtype=jnp.int32)
    block_base = block_lookup(blocks, columns // block)
    orders = block_base * block + columns % block
    phases = orders[:, None] * jnp.arange(points, dtype=jnp.int32)[None, :] % points
    angles = phases.astype(jnp.float32) * (2.0 * math.pi / points)
    cosine = jnp.cos(angles)
    sine = -jnp.sin(angles)
    cos_high = cosine.astype(jnp.bfloat16)
    sin_high = sine.astype(jnp.bfloat16)
    cos_low = (cosine - cos_high.astype(jnp.float32)).astype(jnp.bfloat16)
    sin_low = (sine - sin_high.astype(jnp.float32)).astype(jnp.bfloat16)
    return (jnp.stack([cos_high, sin_high]), jnp.stack([cos_low, sin_low]))


def induction_terms(velocity, magnetic):
    return [
        velocity[1] * magnetic[2] - velocity[2] * magnetic[1],
        velocity[2] * magnetic[0] - velocity[0] * magnetic[2],
        velocity[0] * magnetic[1] - velocity[1] * magnetic[0],
        0.5 * (magnetic[0] * magnetic[0] + magnetic[1] * magnetic[1] + magnetic[2] * magnetic[2]),
    ]


def analyse(lat_rows, legendre_table, positions):
    lat_all, number_items, channels, columns = lat_rows.shape
    block = legendre_table.shape[1]
    owned = columns // block
    arranged = lat_rows.reshape(lat_all, number_items * channels, owned, block).transpose(
        2, 3, 1, 0
    )
    per_slot = jnp.take(arranged, positions, axis=0)
    result = lax.dot_general(
        legendre_table,
        per_slot,
        (((3,), (3,)), ((0, 1), (0, 1))),
        preferred_element_type=jnp.float32,
    )
    return result.transpose(3, 0, 1, 2).reshape(
        number_items, channels, legendre_table.shape[0], block * block
    )


def radial_stencil(padded, shells):
    return (
        padded[0:shells]
        - 8.0 * padded[1 : shells + 1]
        + 8.0 * padded[3 : shells + 3]
        - padded[4 : shells + 4]
    ) / 12.0


def local(coeffs, legendre, lat_weights, m_blocks):
    shells = coeffs.shape[0]
    slot_dev = coeffs.shape[2]
    block = legendre.shape[1]
    lat_all = legendre.shape[2] // block
    groups = lax.axis_size("ma")
    lat_dev = lat_all // groups
    block_total = m_blocks.shape[0]
    owned = block_total // groups
    degrees = block_total * block
    own_index = lax.axis_index("ma")
    own_list = lax.dynamic_slice_in_dim(m_blocks, own_index * owned, owned)
    positions = slot_positions(own_list, slot_dev, block_total + 1)
    legendre_table = legendre.reshape(slot_dev, block, block, lat_all)
    basis_high, basis_low = azimuth_pair(m_blocks, block, PHI_POINTS)
    weights_here = lax.dynamic_slice_in_dim(lat_weights, own_index * lat_dev, lat_dev)
    inv_width = 1.0 / math.sqrt(degrees)
    inv_points = 1.0 / math.sqrt(PHI_POINTS)
    spectra = coeffs.reshape(shells * 12, slot_dev, block, block)
    partial_value = lax.dot_general(
        spectra,
        legendre_table,
        (((3,), (2,)), ((1, 2), (0, 1))),
        preferred_element_type=jnp.float32,
    )
    summed = jax.ops.segment_sum(partial_value, positions, num_segments=owned)
    grouped = summed.transpose(3, 2, 0, 1)
    lat_major = grouped.reshape(lat_all, shells, 12, owned * block).astype(jnp.bfloat16)
    piece = lax.all_to_all(lat_major, "ma", split_axis=0, concat_axis=3, tiled=True)
    cycles = piece.shape[0]
    number_items = piece.shape[1]
    lat_values = piece.reshape(cycles, number_items, 6, 2, degrees)
    field_grid = (
        jnp.einsum("tnfcm,cmp->tnfp", lat_values, basis_high, preferred_element_type=jnp.float32)
        + jnp.einsum("tnfcm,cmp->tnfp", lat_values, basis_low, preferred_element_type=jnp.float32)
    ) * inv_width
    components = [field_grid[:, :, index] for index in range(6)]
    products = jnp.stack(induction_terms(components[0:3], components[3:6]), axis=2)
    product_high = products.astype(jnp.bfloat16)
    product_low = (products - product_high.astype(jnp.float32)).astype(jnp.bfloat16)
    spectral_out = (
        jnp.einsum("tngp,cmp->tngcm", product_high, basis_high, preferred_element_type=jnp.float32)
        + jnp.einsum("tngp,cmp->tngcm", product_high, basis_low, preferred_element_type=jnp.float32)
        + jnp.einsum("tngp,cmp->tngcm", product_low, basis_high, preferred_element_type=jnp.float32)
    ) * inv_points
    spectral_out = spectral_out * weights_here[:, None, None, None, None]
    spectral_out = spectral_out.astype(jnp.bfloat16).reshape(cycles, number_items, 8, degrees)
    lat_back = lax.all_to_all(spectral_out, "ma", split_axis=3, concat_axis=0, tiled=True)
    analysed = analyse(lat_back, legendre_table, positions)
    nonlinear = analysed.astype(jnp.bfloat16)
    padded = with_halo(analysed, (("row", 0),), 2)
    radial_slope = radial_stencil(padded, shells).astype(jnp.bfloat16)
    return (nonlinear, radial_slope)


def solution(mesh):
    placed = (P("row", None, "ma", None), P("ma", None, None), P(), P())
    return jax.shard_map(
        local,
        mesh=mesh,
        in_specs=placed,
        out_specs=(P("row", None, "ma", None), P("row", None, "ma", None)),
        check_vma=False,
    )
```

profile of v0, /device:TPU:6, one launch (start us, length us, event | category | flops | bytes accessed | tf_op | source)
XLA Modules:
  0.0 441.8 jit_solution(7176818943975603104)
XLA Ops:
  1.5 9.1 %copy.65 = bf16[17,64,2048]{1,2,0:T(8,128)(2,1)} copy(bf16[17,64,2048]{2,1,0:T(8,128)(2,1)} %param.5) | data formatting | bytes 8912896 | tf_op args[1]
  10.6 16.8 %copy.67 = bf16[17,64,64,32]{2,3,1,0:T(8,128)(2,1)} copy(bf16[17,64,64,32]{1,3,2,0:T(8,128)(2,1)} %bitcast.94) | data formatting | bytes 8912896 | tf_op jit(solution)/shard_map/reshape | solution.py:102
  27.3 4.8 %copy.64 = bf16[2,12,17,4096]{3,1,0,2:T(8,128)(2,1)} copy(bf16[2,12,17,4096]{3,0,2,1:T(2,128)(2,1)S(1)} %copy-done) | data formatting | bytes 6684672 | tf_op args[0]
  32.1 10.5 %reshape.287 = bf16[24,17,64,64]{3,2,0,1:T(8,128)(2,1)} reshape(bf16[2,12,17,4096]{3,1,0,2:T(8,128)(2,1)} %copy.64) | data formatting | bytes 6684672 | tf_op jit(solution)/shard_map/reshape | solution.py:107
  42.6 10.9 %fusion.10 = f32[17,64,24,32]{3,2,1,0:T(8,128)} fusion(bf16[17,64,64,32]{2,3,1,0:T(8,128)(2,1)} %copy.67, bf16[24,17,64,64]{3,2,0,1:T(8,128)(2,1)} %reshape.287), kind=kOutput, calls=%fused_computation.19 | convolution fusion | flops 106954752 | bytes 11141120 | tf_op jit(solution)/shard_map/dot_general | solution.py:108
  53.5 11.9 %copy.68 = f32[17,64,24,32]{1,3,2,0:T(8,128)} copy(f32[17,64,24,32]{3,2,1,0:T(8,128)} %fusion.10) | data formatting | bytes 6684672 | tf_op jit(solution)/shard_map/dot_general | solution.py:108
  65.5 10.8 %scatter_fusion = f32[2,64,24,32]{1,3,2,0:T(8,128)S(1)} fusion(f32[2,64,24,32]{1,3,2,0:T(8,128)S(1)} %broadcast_in_dim.50, s32[17]{0:T(128)S(1)} %get-tuple-element.21, f32[17,64,24,32]{1,3,2,0:T(8,128)} %copy.68), kind=kCustom, calls=%fused_computation.1 | custom fusion | flops 835584 | bytes 10027076 | tf_op jit(solution)/shard_map/scatter-add | solution.py:114
  77.9 18.8 %all-to-all-start = ((bf16[32,2,12,128]{3,1,2,0:T(2,128)(2,1)}), bf16[32,2,12,128]{3,1,2,0:T(2,128)(2,1)S(1)}, u32[]{:S(2)}, u32[]{:S(2)}) async-start(bf16[32,2,12,128]{3,1,2,0:T(2,128)(2,1)} %copy.70), calls=%async_computation | async-start | bytes 393216 | tf_op jit(solution)/shard_map/all_to_all | solution.py:117
  96.9 58.6 %subtract_convert_fusion.1 = (bf16[1,1024,3072]{2,1,0:T(8,128)(2,1)}, bf16[1,1024,3072]{2,1,0:T(8,128)(2,1)}, bf16[1,1024,3072]{2,1,0:T(8,128)(2,1)}, bf16[1,1024,3072]{2,1,0:T(8,128)(2,1)}) fusion(s32[1024]{0:T(1024)S(1)} %fusion.45), kind=kLoop, calls=%fused_computation.8 | loop fusion | flops 56623104 | bytes 25169920 | tf_op jit(solution)/shard_map/convert_element_type | solution.py:47
  155.7 6.2 %fusion.24 = f32[4,2,6,3072]{3,2,1,0:T(8,128)S(1)} fusion(bf16[1,1024,3072]{2,1,0:T(8,128)(2,1)} %get-tuple-element.18, bf16[1,1024,3072]{2,1,0:T(8,128)(2,1)} %get-tuple-element.16, bf16[4,2,6,2,1024]{4,3,2,1,0:T(2,128)(2,1)S(1)} %reshape.289), kind=kOutput, calls=%fused_computation.35 | convolution fusion | flops 610271232 | bytes 13369344 | tf_op jit(solution)/shard_map/tnfcm,cmp->tnfp/dot_general | solution.py:123
  162.1 7.1 %fusion.25 = f32[4,2,6,3072]{3,2,1,0:T(8,128)S(1)} fusion(f32[4,2,6,3072]{3,2,1,0:T(8,128)S(1)} %fusion.24, bf16[1,1024,3072]{2,1,0:T(8,128)(2,1)S(1)} %bitcast.98, bf16[1,1024,3072]{2,1,0:T(8,128)(2,1)} %get-tuple-element.19, bf16[4,2,6,2,1024]{4,3,2,1,0:T(2,128)(2,1)S(1)} %reshape.289), kind=kOutput, calls=%fused_computation.36 | convolution fusion | flops 610566144 | bytes 13959168 | tf_op jit(solution)/shard_map/tnfcm,cmp->tnfp/dot_general | solution.py:122
  169.9 4.0 fusion.8
  174.0 4.0 fusion.19
  178.0 4.0 fusion.29
  182.2 1.4 copy.75
  183.6 2.8 reshape.315
  186.4 7.2 %all-to-all-start.1 = ((bf16[8,2,4096]{2,1,0:T(2,128)(2,1)}), bf16[8,2,4096]{2,1,0:T(2,128)(2,1)S(1)}, u32[]{:S(2)}, u32[]{:S(2)}) async-start(bf16[8,2,4096]{2,1,0:T(2,128)(2,1)} %reshape.315), calls=%async_computation.1 | async-start | bytes 262144 | tf_op jit(solution)/shard_map/all_to_all | solution.py:136
  193.6 9.6 %all-to-all-done.1 = bf16[8,2,4096]{2,1,0:T(2,128)(2,1)S(1)} async-done(((bf16[8,2,4096]{2,1,0:T(2,128)(2,1)}), bf16[8,2,4096]{2,1,0:T(2,128)(2,1)S(1)}, u32[]{:S(2)}, u32[]{:S(2)}) %all-to-all-start.1) | async-done | bytes 131104 | tf_op jit(solution)/shard_map/all_to_all | solution.py:136
  203.2 2.4 reshape.316
  205.7 1.2 copy.76
  208.1 1.6 broadcast_select_fusion
  209.7 6.4 %copy.78 = bf16[17,64,16,32]{3,2,1,0:T(8,128)(2,1)} copy(bf16[17,64,16,32]{1,3,2,0:T(8,128)(2,1)} %broadcast_select_fusion) | data formatting | bytes 2228224 | tf_op jit(solution)/shard_map/jit(_take)/select_n | solution.py:68
  216.1 7.3 %convolution_bitcast_fusion = f32[16,17,64,64]{3,0,2,1:T(8,128)S(1)} fusion(bf16[17,64,16,32]{3,2,1,0:T(8,128)(2,1)} %copy.78, bf16[17,64,64,32]{2,3,1,0:T(8,128)(2,1)} %copy.67), kind=kOutput, calls=%fused_computation.37 | convolution fusion | flops 71303168 | bytes 10027008 | tf_op jit(solution)/shard_map/dot_general | solution.py:69
  223.5 6.3 %copy.80 = f32[16,17,64,64]{3,2,0,1:T(8,128)} copy(f32[16,17,64,64]{3,0,2,1:T(8,128)S(1)} %convolution_bitcast_fusion) | data formatting | bytes 8912896 | tf_op jit(solution)/shard_map/transpose | solution.py:75
  229.8 8.1 %reshape.292 = f32[2,8,17,4096]{3,1,0,2:T(8,128)} reshape(f32[16,17,64,64]{3,2,0,1:T(8,128)} %copy.80) | data formatting | bytes 8912896 | tf_op jit(solution)/shard_map/reshape | solution.py:75
  237.9 2.9 collective-permute-start
  240.8 5.9 %collective-permute-start.1 = (f32[2,8,17,4096]{3,1,0,2:T(8,128)}, f32[2,8,17,4096]{3,1,0,2:T(8,128)S(1)}, u32[]{:S(2)}, u32[]{:S(2)}) collective-permute-start(f32[2,8,17,4096]{3,1,0,2:T(8,128)} %reshape.292), channel_id=1, source_target_pairs={{8,0},{16,8},{24,16},{32,24},{40,32},{48,40},{56,48},{64,56},{72,6... | collective-permute-start | bytes 13369352 | tf_op jit(solution)/shard_map/ppermute | solution.py:19
  246.8 95.4 %collective-permute-done = f32[2,8,17,4096]{3,1,0,2:T(8,128)S(1)} collective-permute-done((f32[2,8,17,4096]{3,1,0,2:T(8,128)}, f32[2,8,17,4096]{3,1,0,2:T(8,128)S(1)}, u32[]{:S(2)}, u32[]{:S(2)}) %collective-permute-start) | collective-permute-done | bytes 4456480 | tf_op jit(solution)/shard_map/ppermute | solution.py:16
  342.1 91.4 %collective-permute-done.1 = f32[2,8,17,4096]{3,1,0,2:T(8,128)S(1)} collective-permute-done((f32[2,8,17,4096]{3,1,0,2:T(8,128)}, f32[2,8,17,4096]{3,1,0,2:T(8,128)S(1)}, u32[]{:S(2)}, u32[]{:S(2)}) %collective-permute-start.1) | collective-permute-done | bytes 4456480 | tf_op jit(solution)/shard_map/ppermute | solution.py:19
  433.5 4.9 %fusion.16 = (bf16[2,8,17,4096]{3,1,0,2:T(8,128)(2,1)S(1)}, bf16[2,8,17,4096]{3,1,0,2:T(8,128)(2,1)S(1)}) fusion(f32[2,8,17,4096]{3,1,0,2:T(8,128)S(1)} %collective-permute-done.1, f32[2,8,17,4096]{3,1,0,2:T(8,128)} %reshape.292, f32[2,8,17,4096]{3,1,0,2:T(8,128)S(1)} %collective-permute-done), kind=kLoop, calls=%fused_computation.26 | loop fusion | flops 11141120 | bytes 17825792 | tf_op jit(solution)/shard_map/convert_element_type | solution.py:140
  438.4 1.5 copy.81
  440.0 1.5 copy.82
  (49 shorter events, 5.0 us)
Async XLA Ops:
  10.6 16.8 %copy-start = (bf16[2,12,17,4096]{3,0,2,1:T(2,128)(2,1)S(1)}, bf16[2,12,17,4096]{3,0,2,1:T(2,128)(2,1)}, u32[]{:S(2)}) copy-start(bf16[2,12,17,4096]{3,0,2,1:T(2,128)(2,1)} %param.4) | copy-start | bytes 10027012
  65.5 31.3 %copy-start.1 = (s32[16]{0:T(128)S(1)}, s32[16]{0:T(128)}, u32[]{:S(2)}) copy-start(s32[16]{0:T(128)} %param.7) | copy-start | bytes 196
  77.9 77.6 %all-to-all-start = ((bf16[32,2,12,128]{3,1,2,0:T(2,128)(2,1)}), bf16[32,2,12,128]{3,1,2,0:T(2,128)(2,1)S(1)}, u32[]{:S(2)}, u32[]{:S(2)}) async-start(bf16[32,2,12,128]{3,1,2,0:T(2,128)(2,1)} %copy.70), calls=%async_computation | async-start | bytes 393216 | tf_op jit(solution)/shard_map/all_to_all | solution.py:117
  96.9 58.6 %copy-start.2 = (f32[32]{0:T(128)S(1)}, f32[32]{0:T(128)}, u32[]{:S(2)}) copy-start(f32[32]{0:T(128)} %param.6) | copy-start | bytes 388
  155.6 6.3 %slice-start = ((s8[6291456]{0:T(1024)(128)(4,1)}), s8[2097152]{0:T(1024)(128)(4,1)S(1)}, s32[]{:S(2)}) async-start(s8[6291456]{0:T(1024)(128)(4,1)} %bitcast.97), calls=%async_computation.2 | async-start | bytes 4194304
  155.7 6.4 %slice-start.1 = ((s8[6291456]{0:T(1024)(128)(4,1)}), s8[4194304]{0:T(1024)(128)(4,1)S(1)}, s32[]{:S(2)}) async-start(s8[6291456]{0:T(1024)(128)(4,1)} %bitcast.97), calls=%async_computation.3 | async-start | bytes 8388608
  155.7 14.2 %slice-start.4 = ((s8[6291456]{0:T(1024)(128)(4,1)}), s8[4194304]{0:T(1024)(128)(4,1)S(1)}, s32[]{:S(2)}) async-start(s8[6291456]{0:T(1024)(128)(4,1)} %bitcast.101), calls=%async_computation.6 | async-start | bytes 8388608
  155.7 14.2 %slice-start.6 = ((s8[6291456]{0:T(1024)(128)(4,1)}), s8[4194304]{0:T(1024)(128)(4,1)S(1)}, s32[]{:S(2)}) async-start(s8[6291456]{0:T(1024)(128)(4,1)} %bitcast.103), calls=%async_computation.8 | async-start | bytes 8388608
  162.1 7.8 %slice-start.5 = ((s8[6291456]{0:T(1024)(128)(4,1)}), s8[2097152]{0:T(1024)(128)(4,1)S(1)}, s32[]{:S(2)}) async-start(s8[6291456]{0:T(1024)(128)(4,1)} %bitcast.101), calls=%async_computation.7 | async-start | bytes 4194304
  162.1 7.8 %slice-start.7 = ((s8[6291456]{0:T(1024)(128)(4,1)}), s8[2097152]{0:T(1024)(128)(4,1)S(1)}, s32[]{:S(2)}) async-start(s8[6291456]{0:T(1024)(128)(4,1)} %bitcast.103), calls=%async_computation.9 | async-start | bytes 4194304
  162.1 11.9 %slice-start.2 = ((s8[6291456]{0:T(1024)(128)(4,1)}), s8[4194304]{0:T(1024)(128)(4,1)S(1)}, s32[]{:S(2)}) async-start(s8[6291456]{0:T(1024)(128)(4,1)} %bitcast.99), calls=%async_computation.4 | async-start | bytes 8388608
  169.9 4.1 slice-start.3
  186.4 16.8 %all-to-all-start.1 = ((bf16[8,2,4096]{2,1,0:T(2,128)(2,1)}), bf16[8,2,4096]{2,1,0:T(2,128)(2,1)S(1)}, u32[]{:S(2)}, u32[]{:S(2)}) async-start(bf16[8,2,4096]{2,1,0:T(2,128)(2,1)} %reshape.315), calls=%async_computation.1 | async-start | bytes 262144 | tf_op jit(solution)/shard_map/all_to_all | solution.py:136
  237.9 104.2 %collective-permute-start = (f32[2,8,17,4096]{3,1,0,2:T(8,128)}, f32[2,8,17,4096]{3,1,0,2:T(8,128)S(1)}, u32[]{:S(2)}, u32[]{:S(2)}) collective-permute-start(f32[2,8,17,4096]{3,1,0,2:T(8,128)} %reshape.292), channel_id=1, source_target_pairs={{0,8},{8,16},{16,24},{24,32},{32,40},{40,48},{48,56},{56,64},{64,7... | collective-permute-start | bytes 13369352 | tf_op jit(solution)/shard_map/ppermute | solution.py:16
  240.8 192.7 %collective-permute-start.1 = (f32[2,8,17,4096]{3,1,0,2:T(8,128)}, f32[2,8,17,4096]{3,1,0,2:T(8,128)S(1)}, u32[]{:S(2)}, u32[]{:S(2)}) collective-permute-start(f32[2,8,17,4096]{3,1,0,2:T(8,128)} %reshape.292), channel_id=1, source_target_pairs={{8,0},{16,8},{24,16},{32,24},{40,32},{48,40},{56,48},{64,56},{72,6... | collective-permute-start | bytes 13369352 | tf_op jit(solution)/shard_map/ppermute | solution.py:19
where the time goes:
time: 451 us; the launch traced here: 442 us
  waiting for transfers between devices  196 us (43%)
  local copies, waits for them, and re-layouts  88.7 us (20%)
  other arithmetic  76.9 us (17%)
  matrix products  43.6 us (10%)
  starting transfers between devices  34.9 us (8%)
    ppermute x1, waiting for transfers between devices, with_halo(): lax.ppermute(lax.slice_in_dim(block, block.shape[dim] - width, None, axis...  95.4 us
    ppermute x1, waiting for transfers between devices, with_halo(): lax.ppermute(lax.slice_in_dim(block, 0, width, axis=dim), axis, backward)  91.4 us
    convert_element_type x1, other arithmetic, azimuth_pair(): cos_low = (cosine - cos_high.astype(jnp.float32)).astype(jnp.bfloat16)  58.6 us
    unnamed x28, local copies, waits for them, and re-layouts  22.3 us
    all_to_all x1, starting transfers between devices, local(): lax.all_to_all(lat_major, 'ma', split_axis=0, concat_axis=3, tiled=True)  18.8 us
    reshape x1, local copies, waits for them, and re-layouts, local(): legendre_table = legendre.reshape(slot_dev, block, block, lat_all)  16.8 us
    dot_general x1, local copies, waits for them, and re-layouts, local(): lax.dot_general(spectra, legendre_table, (((3,), (2,)), ((1, 2), (0, 1)))...  11.9 us
    dot_general x1, matrix products, local(): lax.dot_general(spectra, legendre_table, (((3,), (2,)), ((1, 2), (0, 1)))...  10.9 us
  transfers between devices with their start and end apart: 4, of which 3 were waited for; matrix products, arithmetic and copies ran while one was open for 13% of the time, Pallas kernels for 0%

commit v1 on v0

v1 whole, which is shorter than its diff:
```python
import math

import jax
import jax.numpy as jnp
import numpy as np
from jax import lax
from jax.experimental import pallas as pl
from jax.experimental.pallas import tpu as pltpu
from jax.sharding import PartitionSpec as P

F32, BF16 = jnp.float32, jnp.bfloat16
POINTS = 3072
QUARTER = POINTS // 4
SLOTS = 17
GROUPS = 16
SPAN = 16


def lane_permutation():
    natural = np.zeros((256, 256), np.float32)
    for j in range(4):
        for c in range(16):
            for a in range(4):
                natural[j * 64 + c * 4 + a, j * 64 + a * 16 + c] = 1.0
    return natural


def lane_masks():
    lanes = np.arange(128) // 32
    return np.stack([np.broadcast_to(lanes == j, (16, 128)) for j in range(4)])


def quarter_table():
    j = np.arange(4)[:, None, None, None]
    b = np.arange(16)[None, :, None, None]
    g = np.arange(16)[None, None, :, None]
    x = np.arange(QUARTER)[None, None, None, :]
    order = b * 64 + g * 4 + j
    turns = (order * (2 * x + 1)) % (2 * POINTS)
    angles = turns * (math.pi / POINTS)
    table = np.stack([np.cos(angles), np.sin(angles)])
    return table.reshape(2, 4, 256, QUARTER)


def own_block(blocks_ref, s):
    lead = blocks_ref[2 * lax.axis_index("ma")]
    return (s >= SPAN - lead).astype(jnp.int32)


def spread_rows(leg, s, rows_scr):
    for c in range(16):
        rows_scr[pl.ds(c, 64, stride=16), :] = leg[s, :, c * 128 : (c + 1) * 128].astype(F32)


def block_weights(rows, masks):
    rolled = [rows] + [pltpu.roll(rows, 32 * r, 1) for r in (1, 2, 3)]
    return jnp.concatenate(
        [rolled[(j - a) % 4][j * 16 : (j + 1) * 16] * masks[j] for j in range(4) for a in range(4)],
        axis=0,
    )


def swap_lane_groups(parts, lane_group):
    results = []
    for a in range(4):
        value = None
        for s in range(4):
            shift = (s - a) % 4
            moved = pltpu.roll(parts[s], 32 * shift, 1) if shift else parts[s]
            value = moved if value is None else jnp.where(lane_group == s, moved, value)
        results.append(value)
    return results


def synth_kernel(blocks_ref, coef_hbm, leg_hbm, perm_ref, mask_ref, out_ref, coef, leg, sem_c, sem_l, rows_scr, acc, turned):
    def fetch(s):
        return (
            pltpu.make_async_copy(leg_hbm.at[s], leg.at[s], sem_l.at[s]),
            pltpu.make_async_copy(coef_hbm.at[:, s], coef.at[s], sem_c.at[s]),
        )

    def start(s, carry):
        for copy in fetch(s):
            copy.start()
        return carry

    lax.fori_loop(0, SLOTS, start, 0)
    acc[...] = jnp.zeros_like(acc)
    masks = [mask_ref[j] for j in range(4)]

    def slot(s, carry):
        for copy in fetch(s):
            copy.wait()
        spread_rows(leg, s, rows_scr)
        base = own_block(blocks_ref, s) * (GROUPS * 24)
        values = jnp.concatenate(
            [coef[s, :, :, g * 256 : (g + 1) * 256].reshape(24, 256) for g in range(GROUPS)], axis=0
        )
        values = jnp.dot(values, perm_ref[...], preferred_element_type=F32).astype(BF16)
        for g in range(GROUPS):
            weights = block_weights(rows_scr[g * 64 : (g + 1) * 64, :].astype(BF16), masks)
            term = jnp.dot(values[g * 24 : (g + 1) * 24], weights, preferred_element_type=F32)
            where = pl.ds(pl.multiple_of(base + g * 24, 8), 24)
            acc[where, :] = acc[where, :] + term
        return carry

    lax.fori_loop(0, SLOTS, slot, 0)
    for comp in range(3):
        for i in range(2):
            parts = []
            for part in range(2):
                for vm in range(2):
                    row = ((vm * 3 + comp) * 2 + part) * 2 + i
                    parts.append(acc[pl.ds(row, 2 * GROUPS, stride=24), :])
            turned[comp * 2 + i] = jnp.concatenate(parts, axis=0).T
    for d in range(8):
        for j in range(4):
            pieces = [turned[n, pl.ds(j * 32 + d, 4, stride=8), :] for n in range(6)]
            out_ref[d, j] = jnp.concatenate(pieces, axis=0).astype(BF16)


def synthesis(m_blocks, coeffs, legendre, perm, masks):
    return pl.pallas_call(
        synth_kernel,
        in_specs=[
            pl.BlockSpec(memory_space=pltpu.SMEM),
            pl.BlockSpec(memory_space=pltpu.HBM),
            pl.BlockSpec(memory_space=pltpu.HBM),
            pl.BlockSpec(memory_space=pltpu.VMEM),
            pl.BlockSpec(memory_space=pltpu.VMEM),
        ],
        out_specs=pl.BlockSpec(memory_space=pltpu.VMEM),
        out_shape=jax.ShapeDtypeStruct((8, 4, 24, 128), BF16),
        scratch_shapes=[
            pltpu.VMEM((SLOTS, 12, 2, 4096), BF16),
            pltpu.VMEM((SLOTS, 64, 2048), BF16),
            pltpu.SemaphoreType.DMA((SLOTS,)),
            pltpu.SemaphoreType.DMA((SLOTS,)),
            pltpu.VMEM((1024, 128), F32),
            pltpu.VMEM((2 * GROUPS * 24, 128), F32),
            pltpu.VMEM((6, 128, 128), F32),
        ],
        compiler_params=pltpu.CompilerParams(vmem_limit_bytes=32 * 2**20),
        name="synthesis",
    )(m_blocks, coeffs, legendre, perm, masks)


def azimuth_kernel(blocks_ref, weights_ref, in_ref, table_hbm, out_ref, table, sem, even_c, odd_c, even_s, odd_s, folded):
    def copies(p):
        source = pl.ds(pl.multiple_of(blocks_ref[p] * 16, 16), 16)
        target = pl.ds(pl.multiple_of(p * 16, 16), 16)
        return [
            pltpu.make_async_copy(table_hbm.at[part, j, source], table.at[part, j, target], sem.at[part, j, p])
            for part in range(2)
            for j in range(4)
        ]

    def start(p, carry):
        for copy in copies(p):
            copy.start()
        return carry

    def finish(p, carry):
        for copy in copies(p):
            copy.wait()
        return carry

    lax.fori_loop(0, 16, start, 0)
    lane_group = lax.broadcasted_iota(jnp.int32, (24, 128), 1) // 32
    left = []
    for j in range(4):
        halves = []
        for h in range(2):
            parts = [in_ref[h * 4 + s, j].astype(F32) * (1.0 / 32.0) for s in range(4)]
            halves.append(swap_lane_groups(parts, lane_group))
        both = [jnp.concatenate([halves[0][n], halves[1][n]], axis=1) for n in range(4)]
        left.append([jnp.concatenate([both[part * 2], both[part * 2 + 1]], axis=0).astype(BF16) for part in range(2)])
    lax.fori_loop(0, 16, finish, 0)
    for part, refs in ((0, (even_c, odd_c)), (1, (even_s, odd_s))):
        for parity in range(2):
            refs[parity][...] = jnp.dot(
                left[parity][part], table[part, parity], preferred_element_type=F32
            ) + jnp.dot(left[parity + 2][part], table[part, parity + 2], preferred_element_type=F32)
    for x in range(QUARTER // 128):
        cols = slice(x * 128, (x + 1) * 128)
        fields = [[], [], [], []]
        for f in range(6):
            rows = slice(f * 8, (f + 1) * 8)
            ce, co, se, so = even_c[rows, cols], odd_c[rows, cols], even_s[rows, cols], odd_s[rows, cols]
            plus, minus = ce + co, ce - co
            total, other = se + so, se - so
            fields[0].append(plus - total)
            fields[1].append(plus + total)
            fields[2].append(minus + other)
            fields[3].append(minus - other)
        products = []
        for n in range(4):
            u0, u1, u2, b0, b1, b2 = fields[n]
            products.append(
                [
                    u1 * b2 - u2 * b1,
                    u2 * b0 - u0 * b2,
                    u0 * b1 - u1 * b0,
                    0.5 * (b0 * b0 + b1 * b1 + b2 * b2),
                ]
            )
        folds = [[], [], [], []]
        for g in range(4):
            p0, p1, p2, p3 = (products[n][g] for n in range(4))
            front, back = p0 + p1, p2 + p3
            left_odd, right_odd = p1 - p0, p2 - p3
            folds[0].append(front + back)
            folds[1].append(front - back)
            folds[2].append(left_odd + right_odd)
            folds[3].append(left_odd - right_odd)
        for n in range(4):
            folded[n, :, cols] = jnp.concatenate(folds[n], axis=0).astype(BF16)
    row = lax.broadcasted_iota(jnp.int32, (8, 1), 0) % 4
    own = lax.axis_index("ma")
    weight = jnp.zeros((8, 1), F32)
    for t in range(4):
        weight = jnp.where(row == t, weights_ref[t * 8 + own], weight)
    lane_group = lax.broadcasted_iota(jnp.int32, (8, 128), 1) // 32
    for j in range(4):
        terms = [
            lax.dot_general(
                folded[part * 2 + j % 2], table[part, j], (((1,), (1,)), ((), ())), preferred_element_type=F32
            )
            for part in range(2)
        ]
        for gh in range(2):
            for h in range(2):
                parts = []
                for gl in range(2):
                    for part in range(2):
                        g = gh * 2 + gl
                        piece = terms[part][g * 8 : (g + 1) * 8, h * 128 : (h + 1) * 128]
                        parts.append((piece * (1.0 / math.sqrt(POINTS))) * weight)
                swapped = swap_lane_groups(parts, lane_group)
                for s in range(4):
                    where = (j * 2 + gh) * 8
                    out_ref[h * 4 + s, where : where + 8, :] = swapped[s].astype(BF16)


def azimuth(m_blocks, lat_weights, received, table):
    grid_shape = pltpu.VMEM((48, QUARTER), F32)
    return pl.pallas_call(
        azimuth_kernel,
        in_specs=[
            pl.BlockSpec(memory_space=pltpu.SMEM),
            pl.BlockSpec(memory_space=pltpu.SMEM),
            pl.BlockSpec(memory_space=pltpu.VMEM),
            pl.BlockSpec(memory_space=pltpu.HBM),
        ],
        out_specs=pl.BlockSpec(memory_space=pltpu.VMEM),
        out_shape=jax.ShapeDtypeStruct((8, 64, 128), BF16),
        scratch_shapes=[
            pltpu.VMEM((2, 4, 256, QUARTER), BF16),
            pltpu.SemaphoreType.DMA((2, 4, 16)),
            grid_shape,
            grid_shape,
            grid_shape,
            grid_shape,
            pltpu.VMEM((4, 32, QUARTER), BF16),
        ],
        compiler_params=pltpu.CompilerParams(vmem_limit_bytes=32 * 2**20),
        name="azimuth",
    )(m_blocks, lat_weights, received, table)


def analysis_kernel(
    blocks_ref, own_ref, low_ref, high_ref, leg_hbm, perm_ref, mask_ref, plain_hbm, slope_hbm,
    leg, sem_l, rows_scr, placed, turned, terms, out, sem_o,
):
    def fetch(s):
        return pltpu.make_async_copy(leg_hbm.at[s], leg.at[s], sem_l.at[s])

    def start(s, carry):
        fetch(s).start()
        return carry

    lax.fori_loop(0, SLOTS, start, 0)
    for n, ref in enumerate((own_ref, low_ref, high_ref)):
        for d in range(8):
            for j in range(4):
                for gh in range(2):
                    where = (j * 2 + gh) * 8
                    placed[n, pl.ds((gh * 4 + j) * 64 + d, 8, stride=8), :] = ref[d, where : where + 8, :].astype(F32)

    def pick(n, gh, j, i):
        return placed[n, (gh * 4 + j) * 64 + i * 32 : (gh * 4 + j) * 64 + (i + 1) * 32, :]

    for gh in range(2):
        columns = [[], [], [], []]
        for j in range(4):
            o0, o1 = pick(0, gh, j, 0), pick(0, gh, j, 1)
            l0, l1 = pick(1, gh, j, 0), pick(1, gh, j, 1)
            h0, h1 = pick(2, gh, j, 0), pick(2, gh, j, 1)
            columns[0].append(o0)
            columns[1].append(o1)
            columns[2].append((l0 - 8.0 * l1 + 8.0 * o1 - h0) / 12.0)
            columns[3].append((l1 - 8.0 * o0 + 8.0 * h0 - h1) / 12.0)
        for n in range(2):
            for i in range(2):
                block = jnp.concatenate(columns[n * 2 + i], axis=0)
                turned[n, (i * 2 + gh) * 128 : (i * 2 + gh + 1) * 128, :] = block.T
    for qg in range(2 * GROUPS):
        pair = [turned[n, pl.ds(qg, 16, stride=32), :] for n in range(2)]
        terms[qg] = jnp.concatenate(pair, axis=0).astype(BF16)
    masks = [mask_ref[j] for j in range(4)]

    def send(s):
        return [
            pltpu.make_async_copy(out.at[s, n, i], ref.at[i, s], sem_o.at[s, n, i])
            for n, ref in enumerate((plain_hbm, slope_hbm))
            for i in range(2)
        ]

    def slot(s, carry):
        fetch(s).wait()
        spread_rows(leg, s, rows_scr)
        base = own_block(blocks_ref, s) * GROUPS
        values = []
        for g in range(GROUPS):
            weights = block_weights(rows_scr[g * 64 : (g + 1) * 64, :].astype(BF16), masks)
            value = lax.dot_general(
                terms[base + g], weights, (((1,), (1,)), ((), ())), preferred_element_type=F32
            )
            values.append(value.astype(BF16))
        values = jnp.concatenate(values, axis=0)
        values = jnp.dot(values, perm_ref[...], preferred_element_type=F32).astype(BF16)
        for g in range(GROUPS):
            for n in range(2):
                for i in range(2):
                    row = g * 32 + n * 16 + i * 8
                    out[s, n, i, :, g * 256 : (g + 1) * 256] = values[row : row + 8]
        for copy in send(s):
            copy.start()
        return carry

    lax.fori_loop(0, SLOTS, slot, 0)

    def finish(s, carry):
        for copy in send(s):
            copy.wait()
        return carry

    lax.fori_loop(0, SLOTS, finish, 0)


def analysis(m_blocks, own, low, high, legendre, perm_back, masks):
    shape = jax.ShapeDtypeStruct((2, SLOTS, 8, 4096), BF16)
    vmem = pl.BlockSpec(memory_space=pltpu.VMEM)
    hbm = pl.BlockSpec(memory_space=pltpu.HBM)
    return pl.pallas_call(
        analysis_kernel,
        in_specs=[pl.BlockSpec(memory_space=pltpu.SMEM), vmem, vmem, vmem, hbm, vmem, vmem],
        out_specs=[hbm, hbm],
        out_shape=[shape, shape],
        scratch_shapes=[
            pltpu.VMEM((SLOTS, 64, 2048), BF16),
            pltpu.SemaphoreType.DMA((SLOTS,)),
            pltpu.VMEM((1024, 128), F32),
            pltpu.VMEM((3, 512, 128), F32),
            pltpu.VMEM((2, 512, 128), F32),
            pltpu.VMEM((2 * GROUPS, 32, 128), BF16),
            pltpu.VMEM((SLOTS, 2, 2, 8, 4096), BF16),
            pltpu.SemaphoreType.DMA((SLOTS, 2, 2)),
        ],
        compiler_params=pltpu.CompilerParams(vmem_limit_bytes=32 * 2**20),
        name="analysis",
    )(m_blocks, own, low, high, legendre, perm_back, masks)


def constants():
    perm = lane_permutation()
    return (
        jnp.asarray(perm, BF16),
        jnp.asarray(perm.T, BF16),
        jnp.asarray(lane_masks(), BF16),
        jnp.asarray(quarter_table(), BF16),
    )


def local(coeffs, legendre, lat_weights, m_blocks):
    perm, perm_back, masks, table = constants()
    sent = synthesis(m_blocks, coeffs.transpose(1, 2, 0, 3), legendre, perm, masks)
    received = lax.all_to_all(sent, "ma", split_axis=0, concat_axis=0, tiled=True)
    sent_back = azimuth(m_blocks, lat_weights, received, table)
    own = lax.all_to_all(sent_back, "ma", split_axis=0, concat_axis=0, tiled=True)
    count = lax.axis_size("row")
    low = lax.ppermute(own, "row", [(r, r + 1) for r in range(count - 1)])
    high = lax.ppermute(own, "row", [(r + 1, r) for r in range(count - 1)])
    plain, slope = analysis(m_blocks, own, low, high, legendre, perm_back, masks)
    return plain.transpose(0, 2, 1, 3), slope.transpose(0, 2, 1, 3)


def solution(mesh):
    placed = (P("row", None, "ma", None), P("ma", None, None), P(), P())
    return jax.shard_map(
        local,
        mesh=mesh,
        in_specs=placed,
        out_specs=(P("row", None, "ma", None), P("row", None, "ma", None)),
        check_vma=False,
    )
```

time: 451 us -> 89 us (0.20); the launches traced: 442 us -> 88.7 us
  waiting for transfers between devices: 196 us -> 7.94 us
  local copies, waits for them, and re-layouts: 88.7 us -> 6.49 us
  other arithmetic: 76.9 us -> 0 us
  matrix products: 43.6 us -> 0 us
  Pallas kernels: 0 us -> 34.6 us
  blocking collectives: 0 us -> 31.4 us
  starting transfers between devices: 34.9 us -> 7.55 us
    ppermute x2, waiting for transfers between devices: 187 us -> 7.94 us  [the longest x1 6.11 us: local(): low = lax.ppermute(own, 'row', [(r, r + 1) for r in range(count - 1)])]
    convert_element_type x3 -> x0, other arithmetic: 63.5 us -> none  [the longest x1 58.6 us: azimuth_pair(): cos_low = (cosine - cos_high.astype(jnp.float32)).astype(jnp.bfloat16)]
    dot_general x7 -> x0, matrix products: 43.6 us -> none  [the longest x1 10.9 us: local(): lax.dot_general(spectra, legendre_table, (((3,), (2,)), ((1, 2), (0, 1)))...]
    reshape x7 -> x0, local copies, waits for them, and re-layouts: 37.1 us -> none  [the longest x1 16.8 us: local(): legendre_table = legendre.reshape(slot_dev, block, block, lat_all)]
    pallas_call x0 -> x3, Pallas kernels: none -> 34.6 us  [the longest x1 15.1 us: analysis(): pl.pallas_call(analysis_kernel, in_specs=[pl.BlockSpec(memory_space=pltpu...]
    all_to_all x0 -> x2, blocking collectives: none -> 31.4 us  [the longest x1 19.4 us: local(): lax.all_to_all(sent, 'ma', split_axis=0, concat_axis=0, tiled=True)]
    all_to_all x2 -> x0, starting transfers between devices: 26 us -> none  [the longest x1 18.8 us: local(): lax.all_to_all(lat_major, 'ma', split_axis=0, concat_axis=3, tiled=True)]
    unnamed x28 -> x18, local copies, waits for them, and re-layouts: 22.3 us -> 6.49 us
  transfers between devices with their start and end apart: 4 -> 2, of which waited for: 3 -> 2; matrix products, arithmetic and copies ran while one was open for 13% -> 0% of each run, Pallas kernels for 0% -> 0%
where the time goes in v1:
time: 89 us; the launch traced here: 88.7 us
  Pallas kernels  34.6 us (39%)
  blocking collectives  31.4 us (35%)
  waiting for transfers between devices  7.94 us (9%)
  starting transfers between devices  7.55 us (8%)
  local copies, waits for them, and re-layouts  6.49 us (7%)
    all_to_all x1, blocking collectives, local(): lax.all_to_all(sent, 'ma', split_axis=0, concat_axis=0, tiled=True)  19.4 us
    pallas_call x1, Pallas kernels, analysis(): pl.pallas_call(analysis_kernel, in_specs=[pl.BlockSpec(memory_space=pltpu...  15.1 us
    all_to_all x1, blocking collectives, local(): lax.all_to_all(sent_back, 'ma', split_axis=0, concat_axis=0, tiled=True)  12 us
    pallas_call x1, Pallas kernels, synthesis(): pl.pallas_call(synth_kernel, in_specs=[pl.BlockSpec(memory_space=pltpu.SM...  11.3 us
    pallas_call x1, Pallas kernels, azimuth(): pl.pallas_call(azimuth_kernel, in_specs=[pl.BlockSpec(memory_space=pltpu....  8.19 us
    unnamed x18, local copies, waits for them, and re-layouts  6.49 us
    ppermute x1, waiting for transfers between devices, local(): low = lax.ppermute(own, 'row', [(r, r + 1) for r in range(count - 1)])  6.11 us
    ppermute x1, starting transfers between devices, local(): high = lax.ppermute(own, 'row', [(r + 1, r) for r in range(count - 1)])  5.63 us
  transfers between devices with their start and end apart: 2, of which 2 were waited for; matrix products, arithmetic and copies ran while one was open for 0% of the time, Pallas kernels for 0%

profile of v1, /device:TPU:6, one launch (start us, length us, event | category | flops | bytes accessed | tf_op | source)
XLA Modules:
  0.0 88.7 jit_solution(17188080052951283669)
XLA Ops:
  0.6 0.0 copy-start
  0.6 2.3 %copy-done = bf16[17,64,2048]{2,1,0:T(8,128)(2,1)S(1)} copy-done((bf16[17,64,2048]{2,1,0:T(8,128)(2,1)S(1)}, bf16[17,64,2048]{2,1,0:T(8,128)(2,1)}, u32[]{:S(2)}) %copy-start) | copy-done | bytes 4456472
  2.9 0.0 copy-start.2
  2.9 1.9 %copy-done.2 = bf16[2,12,17,4096]{3,0,2,1:T(2,128)(2,1)S(1)} copy-done((bf16[2,12,17,4096]{3,0,2,1:T(2,128)(2,1)S(1)}, bf16[2,12,17,4096]{3,0,2,1:T(2,128)(2,1)}, u32[]{:S(2)}) %copy-start.2) | copy-done | bytes 3342360
  4.8 0.0 copy-start.4
  4.8 0.9 %copy-done.4 = bf16[256,256]{1,0:T(8,128)(2,1)S(1)} copy-done((bf16[256,256]{1,0:T(8,128)(2,1)S(1)}, bf16[256,256]{1,0:T(8,128)(2,1)}, u32[]{:S(2)}) %copy-start.4) | copy-done | bytes 131096
  5.7 0.0 copy-start.6
  5.7 0.7 copy-done.6
  6.5 0.0 copy-start.7
  6.5 0.7 copy-done.7
  7.1 0.0 copy-start.3
  7.1 0.0 copy-start.8
  7.1 0.0 copy-start.1
  7.1 11.3 %synthesis.1 = bf16[8,4,24,128]{3,2,1,0:T(8,128)(2,1)S(1)} custom-call(s32[16]{0:T(128)S(1)} %copy-done.7, bf16[12,17,2,4096]{3,2,1,0:T(2,128)(2,1)S(1)} %bitcast.3, bf16[17,64,2048]{2,1,0:T(8,128)(2,1)S(1)} %copy-done, bf16[256,256]{1,0:T(8,128)(2,1)S(1)} %copy-done.4, bf16[4,16,128]{2,1,0:T(8,128)(2,1)S(1)} %copy-done.6), custom_call_target="tpu_custom_call" | custom-call | tf_op jit(solution)/shard_map/synthesis/pallas_call | solution.py:123
  18.5 0.0 copy-start.5
  18.5 19.4 %all_to_all.10.in_ref = bf16[8,4,24,128]{3,2,1,0:T(8,128)(2,1)S(1)} all-to-all(bf16[8,4,24,128]{3,2,1,0:T(8,128)(2,1)S(1)} %synthesis.1), channel_id=1, replica_groups=mesh['row'=32,'ma'=8] {'ma'}, dimensions={0} | all-to-all | bytes 393216 | tf_op jit(solution)/shard_map/all_to_all | solution.py:388
  37.9 0.0 copy-done.3
  37.9 0.0 copy-done.8
  37.9 8.2 %azimuth.1 = bf16[8,64,128]{2,1,0:T(8,128)(2,1)S(1)} custom-call(s32[16]{0:T(128)S(1)} %copy-done.7, f32[32]{0:T(128)S(1)} %copy-done.8, bf16[8,4,24,128]{3,2,1,0:T(8,128)(2,1)S(1)} %all_to_all.10.in_ref, bf16[2,4,256,768]{3,2,1,0:T(8,128)(2,1)S(1)} %copy-done.3), custom_call_target="tpu_custom_call" | custom-call | tf_op jit(solution)/shard_map/azimuth/pallas_call | solution.py:247
  46.1 12.0 %all_to_all.11.own_ref = bf16[8,64,128]{2,1,0:T(8,128)(2,1)S(1)} all-to-all(bf16[8,64,128]{2,1,0:T(8,128)(2,1)S(1)} %azimuth.1), channel_id=1, replica_groups=mesh['row'=32,'ma'=8] {'ma'}, dimensions={0} | all-to-all | bytes 262144 | tf_op jit(solution)/shard_map/all_to_all | solution.py:390
  58.1 5.6 %collective-permute-start.1 = (bf16[8,64,128]{2,1,0:T(8,128)(2,1)S(1)}, bf16[8,64,128]{2,1,0:T(8,128)(2,1)S(1)}, u32[]{:S(2)}, u32[]{:S(2)}) collective-permute-start(bf16[8,64,128]{2,1,0:T(8,128)(2,1)S(1)} %all_to_all.11.own_ref), channel_id=1, source_target_pairs={{8,0},{16,8},{24,16},{32,24},{40,32},{48,40},{56,48},{64,56},{72,6... | collective-permute-start | bytes 393224 | tf_op jit(solution)/shard_map/ppermute | solution.py:393
  63.7 1.9 %collective-permute-start = (bf16[8,64,128]{2,1,0:T(8,128)(2,1)S(1)}, bf16[8,64,128]{2,1,0:T(8,128)(2,1)S(1)}, u32[]{:S(2)}, u32[]{:S(2)}) collective-permute-start(bf16[8,64,128]{2,1,0:T(8,128)(2,1)S(1)} %all_to_all.11.own_ref), channel_id=1, source_target_pairs={{0,8},{8,16},{16,24},{24,32},{32,40},{40,48},{48,56},{56,64},{64,7... | collective-permute-start | bytes 393224 | tf_op jit(solution)/shard_map/ppermute | solution.py:392
  65.7 1.8 %collective-permute-done.1.high_ref = bf16[8,64,128]{2,1,0:T(8,128)(2,1)S(1)} collective-permute-done((bf16[8,64,128]{2,1,0:T(8,128)(2,1)S(1)}, bf16[8,64,128]{2,1,0:T(8,128)(2,1)S(1)}, u32[]{:S(2)}, u32[]{:S(2)}) %collective-permute-start.1) | collective-permute-done | bytes 131104 | tf_op jit(solution)/shard_map/ppermute | solution.py:393
  67.5 6.1 %collective-permute-done.low_ref = bf16[8,64,128]{2,1,0:T(8,128)(2,1)S(1)} collective-permute-done((bf16[8,64,128]{2,1,0:T(8,128)(2,1)S(1)}, bf16[8,64,128]{2,1,0:T(8,128)(2,1)S(1)}, u32[]{:S(2)}, u32[]{:S(2)}) %collective-permute-start) | collective-permute-done | bytes 131104 | tf_op jit(solution)/shard_map/ppermute | solution.py:392
  73.6 0.0 copy-done.1
  73.6 0.0 copy-done.5
  73.6 15.1 %analysis.1 = (bf16[2,17,8,4096]{3,2,1,0:T(8,128)(2,1)}, bf16[2,17,8,4096]{3,2,1,0:T(8,128)(2,1)}) custom-call(s32[16]{0:T(128)S(1)} %copy-done.7, bf16[8,64,128]{2,1,0:T(8,128)(2,1)S(1)} %all_to_all.11.own_ref, bf16[8,64,128]{2,1,0:T(8,128)(2,1)S(1)} %collective-permute-done.low_ref, bf16[8,64,128]{2,1,0:T(8,128)(2,1)S(1)} %collective-permute-done.1.high_ref, ...), custom_call_target="tpu_custom_call" | custom-call | tf_op jit(solution)/shard_map/analysis/pallas_call | solution.py:355
Async XLA Ops:
  0.6 2.3 %copy-start = (bf16[17,64,2048]{2,1,0:T(8,128)(2,1)S(1)}, bf16[17,64,2048]{2,1,0:T(8,128)(2,1)}, u32[]{:S(2)}) copy-start(bf16[17,64,2048]{2,1,0:T(8,128)(2,1)} %leg_hbm.3) | copy-start | bytes 13369348
  2.9 1.9 %copy-start.2 = (bf16[2,12,17,4096]{3,0,2,1:T(2,128)(2,1)S(1)}, bf16[2,12,17,4096]{3,0,2,1:T(2,128)(2,1)}, u32[]{:S(2)}) copy-start(bf16[2,12,17,4096]{3,0,2,1:T(2,128)(2,1)} %param.8) | copy-start | bytes 10027012
  4.8 0.9 %copy-start.4 = (bf16[256,256]{1,0:T(8,128)(2,1)S(1)}, bf16[256,256]{1,0:T(8,128)(2,1)}, u32[]{:S(2)}) copy-start(bf16[256,256]{1,0:T(8,128)(2,1)} %constant.8.clone.perm_ref) | copy-start | bytes 393220
  5.7 0.7 copy-start.6
  6.5 0.7 copy-start.7
  7.1 30.8 %copy-start.3 = (bf16[2,4,256,768]{3,2,1,0:T(8,128)(2,1)S(1)}, bf16[2,4,256,768]{3,2,1,0:T(8,128)(2,1)}, u32[]{:S(2)}) copy-start(bf16[2,4,256,768]{3,2,1,0:T(8,128)(2,1)} %constant.11.clone.table_hbm) | copy-start | bytes 9437188
  7.1 30.8 %copy-start.8 = (f32[32]{0:T(128)S(1)}, f32[32]{0:T(128)}, u32[]{:S(2)}) copy-start(f32[32]{0:T(128)} %weights_ref.1) | copy-start | bytes 388
  7.1 66.5 %copy-start.1 = (bf16[17,64,2048]{2,1,0:T(8,128)(2,1)S(1)}, bf16[17,64,2048]{2,1,0:T(8,128)(2,1)}, u32[]{:S(2)}) copy-start(bf16[17,64,2048]{2,1,0:T(8,128)(2,1)} %leg_hbm.3) | copy-start | bytes 13369348
  18.5 55.2 %copy-start.5 = (bf16[256,256]{1,0:T(8,128)(2,1)S(1)}, bf16[256,256]{1,0:T(8,128)(2,1)}, u32[]{:S(2)}) copy-start(bf16[256,256]{1,0:T(8,128)(2,1)} %constant.9.clone.perm_ref) | copy-start | bytes 393220
  58.1 9.4 %collective-permute-start.1 = (bf16[8,64,128]{2,1,0:T(8,128)(2,1)S(1)}, bf16[8,64,128]{2,1,0:T(8,128)(2,1)S(1)}, u32[]{:S(2)}, u32[]{:S(2)}) collective-permute-start(bf16[8,64,128]{2,1,0:T(8,128)(2,1)S(1)} %all_to_all.11.own_ref), channel_id=1, source_target_pairs={{8,0},{16,8},{24,16},{32,24},{40,32},{48,40},{56,48},{64,56},{72,6... | collective-permute-start | bytes 393224 | tf_op jit(solution)/shard_map/ppermute | solution.py:393
  63.7 9.9 %collective-permute-start = (bf16[8,64,128]{2,1,0:T(8,128)(2,1)S(1)}, bf16[8,64,128]{2,1,0:T(8,128)(2,1)S(1)}, u32[]{:S(2)}, u32[]{:S(2)}) collective-permute-start(bf16[8,64,128]{2,1,0:T(8,128)(2,1)S(1)} %all_to_all.11.own_ref), channel_id=1, source_target_pairs={{0,8},{8,16},{16,24},{24,32},{32,40},{40,48},{48,56},{56,64},{64,7... | collective-permute-start | bytes 393224 | tf_op jit(solution)/shard_map/ppermute | solution.py:392

commit v2 on v1

--- a/solution.py
+++ b/solution.py
@@ -16,18 +16,16 @@
 SPAN = 16
 
 
-def lane_permutation():
-    natural = np.zeros((256, 256), np.float32)
-    for j in range(4):
-        for c in range(16):
-            for a in range(4):
-                natural[j * 64 + c * 4 + a, j * 64 + a * 16 + c] = 1.0
-    return natural
+def lane_permutation(back=False):
+    natural = lax.broadcasted_iota(jnp.int32, (256, 256), 1 if back else 0)
+    grouped = lax.broadcasted_iota(jnp.int32, (256, 256), 0 if back else 1)
+    target = natural // 64 * 64 + natural % 4 * 16 + natural % 64 // 4
+    return (target == grouped).astype(F32).astype(BF16)
 
 
 def lane_masks():
-    lanes = np.arange(128) // 32
-    return np.stack([np.broadcast_to(lanes == j, (16, 128)) for j in range(4)])
+    group = lax.broadcasted_iota(jnp.int32, (16, 128), 1) // 32
+    return [(group == j).astype(F32).astype(BF16) for j in range(4)]
 
 
 def quarter_table():
@@ -54,10 +52,15 @@
 
 def block_weights(rows, masks):
     rolled = [rows] + [pltpu.roll(rows, 32 * r, 1) for r in (1, 2, 3)]
-    return jnp.concatenate(
-        [rolled[(j - a) % 4][j * 16 : (j + 1) * 16] * masks[j] for j in range(4) for a in range(4)],
-        axis=0,
-    )
+    pieces = []
+    for j in range(2):
+        for a in range(4):
+            first, second = j, 2 + j
+            pieces.append(
+                rolled[(first - a) % 4][first * 16 : (first + 1) * 16] * masks[first]
+                + rolled[(second - a) % 4][second * 16 : (second + 1) * 16] * masks[second]
+            )
+    return jnp.concatenate(pieces, axis=0)
 
 
 def swap_lane_groups(parts, lane_group):
@@ -72,7 +75,7 @@
     return results
 
 
-def synth_kernel(blocks_ref, coef_hbm, leg_hbm, perm_ref, mask_ref, out_ref, coef, leg, sem_c, sem_l, rows_scr, acc, turned):
+def synth_kernel(blocks_ref, coef_hbm, leg_hbm, out_ref, coef, leg, sem_c, sem_l, rows_scr, acc, turned):
     def fetch(s):
         return (
             pltpu.make_async_copy(leg_hbm.at[s], leg.at[s], sem_l.at[s]),
@@ -86,7 +89,9 @@
 
     lax.fori_loop(0, SLOTS, start, 0)
     acc[...] = jnp.zeros_like(acc)
-    masks = [mask_ref[j] for j in range(4)]
+    masks = lane_masks()
+    perm = lane_permutation()
+    lower = lax.broadcasted_iota(jnp.int32, (24, 128), 1) < 64
 
     def slot(s, carry):
         for copy in fetch(s):
@@ -96,12 +101,14 @@
         values = jnp.concatenate(
             [coef[s, :, :, g * 256 : (g + 1) * 256].reshape(24, 256) for g in range(GROUPS)], axis=0
         )
-        values = jnp.dot(values, perm_ref[...], preferred_element_type=F32).astype(BF16)
+        values = jnp.dot(values, perm, preferred_element_type=F32)
         for g in range(GROUPS):
             weights = block_weights(rows_scr[g * 64 : (g + 1) * 64, :].astype(BF16), masks)
-            term = jnp.dot(values[g * 24 : (g + 1) * 24], weights, preferred_element_type=F32)
+            rows = slice(g * 24, (g + 1) * 24)
+            stacked = jnp.concatenate([values[rows, :128], values[rows, 128:]], axis=0).astype(BF16)
+            term = jnp.dot(stacked, weights, preferred_element_type=F32)
             where = pl.ds(pl.multiple_of(base + g * 24, 8), 24)
-            acc[where, :] = acc[where, :] + term
+            acc[where, :] = acc[where, :] + jnp.where(lower, term[:24], term[24:])
         return carry
 
     lax.fori_loop(0, SLOTS, slot, 0)
@@ -119,15 +126,13 @@
             out_ref[d, j] = jnp.concatenate(pieces, axis=0).astype(BF16)
 
 
-def synthesis(m_blocks, coeffs, legendre, perm, masks):
+def synthesis(m_blocks, coeffs, legendre):
     return pl.pallas_call(
         synth_kernel,
         in_specs=[
             pl.BlockSpec(memory_space=pltpu.SMEM),
             pl.BlockSpec(memory_space=pltpu.HBM),
             pl.BlockSpec(memory_space=pltpu.HBM),
-            pl.BlockSpec(memory_space=pltpu.VMEM),
-            pl.BlockSpec(memory_space=pltpu.VMEM),
         ],
         out_specs=pl.BlockSpec(memory_space=pltpu.VMEM),
         out_shape=jax.ShapeDtypeStruct((8, 4, 24, 128), BF16),
@@ -140,32 +145,17 @@
             pltpu.VMEM((2 * GROUPS * 24, 128), F32),
             pltpu.VMEM((6, 128, 128), F32),
         ],
-        compiler_params=pltpu.CompilerParams(vmem_limit_bytes=32 * 2**20),
+        compiler_params=pltpu.CompilerParams(vmem_limit_bytes=60 * 2**20),
         name="synthesis",
-    )(m_blocks, coeffs, legendre, perm, masks)
-
-
-def azimuth_kernel(blocks_ref, weights_ref, in_ref, table_hbm, out_ref, table, sem, even_c, odd_c, even_s, odd_s, folded):
-    def copies(p):
-        source = pl.ds(pl.multiple_of(blocks_ref[p] * 16, 16), 16)
-        target = pl.ds(pl.multiple_of(p * 16, 16), 16)
-        return [
-            pltpu.make_async_copy(table_hbm.at[part, j, source], table.at[part, j, target], sem.at[part, j, p])
-            for part in range(2)
-            for j in range(4)
-        ]
-
-    def start(p, carry):
-        for copy in copies(p):
-            copy.start()
-        return carry
-
-    def finish(p, carry):
-        for copy in copies(p):
-            copy.wait()
-        return carry
-
-    lax.fori_loop(0, 16, start, 0)
+    )(m_blocks, coeffs, legendre)
+
+
+def azimuth_kernel(blocks_ref, weights_ref, in_ref, table, out_ref, even_c, odd_c, even_s, odd_s, folded):
+    starts = [pl.multiple_of(blocks_ref[p] * 16, 16) for p in range(16)]
+
+    def basis(part, j):
+        return jnp.concatenate([table[part, j, pl.ds(start, 16), :] for start in starts], axis=0)
+
     lane_group = lax.broadcasted_iota(jnp.int32, (24, 128), 1) // 32
     left = []
     for j in range(4):
@@ -175,12 +165,11 @@
             halves.append(swap_lane_groups(parts, lane_group))
         both = [jnp.concatenate([halves[0][n], halves[1][n]], axis=1) for n in range(4)]
         left.append([jnp.concatenate([both[part * 2], both[part * 2 + 1]], axis=0).astype(BF16) for part in range(2)])
-    lax.fori_loop(0, 16, finish, 0)
     for part, refs in ((0, (even_c, odd_c)), (1, (even_s, odd_s))):
         for parity in range(2):
             refs[parity][...] = jnp.dot(
-                left[parity][part], table[part, parity], preferred_element_type=F32
-            ) + jnp.dot(left[parity + 2][part], table[part, parity + 2], preferred_element_type=F32)
+                left[parity][part], basis(part, parity), preferred_element_type=F32
+            ) + jnp.dot(left[parity + 2][part], basis(part, parity + 2), preferred_element_type=F32)
     for x in range(QUARTER // 128):
         cols = slice(x * 128, (x + 1) * 128)
         fields = [[], [], [], []]
@@ -224,7 +213,7 @@
     for j in range(4):
         terms = [
             lax.dot_general(
-                folded[part * 2 + j % 2], table[part, j], (((1,), (1,)), ((), ())), preferred_element_type=F32
+                folded[part * 2 + j % 2], basis(part, j), (((1,), (1,)), ((), ())), preferred_element_type=F32
             )
             for part in range(2)
         ]
@@ -250,13 +239,11 @@
             pl.BlockSpec(memory_space=pltpu.SMEM),
             pl.BlockSpec(memory_space=pltpu.SMEM),
             pl.BlockSpec(memory_space=pltpu.VMEM),
-            pl.BlockSpec(memory_space=pltpu.HBM),
+            pl.BlockSpec(memory_space=pltpu.VMEM),
         ],
         out_specs=pl.BlockSpec(memory_space=pltpu.VMEM),
         out_shape=jax.ShapeDtypeStruct((8, 64, 128), BF16),
         scratch_shapes=[
-            pltpu.VMEM((2, 4, 256, QUARTER), BF16),
-            pltpu.SemaphoreType.DMA((2, 4, 16)),
             grid_shape,
             grid_shape,
             grid_shape,
@@ -269,7 +256,7 @@
 
 
 def analysis_kernel(
-    blocks_ref, own_ref, low_ref, high_ref, leg_hbm, perm_ref, mask_ref, plain_hbm, slope_hbm,
+    blocks_ref, own_ref, low_ref, high_ref, leg_hbm, plain_hbm, slope_hbm,
     leg, sem_l, rows_scr, placed, turned, terms, out, sem_o,
 ):
     def fetch(s):
@@ -304,10 +291,14 @@
             for i in range(2):
                 block = jnp.concatenate(columns[n * 2 + i], axis=0)
                 turned[n, (i * 2 + gh) * 128 : (i * 2 + gh + 1) * 128, :] = block.T
+    lower = lax.broadcasted_iota(jnp.int32, (32, 128), 1) < 64
     for qg in range(2 * GROUPS):
         pair = [turned[n, pl.ds(qg, 16, stride=32), :] for n in range(2)]
-        terms[qg] = jnp.concatenate(pair, axis=0).astype(BF16)
-    masks = [mask_ref[j] for j in range(4)]
+        both = jnp.concatenate(pair, axis=0)
+        halves = [jnp.where(lower, both, 0.0), jnp.where(lower, 0.0, both)]
+        terms[qg] = jnp.concatenate(halves, axis=0).astype(BF16)
+    masks = lane_masks()
+    perm = lane_permutation(back=True)
 
     def send(s):
         return [
@@ -326,9 +317,9 @@
             value = lax.dot_general(
                 terms[base + g], weights, (((1,), (1,)), ((), ())), preferred_element_type=F32
             )
-            values.append(value.astype(BF16))
+            values.append(jnp.concatenate([value[:32], value[32:]], axis=1).astype(BF16))
         values = jnp.concatenate(values, axis=0)
-        values = jnp.dot(values, perm_ref[...], preferred_element_type=F32).astype(BF16)
+        values = jnp.dot(values, perm, preferred_element_type=F32).astype(BF16)
         for g in range(GROUPS):
             for n in range(2):
                 for i in range(2):
@@ -348,13 +339,13 @@
     lax.fori_loop(0, SLOTS, finish, 0)
 
 
-def analysis(m_blocks, own, low, high, legendre, perm_back, masks):
+def analysis(m_blocks, own, low, high, legendre):
     shape = jax.ShapeDtypeStruct((2, SLOTS, 8, 4096), BF16)
     vmem = pl.BlockSpec(memory_space=pltpu.VMEM)
     hbm = pl.BlockSpec(memory_space=pltpu.HBM)
     return pl.pallas_call(
         analysis_kernel,
-        in_specs=[pl.BlockSpec(memory_space=pltpu.SMEM), vmem, vmem, vmem, hbm, vmem, vmem],
+        in_specs=[pl.BlockSpec(memory_space=pltpu.SMEM), vmem, vmem, vmem, hbm],
         out_specs=[hbm, hbm],
         out_shape=[shape, shape],
         scratch_shapes=[
@@ -363,35 +354,25 @@
             pltpu.VMEM((1024, 128), F32),
             pltpu.VMEM((3, 512, 128), F32),
             pltpu.VMEM((2, 512, 128), F32),
-            pltpu.VMEM((2 * GROUPS, 32, 128), BF16),
+            pltpu.VMEM((2 * GROUPS, 64, 128), BF16),
             pltpu.VMEM((SLOTS, 2, 2, 8, 4096), BF16),
             pltpu.SemaphoreType.DMA((SLOTS, 2, 2)),
         ],
         compiler_params=pltpu.CompilerParams(vmem_limit_bytes=32 * 2**20),
         name="analysis",
-    )(m_blocks, own, low, high, legendre, perm_back, masks)
-
-
-def constants():
-    perm = lane_permutation()
-    return (
-        jnp.asarray(perm, BF16),
-        jnp.asarray(perm.T, BF16),
-        jnp.asarray(lane_masks(), BF16),
-        jnp.asarray(quarter_table(), BF16),
-    )
+    )(m_blocks, own, low, high, legendre)
 
 
 def local(coeffs, legendre, lat_weights, m_blocks):
-    perm, perm_back, masks, table = constants()
-    sent = synthesis(m_blocks, coeffs.transpose(1, 2, 0, 3), legendre, perm, masks)
+    table = jnp.asarray(quarter_table(), BF16)
+    sent = synthesis(m_blocks, coeffs.transpose(1, 2, 0, 3), legendre)
     received = lax.all_to_all(sent, "ma", split_axis=0, concat_axis=0, tiled=True)
     sent_back = azimuth(m_blocks, lat_weights, received, table)
     own = lax.all_to_all(sent_back, "ma", split_axis=0, concat_axis=0, tiled=True)
     count = lax.axis_size("row")
     low = lax.ppermute(own, "row", [(r, r + 1) for r in range(count - 1)])
     high = lax.ppermute(own, "row", [(r + 1, r) for r in range(count - 1)])
-    plain, slope = analysis(m_blocks, own, low, high, legendre, perm_back, masks)
+    plain, slope = analysis(m_blocks, own, low, high, legendre)
     return plain.transpose(0, 2, 1, 3), slope.transpose(0, 2, 1, 3)
 
 

time: 89 us -> 80.8 us (0.908)
  local copies, waits for them, and re-layouts: 6.49 us -> 2.28 us
  Pallas kernels: 34.6 us -> 30.6 us
    pallas_call x1, Pallas kernels: 8.19 us -> 2.35 us  [azimuth(): pl.pallas_call(azimuth_kernel, in_specs=[pl.BlockSpec(memory_space=pltpu....]
    unnamed x18 -> x8, local copies, waits for them, and re-layouts: 6.49 us -> 2.28 us
    pallas_call x1, Pallas kernels: 11.3 us -> 12.7 us  [synthesis(): pl.pallas_call(synth_kernel, in_specs=[pl.BlockSpec(memory_space=pltpu.SM...]
where the time goes in v2:
time: 80.8 us; the launch traced here: 80.5 us
  blocking collectives  31.5 us (39%)
  Pallas kernels  30.6 us (38%)
  waiting for transfers between devices  7.94 us (10%)
  starting transfers between devices  7.55 us (9%)
  local copies, waits for them, and re-layouts  2.28 us (3%)
    all_to_all x1, blocking collectives, local(): lax.all_to_all(sent, 'ma', split_axis=0, concat_axis=0, tiled=True)  19.5 us
    pallas_call x1, Pallas kernels, analysis(): pl.pallas_call(analysis_kernel, in_specs=[pl.BlockSpec(memory_space=pltpu...  15.6 us
    pallas_call x1, Pallas kernels, synthesis(): pl.pallas_call(synth_kernel, in_specs=[pl.BlockSpec(memory_space=pltpu.SM...  12.7 us
    all_to_all x1, blocking collectives, local(): lax.all_to_all(sent_back, 'ma', split_axis=0, concat_axis=0, tiled=True)  12 us
    ppermute x1, waiting for transfers between devices, local(): low = lax.ppermute(own, 'row', [(r, r + 1) for r in range(count - 1)])  6.11 us
    ppermute x1, starting transfers between devices, local(): high = lax.ppermute(own, 'row', [(r + 1, r) for r in range(count - 1)])  5.63 us
    pallas_call x1, Pallas kernels, azimuth(): pl.pallas_call(azimuth_kernel, in_specs=[pl.BlockSpec(memory_space=pltpu....  2.35 us
    unnamed x8, local copies, waits for them, and re-layouts  2.28 us
  transfers between devices with their start and end apart: 2, of which 2 were waited for; matrix products, arithmetic and copies ran while one was open for 0% of the time, Pallas kernels for 0%

profile of v2, /device:TPU:6, one launch (start us, length us, event | category | flops | bytes accessed | tf_op | source)
XLA Modules:
  0.0 80.5 jit_solution(14942724609896912389)
XLA Ops:
  0.6 0.0 copy-start.1
  0.6 0.0 copy-start.2
  0.7 0.0 copy-start.3
  0.7 12.7 %synthesis.1 = bf16[8,4,24,128]{3,2,1,0:T(8,128)(2,1)} custom-call(s32[16]{0:T(128)} %blocks_ref.5, bf16[12,17,2,4096]{3,2,1,0:T(2,128)(2,1)} %bitcast.3, bf16[17,64,2048]{2,1,0:T(8,128)(2,1)} %leg_hbm.3), custom_call_target="tpu_custom_call" | custom-call | tf_op jit(solution)/shard_map/synthesis/pallas_call | solution.py:130
  13.3 19.5 %all_to_all.10.in_ref = bf16[8,4,24,128]{3,2,1,0:T(8,128)(2,1)S(1)} all-to-all(bf16[8,4,24,128]{3,2,1,0:T(8,128)(2,1)} %synthesis.1), channel_id=1, replica_groups=mesh['row'=32,'ma'=8] {'ma'}, dimensions={0} | all-to-all | bytes 393216 | tf_op jit(solution)/shard_map/all_to_all | solution.py:369
  32.8 0.0 copy-done.1
  32.9 0.0 copy-done.2
  32.9 0.0 copy-done.3
  32.9 2.3 %azimuth.1 = bf16[8,64,128]{2,1,0:T(8,128)(2,1)S(1)} custom-call(s32[16]{0:T(128)S(1)} %copy-done.2, f32[32]{0:T(128)S(1)} %copy-done.3, bf16[8,4,24,128]{3,2,1,0:T(8,128)(2,1)S(1)} %all_to_all.10.in_ref, bf16[2,4,256,768]{3,2,1,0:T(8,128)(2,1)S(1)} %copy-done.1), custom_call_target="tpu_custom_call" | custom-call | tf_op jit(solution)/shard_map/azimuth/pallas_call | solution.py:236
  35.2 12.0 %all_to_all.11.own_ref = bf16[8,64,128]{2,1,0:T(8,128)(2,1)S(1)} all-to-all(bf16[8,64,128]{2,1,0:T(8,128)(2,1)S(1)} %azimuth.1), channel_id=1, replica_groups=mesh['row'=32,'ma'=8] {'ma'}, dimensions={0} | all-to-all | bytes 262144 | tf_op jit(solution)/shard_map/all_to_all | solution.py:371
  47.2 5.6 %collective-permute-start.1 = (bf16[8,64,128]{2,1,0:T(8,128)(2,1)S(1)}, bf16[8,64,128]{2,1,0:T(8,128)(2,1)S(1)}, u32[]{:S(2)}, u32[]{:S(2)}) collective-permute-start(bf16[8,64,128]{2,1,0:T(8,128)(2,1)S(1)} %all_to_all.11.own_ref), channel_id=1, source_target_pairs={{8,0},{16,8},{24,16},{32,24},{40,32},{48,40},{56,48},{64,56},{72,6... | collective-permute-start | bytes 393224 | tf_op jit(solution)/shard_map/ppermute | solution.py:374
  52.8 1.9 %collective-permute-start = (bf16[8,64,128]{2,1,0:T(8,128)(2,1)S(1)}, bf16[8,64,128]{2,1,0:T(8,128)(2,1)S(1)}, u32[]{:S(2)}, u32[]{:S(2)}) collective-permute-start(bf16[8,64,128]{2,1,0:T(8,128)(2,1)S(1)} %all_to_all.11.own_ref), channel_id=1, source_target_pairs={{0,8},{8,16},{16,24},{24,32},{32,40},{40,48},{48,56},{56,64},{64,7... | collective-permute-start | bytes 393224 | tf_op jit(solution)/shard_map/ppermute | solution.py:373
  54.8 1.8 %collective-permute-done.1.high_ref = bf16[8,64,128]{2,1,0:T(8,128)(2,1)S(1)} collective-permute-done((bf16[8,64,128]{2,1,0:T(8,128)(2,1)S(1)}, bf16[8,64,128]{2,1,0:T(8,128)(2,1)S(1)}, u32[]{:S(2)}, u32[]{:S(2)}) %collective-permute-start.1) | collective-permute-done | bytes 131104 | tf_op jit(solution)/shard_map/ppermute | solution.py:374
  56.6 6.1 %collective-permute-done.low_ref = bf16[8,64,128]{2,1,0:T(8,128)(2,1)S(1)} collective-permute-done((bf16[8,64,128]{2,1,0:T(8,128)(2,1)S(1)}, bf16[8,64,128]{2,1,0:T(8,128)(2,1)S(1)}, u32[]{:S(2)}, u32[]{:S(2)}) %collective-permute-start) | collective-permute-done | bytes 131104 | tf_op jit(solution)/shard_map/ppermute | solution.py:373
  62.7 0.0 copy-start
  62.7 2.3 %copy-done = bf16[17,64,2048]{2,1,0:T(8,128)(2,1)S(1)} copy-done((bf16[17,64,2048]{2,1,0:T(8,128)(2,1)S(1)}, bf16[17,64,2048]{2,1,0:T(8,128)(2,1)}, u32[]{:S(2)}) %copy-start) | copy-done | bytes 4456472
  65.0 15.6 %analysis.1 = (bf16[2,17,8,4096]{3,2,1,0:T(8,128)(2,1)}, bf16[2,17,8,4096]{3,2,1,0:T(8,128)(2,1)}) custom-call(s32[16]{0:T(128)S(1)} %copy-done.2, bf16[8,64,128]{2,1,0:T(8,128)(2,1)S(1)} %all_to_all.11.own_ref, bf16[8,64,128]{2,1,0:T(8,128)(2,1)S(1)} %collective-permute-done.low_ref, bf16[8,64,128]{2,1,0:T(8,128)(2,1)S(1)} %collective-permute-done.1.high_ref, ...), custom_call_target="tpu_custom_call" | custom-call | tf_op jit(solution)/shard_map/analysis/pallas_call | solution.py:346
Async XLA Ops:
  0.6 32.2 %copy-start.1 = (bf16[2,4,256,768]{3,2,1,0:T(8,128)(2,1)S(1)}, bf16[2,4,256,768]{3,2,1,0:T(8,128)(2,1)}, u32[]{:S(2)}) copy-start(bf16[2,4,256,768]{3,2,1,0:T(8,128)(2,1)} %constant.2.clone.table) | copy-start | bytes 9437188
  0.6 32.2 %copy-start.2 = (s32[16]{0:T(128)S(1)}, s32[16]{0:T(128)}, u32[]{:S(2)}) copy-start(s32[16]{0:T(128)} %blocks_ref.5) | copy-start | bytes 196
  0.7 32.2 %copy-start.3 = (f32[32]{0:T(128)S(1)}, f32[32]{0:T(128)}, u32[]{:S(2)}) copy-start(f32[32]{0:T(128)} %weights_ref.1) | copy-start | bytes 388
  47.2 9.4 %collective-permute-start.1 = (bf16[8,64,128]{2,1,0:T(8,128)(2,1)S(1)}, bf16[8,64,128]{2,1,0:T(8,128)(2,1)S(1)}, u32[]{:S(2)}, u32[]{:S(2)}) collective-permute-start(bf16[8,64,128]{2,1,0:T(8,128)(2,1)S(1)} %all_to_all.11.own_ref), channel_id=1, source_target_pairs={{8,0},{16,8},{24,16},{32,24},{40,32},{48,40},{56,48},{64,56},{72,6... | collective-permute-start | bytes 393224 | tf_op jit(solution)/shard_map/ppermute | solution.py:374
  52.8 9.9 %collective-permute-start = (bf16[8,64,128]{2,1,0:T(8,128)(2,1)S(1)}, bf16[8,64,128]{2,1,0:T(8,128)(2,1)S(1)}, u32[]{:S(2)}, u32[]{:S(2)}) collective-permute-start(bf16[8,64,128]{2,1,0:T(8,128)(2,1)S(1)} %all_to_all.11.own_ref), channel_id=1, source_target_pairs={{0,8},{8,16},{16,24},{24,32},{32,40},{40,48},{48,56},{56,64},{64,7... | collective-permute-start | bytes 393224 | tf_op jit(solution)/shard_map/ppermute | solution.py:373
  62.7 2.3 %copy-start = (bf16[17,64,2048]{2,1,0:T(8,128)(2,1)S(1)}, bf16[17,64,2048]{2,1,0:T(8,128)(2,1)}, u32[]{:S(2)}) copy-start(bf16[17,64,2048]{2,1,0:T(8,128)(2,1)} %leg_hbm.3) | copy-start | bytes 13369348

commit v3 on v2

--- a/solution.py
+++ b/solution.py
@@ -45,9 +45,14 @@
     return (s >= SPAN - lead).astype(jnp.int32)
 
 
-def spread_rows(leg, s, rows_scr):
+def spread_rows(table, chunks):
     for c in range(16):
-        rows_scr[pl.ds(c, 64, stride=16), :] = leg[s, :, c * 128 : (c + 1) * 128].astype(F32)
+        chunks[c * 72 : c * 72 + 64, :] = table[:, c * 128 : (c + 1) * 128].astype(F32)
+
+
+def group_rows(chunks, g):
+    pieces = [chunks[pl.ds(g * 4 + j, 16, stride=72), :] for j in range(4)]
+    return jnp.concatenate(pieces, axis=0).astype(BF16)
 
 
 def block_weights(rows, masks):
@@ -75,7 +80,10 @@
     return results
 
 
-def synth_kernel(blocks_ref, coef_hbm, leg_hbm, out_ref, coef, leg, sem_c, sem_l, rows_scr, acc, turned):
+def synth_kernel(
+    blocks_ref, coef_hbm, leg_hbm, out_ref, weights_hbm,
+    coef, leg, sem_c, sem_l, sem_w, chunks_even, chunks_odd, weights_even, weights_odd, values_even, values_odd, acc, turned,
+):
     def fetch(s):
         return (
             pltpu.make_async_copy(leg_hbm.at[s], leg.at[s], sem_l.at[s]),
@@ -93,25 +101,53 @@
     perm = lane_permutation()
     lower = lax.broadcasted_iota(jnp.int32, (24, 128), 1) < 64
 
-    def slot(s, carry):
+    def prepare(s, chunks, weights, values):
+        spread_rows(leg.at[s], chunks)
+        for g in range(GROUPS):
+            weights[g] = block_weights(group_rows(chunks, g), masks)
+        rows = jnp.concatenate(
+            [coef[s, :, :, g * 256 : (g + 1) * 256].reshape(24, 256) for g in range(GROUPS)], axis=0
+        )
+        rows = jnp.dot(rows, perm, preferred_element_type=F32)
+        for g in range(GROUPS):
+            part = rows[g * 24 : (g + 1) * 24]
+            values[g * 48 : (g + 1) * 48, :] = jnp.concatenate([part[:, :128], part[:, 128:]], axis=0).astype(BF16)
+
+    def combine(s, weights, values):
+        base = own_block(blocks_ref, s) * (GROUPS * 24)
+        for g in range(GROUPS):
+            term = jnp.dot(values[g * 48 : (g + 1) * 48, :], weights[g], preferred_element_type=F32)
+            where = pl.ds(pl.multiple_of(base + g * 24, 8), 24)
+            acc[where, :] = acc[where, :] + jnp.where(lower, term[:24], term[24:])
+
+    def arrive(s):
         for copy in fetch(s):
             copy.wait()
-        spread_rows(leg, s, rows_scr)
-        base = own_block(blocks_ref, s) * (GROUPS * 24)
-        values = jnp.concatenate(
-            [coef[s, :, :, g * 256 : (g + 1) * 256].reshape(24, 256) for g in range(GROUPS)], axis=0
-        )
-        values = jnp.dot(values, perm, preferred_element_type=F32)
-        for g in range(GROUPS):
-            weights = block_weights(rows_scr[g * 64 : (g + 1) * 64, :].astype(BF16), masks)
-            rows = slice(g * 24, (g + 1) * 24)
-            stacked = jnp.concatenate([values[rows, :128], values[rows, 128:]], axis=0).astype(BF16)
-            term = jnp.dot(stacked, weights, preferred_element_type=F32)
-            where = pl.ds(pl.multiple_of(base + g * 24, 8), 24)
-            acc[where, :] = acc[where, :] + jnp.where(lower, term[:24], term[24:])
-        return carry
-
-    lax.fori_loop(0, SLOTS, slot, 0)
+
+    def keep_even(t):
+        return pltpu.make_async_copy(weights_even.at[t], weights_hbm.at[2 * t], sem_w.at[2 * t])
+
+    def keep_odd(t):
+        return pltpu.make_async_copy(weights_odd.at[t], weights_hbm.at[2 * t + 1], sem_w.at[2 * t + 1])
+
+    arrive(0)
+    prepare(0, chunks_even, weights_even.at[0], values_even)
+
+    def pair(t, carry):
+        keep_even(t).start()
+        arrive(2 * t + 1)
+        arrive(2 * t + 2)
+        prepare(2 * t + 1, chunks_odd, weights_odd.at[t], values_odd)
+        combine(2 * t, weights_even.at[t], values_even)
+        prepare(2 * t + 2, chunks_even, weights_even.at[t + 1], values_even)
+        combine(2 * t + 1, weights_odd.at[t], values_odd)
+        keep_odd(t).start()
+        return carry
+
+    lax.fori_loop(0, SLOTS // 2, pair, 0)
+    last = SLOTS // 2
+    keep_even(last).start()
+    combine(SLOTS - 1, weights_even.at[last], values_even)
     for comp in range(3):
         for i in range(2):
             parts = []
@@ -125,6 +161,14 @@
             pieces = [turned[n, pl.ds(j * 32 + d, 4, stride=8), :] for n in range(6)]
             out_ref[d, j] = jnp.concatenate(pieces, axis=0).astype(BF16)
 
+    def finish(t, carry):
+        keep_even(t).wait()
+        keep_odd(t).wait()
+        return carry
+
+    lax.fori_loop(0, last, finish, 0)
+    keep_even(last).wait()
+
 
 def synthesis(m_blocks, coeffs, legendre):
     return pl.pallas_call(
@@ -134,14 +178,23 @@
             pl.BlockSpec(memory_space=pltpu.HBM),
             pl.BlockSpec(memory_space=pltpu.HBM),
         ],
-        out_specs=pl.BlockSpec(memory_space=pltpu.VMEM),
-        out_shape=jax.ShapeDtypeStruct((8, 4, 24, 128), BF16),
+        out_specs=[pl.BlockSpec(memory_space=pltpu.VMEM), pl.BlockSpec(memory_space=pltpu.HBM)],
+        out_shape=[
+            jax.ShapeDtypeStruct((8, 4, 24, 128), BF16),
+            jax.ShapeDtypeStruct((SLOTS, GROUPS, 128, 128), BF16),
+        ],
         scratch_shapes=[
             pltpu.VMEM((SLOTS, 12, 2, 4096), BF16),
             pltpu.VMEM((SLOTS, 64, 2048), BF16),
             pltpu.SemaphoreType.DMA((SLOTS,)),
             pltpu.SemaphoreType.DMA((SLOTS,)),
-            pltpu.VMEM((1024, 128), F32),
+            pltpu.SemaphoreType.DMA((SLOTS,)),
+            pltpu.VMEM((16 * 72, 128), F32),
+            pltpu.VMEM((16 * 72, 128), F32),
+            pltpu.VMEM((SLOTS // 2 + 1, GROUPS, 128, 128), BF16),
+            pltpu.VMEM((SLOTS // 2, GROUPS, 128, 128), BF16),
+            pltpu.VMEM((GROUPS * 48, 128), BF16),
+            pltpu.VMEM((GROUPS * 48, 128), BF16),
             pltpu.VMEM((2 * GROUPS * 24, 128), F32),
             pltpu.VMEM((6, 128, 128), F32),
         ],
@@ -256,11 +309,11 @@
 
 
 def analysis_kernel(
-    blocks_ref, own_ref, low_ref, high_ref, leg_hbm, plain_hbm, slope_hbm,
-    leg, sem_l, rows_scr, placed, turned, terms, out, sem_o,
+    blocks_ref, own_ref, low_ref, high_ref, weights_hbm, plain_hbm, slope_hbm,
+    weights, sem_w, placed, turned, terms, values_even, values_odd, out, sem_o,
 ):
     def fetch(s):
-        return pltpu.make_async_copy(leg_hbm.at[s], leg.at[s], sem_l.at[s])
+        return pltpu.make_async_copy(weights_hbm.at[s], weights.at[s], sem_w.at[s])
 
     def start(s, carry):
         fetch(s).start()
@@ -290,14 +343,16 @@
         for n in range(2):
             for i in range(2):
                 block = jnp.concatenate(columns[n * 2 + i], axis=0)
-                turned[n, (i * 2 + gh) * 128 : (i * 2 + gh + 1) * 128, :] = block.T
+                block = block.T
+                for quad in range(4):
+                    row = ((i * 2 + gh) * 4 + quad) * 40
+                    turned[n, row : row + 32, :] = block[quad * 32 : (quad + 1) * 32]
     lower = lax.broadcasted_iota(jnp.int32, (32, 128), 1) < 64
     for qg in range(2 * GROUPS):
-        pair = [turned[n, pl.ds(qg, 16, stride=32), :] for n in range(2)]
+        pair = [turned[n, pl.ds(qg, 16, stride=40), :] for n in range(2)]
         both = jnp.concatenate(pair, axis=0)
         halves = [jnp.where(lower, both, 0.0), jnp.where(lower, 0.0, both)]
         terms[qg] = jnp.concatenate(halves, axis=0).astype(BF16)
-    masks = lane_masks()
     perm = lane_permutation(back=True)
 
     def send(s):
@@ -307,29 +362,43 @@
             for i in range(2)
         ]
 
-    def slot(s, carry):
-        fetch(s).wait()
-        spread_rows(leg, s, rows_scr)
+    def expand(s, values):
         base = own_block(blocks_ref, s) * GROUPS
-        values = []
         for g in range(GROUPS):
-            weights = block_weights(rows_scr[g * 64 : (g + 1) * 64, :].astype(BF16), masks)
             value = lax.dot_general(
-                terms[base + g], weights, (((1,), (1,)), ((), ())), preferred_element_type=F32
+                terms[base + g], weights[s, g], (((1,), (1,)), ((), ())), preferred_element_type=F32
             )
-            values.append(jnp.concatenate([value[:32], value[32:]], axis=1).astype(BF16))
-        values = jnp.concatenate(values, axis=0)
-        values = jnp.dot(values, perm, preferred_element_type=F32).astype(BF16)
+            values[g * 32 : (g + 1) * 32, :] = jnp.concatenate([value[:32], value[32:]], axis=1).astype(BF16)
+
+    def order(s, values):
+        natural = jnp.dot(values[...], perm, preferred_element_type=F32).astype(BF16)
         for g in range(GROUPS):
             for n in range(2):
                 for i in range(2):
                     row = g * 32 + n * 16 + i * 8
-                    out[s, n, i, :, g * 256 : (g + 1) * 256] = values[row : row + 8]
+                    out[s, n, i, :, g * 256 : (g + 1) * 256] = natural[row : row + 8]
+
+    def leave(s):
         for copy in send(s):
             copy.start()
-        return carry
-
-    lax.fori_loop(0, SLOTS, slot, 0)
+
+    fetch(0).wait()
+    expand(0, values_even)
+
+    def pair(t, carry):
+        fetch(2 * t + 1).wait()
+        fetch(2 * t + 2).wait()
+        expand(2 * t + 1, values_odd)
+        order(2 * t, values_even)
+        expand(2 * t + 2, values_even)
+        order(2 * t + 1, values_odd)
+        leave(2 * t)
+        leave(2 * t + 1)
+        return carry
+
+    lax.fori_loop(0, SLOTS // 2, pair, 0)
+    order(SLOTS - 1, values_even)
+    leave(SLOTS - 1)
 
     def finish(s, carry):
         for copy in send(s):
@@ -339,7 +408,7 @@
     lax.fori_loop(0, SLOTS, finish, 0)
 
 
-def analysis(m_blocks, own, low, high, legendre):
+def analysis(m_blocks, own, low, high, weights):
     shape = jax.ShapeDtypeStruct((2, SLOTS, 8, 4096), BF16)
     vmem = pl.BlockSpec(memory_space=pltpu.VMEM)
     hbm = pl.BlockSpec(memory_space=pltpu.HBM)
@@ -349,30 +418,31 @@
         out_specs=[hbm, hbm],
         out_shape=[shape, shape],
         scratch_shapes=[
-            pltpu.VMEM((SLOTS, 64, 2048), BF16),
+            pltpu.VMEM((SLOTS, GROUPS, 128, 128), BF16),
             pltpu.SemaphoreType.DMA((SLOTS,)),
-            pltpu.VMEM((1024, 128), F32),
             pltpu.VMEM((3, 512, 128), F32),
-            pltpu.VMEM((2, 512, 128), F32),
+            pltpu.VMEM((2, 16 * 40, 128), F32),
             pltpu.VMEM((2 * GROUPS, 64, 128), BF16),
+            pltpu.VMEM((GROUPS * 32, 256), BF16),
+            pltpu.VMEM((GROUPS * 32, 256), BF16),
             pltpu.VMEM((SLOTS, 2, 2, 8, 4096), BF16),
             pltpu.SemaphoreType.DMA((SLOTS, 2, 2)),
         ],
-        compiler_params=pltpu.CompilerParams(vmem_limit_bytes=32 * 2**20),
+        compiler_params=pltpu.CompilerParams(vmem_limit_bytes=60 * 2**20),
         name="analysis",
-    )(m_blocks, own, low, high, legendre)
+    )(m_blocks, own, low, high, weights)
 
 
 def local(coeffs, legendre, lat_weights, m_blocks):
     table = jnp.asarray(quarter_table(), BF16)
-    sent = synthesis(m_blocks, coeffs.transpose(1, 2, 0, 3), legendre)
+    sent, weights = synthesis(m_blocks, coeffs.transpose(1, 2, 0, 3), legendre)
     received = lax.all_to_all(sent, "ma", split_axis=0, concat_axis=0, tiled=True)
     sent_back = azimuth(m_blocks, lat_weights, received, table)
     own = lax.all_to_all(sent_back, "ma", split_axis=0, concat_axis=0, tiled=True)
     count = lax.axis_size("row")
     low = lax.ppermute(own, "row", [(r, r + 1) for r in range(count - 1)])
     high = lax.ppermute(own, "row", [(r + 1, r) for r in range(count - 1)])
-    plain, slope = analysis(m_blocks, own, low, high, legendre)
+    plain, slope = analysis(m_blocks, own, low, high, weights)
     return plain.transpose(0, 2, 1, 3), slope.transpose(0, 2, 1, 3)
 
 

time: 80.8 us -> 72.3 us (0.89)
  Pallas kernels: 30.6 us -> 23.6 us
  local copies, waits for them, and re-layouts: 2.28 us -> 0.67 us
    pallas_call x1, Pallas kernels: 15.6 us -> 11.7 us  [analysis(): pl.pallas_call(analysis_kernel, in_specs=[pl.BlockSpec(memory_space=pltpu...]
    pallas_call x1, Pallas kernels: 12.7 us -> 9.56 us  [synthesis(): pl.pallas_call(synth_kernel, in_specs=[pl.BlockSpec(memory_space=pltpu.SM...]
    unnamed x8 -> x12, local copies, waits for them, and re-layouts: 2.28 us -> 0.67 us
where the time goes in v3:
time: 72.3 us; the launch traced here: 72 us
  blocking collectives  31.5 us (44%)
  Pallas kernels  23.6 us (33%)
  waiting for transfers between devices  7.94 us (11%)
  starting transfers between devices  7.56 us (10%)
    all_to_all x1, blocking collectives, local(): lax.all_to_all(sent, 'ma', split_axis=0, concat_axis=0, tiled=True)  19.5 us
    all_to_all x1, blocking collectives, local(): lax.all_to_all(sent_back, 'ma', split_axis=0, concat_axis=0, tiled=True)  12 us
    pallas_call x1, Pallas kernels, analysis(): pl.pallas_call(analysis_kernel, in_specs=[pl.BlockSpec(memory_space=pltpu...  11.7 us
    pallas_call x1, Pallas kernels, synthesis(): pl.pallas_call(synth_kernel, in_specs=[pl.BlockSpec(memory_space=pltpu.SM...  9.56 us
    ppermute x1, waiting for transfers between devices, local(): low = lax.ppermute(own, 'row', [(r, r + 1) for r in range(count - 1)])  6.11 us
    ppermute x1, starting transfers between devices, local(): high = lax.ppermute(own, 'row', [(r + 1, r) for r in range(count - 1)])  5.64 us
    pallas_call x1, Pallas kernels, azimuth(): pl.pallas_call(azimuth_kernel, in_specs=[pl.BlockSpec(memory_space=pltpu....  2.34 us
    ppermute x1, starting transfers between devices, local(): low = lax.ppermute(own, 'row', [(r, r + 1) for r in range(count - 1)])  1.92 us
  transfers between devices with their start and end apart: 2, of which 2 were waited for; matrix products, arithmetic and copies ran while one was open for 0% of the time, Pallas kernels for 0%

profile of v3, /device:TPU:6, one launch (start us, length us, event | category | flops | bytes accessed | tf_op | source)
XLA Modules:
  0.0 72.0 jit_solution(9070626844273059307)
XLA Ops:
  0.6 0.0 copy-start
  0.6 0.0 copy-start.1
  0.7 0.0 copy-start.2
  0.7 9.6 %synthesis.1 = (bf16[8,4,24,128]{3,2,1,0:T(8,128)(2,1)}, bf16[17,16,128,128]{3,2,1,0:T(8,128)(2,1)}) custom-call(s32[16]{0:T(128)} %blocks_ref.5, bf16[12,17,2,4096]{3,2,1,0:T(2,128)(2,1)} %bitcast.3, bf16[17,64,2048]{2,1,0:T(8,128)(2,1)} %leg_hbm.1), custom_call_target="tpu_custom_call" | custom-call | tf_op jit(solution)/shard_map/synthesis/pallas_call | solution.py:174
  10.2 19.5 %all_to_all.10.in_ref = bf16[8,4,24,128]{3,2,1,0:T(8,128)(2,1)S(1)} all-to-all(bf16[8,4,24,128]{3,2,1,0:T(8,128)(2,1)} %get-tuple-element.6), channel_id=1, replica_groups=mesh['row'=32,'ma'=8] {'ma'}, dimensions={0} | all-to-all | bytes 393216 | tf_op jit(solution)/shard_map/all_to_all | solution.py:439
  29.8 0.0 copy-done
  29.8 0.0 copy-done.1
  29.8 0.0 copy-done.2
  29.8 2.3 %azimuth.1 = bf16[8,64,128]{2,1,0:T(8,128)(2,1)S(1)} custom-call(s32[16]{0:T(128)S(1)} %copy-done.1, f32[32]{0:T(128)S(1)} %copy-done.2, bf16[8,4,24,128]{3,2,1,0:T(8,128)(2,1)S(1)} %all_to_all.10.in_ref, bf16[2,4,256,768]{3,2,1,0:T(8,128)(2,1)S(1)} %copy-done), custom_call_target="tpu_custom_call" | custom-call | tf_op jit(solution)/shard_map/azimuth/pallas_call | solution.py:289
  32.1 12.0 %all_to_all.11.own_ref = bf16[8,64,128]{2,1,0:T(8,128)(2,1)S(1)} all-to-all(bf16[8,64,128]{2,1,0:T(8,128)(2,1)S(1)} %azimuth.1), channel_id=1, replica_groups=mesh['row'=32,'ma'=8] {'ma'}, dimensions={0} | all-to-all | bytes 262144 | tf_op jit(solution)/shard_map/all_to_all | solution.py:441
  44.1 0.0 copy-start.3
  44.1 5.6 %collective-permute-start.1 = (bf16[8,64,128]{2,1,0:T(8,128)(2,1)S(1)}, bf16[8,64,128]{2,1,0:T(8,128)(2,1)S(1)}, u32[]{:S(2)}, u32[]{:S(2)}) collective-permute-start(bf16[8,64,128]{2,1,0:T(8,128)(2,1)S(1)} %all_to_all.11.own_ref), channel_id=1, source_target_pairs={{8,0},{16,8},{24,16},{32,24},{40,32},{48,40},{56,48},{64,56},{72,6... | collective-permute-start | bytes 393224 | tf_op jit(solution)/shard_map/ppermute | solution.py:444
  49.7 1.9 %collective-permute-start = (bf16[8,64,128]{2,1,0:T(8,128)(2,1)S(1)}, bf16[8,64,128]{2,1,0:T(8,128)(2,1)S(1)}, u32[]{:S(2)}, u32[]{:S(2)}) collective-permute-start(bf16[8,64,128]{2,1,0:T(8,128)(2,1)S(1)} %all_to_all.11.own_ref), channel_id=1, source_target_pairs={{0,8},{8,16},{16,24},{24,32},{32,40},{40,48},{48,56},{56,64},{64,7... | collective-permute-start | bytes 393224 | tf_op jit(solution)/shard_map/ppermute | solution.py:443
  51.7 1.8 %collective-permute-done.1.high_ref = bf16[8,64,128]{2,1,0:T(8,128)(2,1)S(1)} collective-permute-done((bf16[8,64,128]{2,1,0:T(8,128)(2,1)S(1)}, bf16[8,64,128]{2,1,0:T(8,128)(2,1)S(1)}, u32[]{:S(2)}, u32[]{:S(2)}) %collective-permute-start.1) | collective-permute-done | bytes 131104 | tf_op jit(solution)/shard_map/ppermute | solution.py:444
  53.5 0.0 copy-start.4
  53.5 6.1 %collective-permute-done.low_ref = bf16[8,64,128]{2,1,0:T(8,128)(2,1)S(1)} collective-permute-done((bf16[8,64,128]{2,1,0:T(8,128)(2,1)S(1)}, bf16[8,64,128]{2,1,0:T(8,128)(2,1)S(1)}, u32[]{:S(2)}, u32[]{:S(2)}) %collective-permute-start) | collective-permute-done | bytes 131104 | tf_op jit(solution)/shard_map/ppermute | solution.py:443
  59.6 0.0 copy-start.5
  59.6 0.0 copy-done.3
  59.6 0.0 copy-done.4
  59.6 0.6 copy-done.5
  60.3 11.7 %analysis.1 = (bf16[2,17,8,4096]{3,2,1,0:T(8,128)(2,1)}, bf16[2,17,8,4096]{3,2,1,0:T(8,128)(2,1)}) custom-call(s32[16]{0:T(128)} %blocks_ref.5, bf16[8,64,128]{2,1,0:T(8,128)(2,1)} %copy-done.3, bf16[8,64,128]{2,1,0:T(8,128)(2,1)} %copy-done.5, bf16[8,64,128]{2,1,0:T(8,128)(2,1)} %copy-done.4, bf16[17,16,128,128]{3,2,1,0:T(8,128)(2,1)} %get-tuple-element.7.weights_hbm), custom_call_target="tpu_custom_call" | custom-call | tf_op jit(solution)/shard_map/analysis/pallas_call | solution.py:415
Async XLA Ops:
  0.6 29.1 %copy-start = (bf16[2,4,256,768]{3,2,1,0:T(8,128)(2,1)S(1)}, bf16[2,4,256,768]{3,2,1,0:T(8,128)(2,1)}, u32[]{:S(2)}) copy-start(bf16[2,4,256,768]{3,2,1,0:T(8,128)(2,1)} %constant.2.clone.table) | copy-start | bytes 9437188
  0.6 29.1 %copy-start.1 = (s32[16]{0:T(128)S(1)}, s32[16]{0:T(128)}, u32[]{:S(2)}) copy-start(s32[16]{0:T(128)} %blocks_ref.5) | copy-start | bytes 196
  0.7 29.1 %copy-start.2 = (f32[32]{0:T(128)S(1)}, f32[32]{0:T(128)}, u32[]{:S(2)}) copy-start(f32[32]{0:T(128)} %weights_ref.1) | copy-start | bytes 388
  44.1 15.5 %copy-start.3 = (bf16[8,64,128]{2,1,0:T(8,128)(2,1)}, bf16[8,64,128]{2,1,0:T(8,128)(2,1)S(1)}, u32[]{:S(2)}) copy-start(bf16[8,64,128]{2,1,0:T(8,128)(2,1)S(1)} %all_to_all.11.own_ref) | copy-start | bytes 393220
  44.1 9.4 %collective-permute-start.1 = (bf16[8,64,128]{2,1,0:T(8,128)(2,1)S(1)}, bf16[8,64,128]{2,1,0:T(8,128)(2,1)S(1)}, u32[]{:S(2)}, u32[]{:S(2)}) collective-permute-start(bf16[8,64,128]{2,1,0:T(8,128)(2,1)S(1)} %all_to_all.11.own_ref), channel_id=1, source_target_pairs={{8,0},{16,8},{24,16},{32,24},{40,32},{48,40},{56,48},{64,56},{72,6... | collective-permute-start | bytes 393224 | tf_op jit(solution)/shard_map/ppermute | solution.py:444
  49.7 9.9 %collective-permute-start = (bf16[8,64,128]{2,1,0:T(8,128)(2,1)S(1)}, bf16[8,64,128]{2,1,0:T(8,128)(2,1)S(1)}, u32[]{:S(2)}, u32[]{:S(2)}) collective-permute-start(bf16[8,64,128]{2,1,0:T(8,128)(2,1)S(1)} %all_to_all.11.own_ref), channel_id=1, source_target_pairs={{0,8},{8,16},{16,24},{24,32},{32,40},{40,48},{48,56},{56,64},{64,7... | collective-permute-start | bytes 393224 | tf_op jit(solution)/shard_map/ppermute | solution.py:443
  53.5 6.1 %copy-start.4 = (bf16[8,64,128]{2,1,0:T(8,128)(2,1)}, bf16[8,64,128]{2,1,0:T(8,128)(2,1)S(1)}, u32[]{:S(2)}) copy-start(bf16[8,64,128]{2,1,0:T(8,128)(2,1)S(1)} %collective-permute-done.1.high_ref) | copy-start | bytes 393220
  59.6 0.7 copy-start.5

commit v4 on v3

--- a/solution.py
+++ b/solution.py
@@ -1,3 +1,4 @@
+import functools
 import math
 
 import jax
@@ -170,6 +171,10 @@
     keep_even(last).wait()
 
 
+def in_hbm(x):
+    return pltpu.with_memory_space_constraint(x, pltpu.HBM)
+
+
 def synthesis(m_blocks, coeffs, legendre):
     return pl.pallas_call(
         synth_kernel,
@@ -181,7 +186,7 @@
         out_specs=[pl.BlockSpec(memory_space=pltpu.VMEM), pl.BlockSpec(memory_space=pltpu.HBM)],
         out_shape=[
             jax.ShapeDtypeStruct((8, 4, 24, 128), BF16),
-            jax.ShapeDtypeStruct((SLOTS, GROUPS, 128, 128), BF16),
+            pltpu.HBM((SLOTS, GROUPS, 128, 128), BF16),
         ],
         scratch_shapes=[
             pltpu.VMEM((SLOTS, 12, 2, 4096), BF16),
@@ -200,7 +205,7 @@
         ],
         compiler_params=pltpu.CompilerParams(vmem_limit_bytes=60 * 2**20),
         name="synthesis",
-    )(m_blocks, coeffs, legendre)
+    )(m_blocks, in_hbm(coeffs), in_hbm(legendre))
 
 
 def azimuth_kernel(blocks_ref, weights_ref, in_ref, table, out_ref, even_c, odd_c, even_s, odd_s, folded):
@@ -308,19 +313,87 @@
     )(m_blocks, lat_weights, received, table)
 
 
-def analysis_kernel(
-    blocks_ref, own_ref, low_ref, high_ref, weights_hbm, plain_hbm, slope_hbm,
-    weights, sem_w, placed, turned, terms, values_even, values_odd, out, sem_o,
-):
+def turn_kernel(first, weights_hbm, out_hbm, weights, turned, sem_in, sem_out):
+    count = turned.shape[0]
+
     def fetch(s):
-        return pltpu.make_async_copy(weights_hbm.at[s], weights.at[s], sem_w.at[s])
+        return pltpu.make_async_copy(weights_hbm.at[first + s], weights.at[s], sem_in.at[s])
+
+    def leave(s):
+        return pltpu.make_async_copy(turned.at[s], out_hbm.at[s], sem_out.at[s])
 
     def start(s, carry):
         fetch(s).start()
         return carry
 
-    lax.fori_loop(0, SLOTS, start, 0)
-    for n, ref in enumerate((own_ref, low_ref, high_ref)):
+    lax.fori_loop(0, count, start, 0)
+    perm = lane_permutation(back=True)[:128, :128]
+
+    def slot(s, carry):
+        fetch(s).wait()
+        for g in range(0, GROUPS, 2):
+            one, two = weights[s, g], weights[s, g + 1]
+            both = jnp.concatenate(
+                [one[:64] + pltpu.roll(two[:64], 32, 1), pltpu.roll(one[64:], 96, 1) + two[64:]], axis=0
+            )
+            both = lax.dot_general(both, perm, (((0,), (0,)), ((), ())), preferred_element_type=F32)
+            for n in range(2):
+                rows = [both[(u * 2 + n) * 32 : (u * 2 + n + 1) * 32] for u in range(2)]
+                turned[s, g + n] = jnp.concatenate(rows, axis=0).astype(BF16)
+        leave(s).start()
+        return carry
+
+    lax.fori_loop(0, count, slot, 0)
+
+    def finish(s, carry):
+        leave(s).wait()
+        return carry
+
+    lax.fori_loop(0, count, finish, 0)
+
+
+def turn(weights, first, count):
+    shape = (count, GROUPS, 64, 128)
+    return pl.pallas_call(
+        functools.partial(turn_kernel, first),
+        in_specs=[pl.BlockSpec(memory_space=pltpu.HBM)],
+        out_specs=pl.BlockSpec(memory_space=pltpu.HBM),
+        out_shape=pltpu.HBM(shape, BF16),
+        scratch_shapes=[
+            pltpu.VMEM((count, GROUPS, 128, 128), BF16),
+            pltpu.VMEM(shape, BF16),
+            pltpu.SemaphoreType.DMA((count,)),
+            pltpu.SemaphoreType.DMA((count,)),
+        ],
+        compiler_params=pltpu.CompilerParams(vmem_limit_bytes=32 * 2**20),
+        cost_estimate=pl.CostEstimate(
+            flops=2 * count * GROUPS * 128**3, bytes_accessed=4 * count * GROUPS * 128**2, transcendentals=0
+        ),
+        name="turn",
+    )(in_hbm(weights))
+
+
+def analysis_kernel(
+    blocks_ref, *refs, count,
+):
+    messages = refs[:count]
+    first_hbm, second_hbm, out_hbm, weights, sem_w, placed, turned, terms, out, sem_o = refs[count:]
+    split = first_hbm.shape[0]
+
+    def fetch(s, source):
+        return pltpu.make_async_copy(source, weights.at[s], sem_w.at[s])
+
+    def start_first(s, carry):
+        fetch(s, first_hbm.at[s]).start()
+        return carry
+
+    def start_second(s, carry):
+        fetch(split + s, second_hbm.at[s]).start()
+        return carry
+
+    lax.fori_loop(0, split, start_first, 0)
+    lax.fori_loop(0, SLOTS - split, start_second, 0)
+    for n, ref in enumerate(messages):
         for d in range(8):
             for j in range(4):
                 for gh in range(2):
@@ -330,74 +403,68 @@
     def pick(n, gh, j, i):
         return placed[n, (gh * 4 + j) * 64 + i * 32 : (gh * 4 + j) * 64 + (i + 1) * 32, :]
 
+    row = lax.axis_index("row")
+    has_low, has_high = row > 0, row < lax.axis_size("row") - 1
+
+    def shells(gh, j):
+        own = [pick(0, gh, j, i) for i in range(2)]
+        if count == 1:
+            return own
+        low = [jnp.where(has_low, pick(1, gh, j, i), 0.0) for i in range(2)]
+        high = [jnp.where(has_high, pick(2, gh, j, i), 0.0) for i in range(2)]
+        return [
+            (low[0] - 8.0 * low[1] + 8.0 * own[1] - high[0]) / 12.0,
+            (low[1] - 8.0 * own[0] + 8.0 * high[0] - high[1]) / 12.0,
+        ]
+
     for gh in range(2):
-        columns = [[], [], [], []]
-        for j in range(4):
-            o0, o1 = pick(0, gh, j, 0), pick(0, gh, j, 1)
-            l0, l1 = pick(1, gh, j, 0), pick(1, gh, j, 1)
-            h0, h1 = pick(2, gh, j, 0), pick(2, gh, j, 1)
-            columns[0].append(o0)
-            columns[1].append(o1)
-            columns[2].append((l0 - 8.0 * l1 + 8.0 * o1 - h0) / 12.0)
-            columns[3].append((l1 - 8.0 * o0 + 8.0 * h0 - h1) / 12.0)
-        for n in range(2):
-            for i in range(2):
-                block = jnp.concatenate(columns[n * 2 + i], axis=0)
-                block = block.T
-                for quad in range(4):
-                    row = ((i * 2 + gh) * 4 + quad) * 40
-                    turned[n, row : row + 32, :] = block[quad * 32 : (quad + 1) * 32]
-    lower = lax.broadcasted_iota(jnp.int32, (32, 128), 1) < 64
+        columns = [shells(gh, j) for j in range(4)]
+        for i in range(2):
+            block = jnp.concatenate([columns[j][i] for j in range(4)], axis=0).T
+            for quad in range(4):
+                where = ((i * 2 + gh) * 4 + quad) * 40
+                turned[where : where + 32, :] = block[quad * 32 : (quad + 1) * 32]
+    lower = lax.broadcasted_iota(jnp.int32, (16, 128), 1) < 64
     for qg in range(2 * GROUPS):
-        pair = [turned[n, pl.ds(qg, 16, stride=40), :] for n in range(2)]
-        both = jnp.concatenate(pair, axis=0)
+        both = turned[pl.ds(qg, 16, stride=40), :]
         halves = [jnp.where(lower, both, 0.0), jnp.where(lower, 0.0, both)]
         terms[qg] = jnp.concatenate(halves, axis=0).astype(BF16)
-    perm = lane_permutation(back=True)
 
     def send(s):
-        return [
-            pltpu.make_async_copy(out.at[s, n, i], ref.at[i, s], sem_o.at[s, n, i])
-            for n, ref in enumerate((plain_hbm, slope_hbm))
-            for i in range(2)
-        ]
-
-    def expand(s, values):
+        return [pltpu.make_async_copy(out.at[s, i], out_hbm.at[i, s], sem_o.at[s, i]) for i in range(2)]
+
+    group = lax.broadcasted_iota(jnp.int32, (32, 128), 1) // 64
+    halves = [(group == j).astype(F32).astype(BF16) for j in range(2)]
+
+    def slot(s):
         base = own_block(blocks_ref, s) * GROUPS
         for g in range(GROUPS):
-            value = lax.dot_general(
-                terms[base + g], weights[s, g], (((1,), (1,)), ((), ())), preferred_element_type=F32
-            )
-            values[g * 32 : (g + 1) * 32, :] = jnp.concatenate([value[:32], value[32:]], axis=1).astype(BF16)
-
-    def order(s, values):
-        natural = jnp.dot(values[...], perm, preferred_element_type=F32).astype(BF16)
-        for g in range(GROUPS):
-            for n in range(2):
-                for i in range(2):
-                    row = g * 32 + n * 16 + i * 8
-                    out[s, n, i, :, g * 256 : (g + 1) * 256] = natural[row : row + 8]
+            narrow = weights[s, g]
+            blocks = [narrow[u * 32 : (u + 1) * 32] * halves[j] for u in range(2) for j in range(2)]
+            value = jnp.dot(terms[base + g], jnp.concatenate(blocks, axis=0), preferred_element_type=F32)
+            value = jnp.concatenate([value[:16], value[16:]], axis=1).astype(BF16)
+            for i in range(2):
+                out[s, i, :, g * 256 : (g + 1) * 256] = value[i * 8 : (i + 1) * 8]
+
+    def arrive(s):
+        fetch(s, first_hbm.at[0]).wait()
 
     def leave(s):
         for copy in send(s):
             copy.start()
 
-    fetch(0).wait()
-    expand(0, values_even)
-
     def pair(t, carry):
-        fetch(2 * t + 1).wait()
-        fetch(2 * t + 2).wait()
-        expand(2 * t + 1, values_odd)
-        order(2 * t, values_even)
-        expand(2 * t + 2, values_even)
-        order(2 * t + 1, values_odd)
+        arrive(2 * t)
+        arrive(2 * t + 1)
+        slot(2 * t)
+        slot(2 * t + 1)
         leave(2 * t)
         leave(2 * t + 1)
         return carry
 
     lax.fori_loop(0, SLOTS // 2, pair, 0)
-    order(SLOTS - 1, values_even)
+    arrive(SLOTS - 1)
+    slot(SLOTS - 1)
     leave(SLOTS - 1)
 
     def finish(s, carry):
@@ -408,41 +475,48 @@
     lax.fori_loop(0, SLOTS, finish, 0)
 
 
-def analysis(m_blocks, own, low, high, weights):
-    shape = jax.ShapeDtypeStruct((2, SLOTS, 8, 4096), BF16)
+def analysis(name, m_blocks, messages, first, second):
     vmem = pl.BlockSpec(memory_space=pltpu.VMEM)
     hbm = pl.BlockSpec(memory_space=pltpu.HBM)
+    count = len(messages)
     return pl.pallas_call(
-        analysis_kernel,
-        in_specs=[pl.BlockSpec(memory_space=pltpu.SMEM), vmem, vmem, vmem, hbm],
-        out_specs=[hbm, hbm],
-        out_shape=[shape, shape],
+        functools.partial(analysis_kernel, count=count),
+        in_specs=[pl.BlockSpec(memory_space=pltpu.SMEM)] + [vmem] * count + [hbm, hbm],
+        out_specs=hbm,
+        out_shape=jax.ShapeDtypeStruct((2, SLOTS, 8, 4096), BF16),
         scratch_shapes=[
-            pltpu.VMEM((SLOTS, GROUPS, 128, 128), BF16),
+            pltpu.VMEM((SLOTS, GROUPS, 64, 128), BF16),
             pltpu.SemaphoreType.DMA((SLOTS,)),
-            pltpu.VMEM((3, 512, 128), F32),
-            pltpu.VMEM((2, 16 * 40, 128), F32),
-            pltpu.VMEM((2 * GROUPS, 64, 128), BF16),
-            pltpu.VMEM((GROUPS * 32, 256), BF16),
-            pltpu.VMEM((GROUPS * 32, 256), BF16),
-            pltpu.VMEM((SLOTS, 2, 2, 8, 4096), BF16),
-            pltpu.SemaphoreType.DMA((SLOTS, 2, 2)),
-        ],
-        compiler_params=pltpu.CompilerParams(vmem_limit_bytes=60 * 2**20),
-        name="analysis",
-    )(m_blocks, own, low, high, weights)
+            pltpu.VMEM((count, 512, 128), F32),
+            pltpu.VMEM((16 * 40, 128), F32),
+            pltpu.VMEM((2 * GROUPS, 32, 128), BF16),
+            pltpu.VMEM((SLOTS, 2, 8, 4096), BF16),
+            pltpu.SemaphoreType.DMA((SLOTS, 2)),
+        ],
+        compiler_params=pltpu.CompilerParams(vmem_limit_bytes=24 * 2**20),
+        cost_estimate=pl.CostEstimate(
+            flops=2 * SLOTS * GROUPS * 32 * 128**2, bytes_accessed=12 * 2**20, transcendentals=0
+        ),
+        name=name,
+    )(m_blocks, *messages, in_hbm(first), in_hbm(second))
 
 
 def local(coeffs, legendre, lat_weights, m_blocks):
     table = jnp.asarray(quarter_table(), BF16)
     sent, weights = synthesis(m_blocks, coeffs.transpose(1, 2, 0, 3), legendre)
+    first = turn(weights, 0, 9)
     received = lax.all_to_all(sent, "ma", split_axis=0, concat_axis=0, tiled=True)
+    received, first, weights = lax.optimization_barrier((received, first, weights))
     sent_back = azimuth(m_blocks, lat_weights, received, table)
+    sent_back, weights = lax.optimization_barrier((sent_back, weights))
+    second = turn(weights, 9, 8)
     own = lax.all_to_all(sent_back, "ma", split_axis=0, concat_axis=0, tiled=True)
+    own, second = lax.optimization_barrier((own, second))
     count = lax.axis_size("row")
-    low = lax.ppermute(own, "row", [(r, r + 1) for r in range(count - 1)])
-    high = lax.ppermute(own, "row", [(r + 1, r) for r in range(count - 1)])
-    plain, slope = analysis(m_blocks, own, low, high, weights)
+    low = lax.ppermute(own, "row", [(r, (r + 1) % count) for r in range(count)])
+    high = lax.ppermute(own, "row", [((r + 1) % count, r) for r in range(count)])
+    plain = analysis("plain", m_blocks, [own], first, second)
+    slope = analysis("slope", m_blocks, [own, low, high], first, second)
     return plain.transpose(0, 2, 1, 3), slope.transpose(0, 2, 1, 3)
 
 

time: 72.3 us -> 65.5 us (0.906)
  the two profiles are of different devices: /device:TPU:6 before, /device:TPU:1 now
where the time goes in v4:
time: 65.5 us; the launch traced here: 65.2 us
  Pallas kernels  34.8 us (53%)
  starting transfers between devices  21.2 us (32%)
  waiting for transfers between devices  8.56 us (13%)
  between operations  0.68 us (1%)
    pallas_call x2, Pallas kernels, analysis(): pl.pallas_call(functools.partial(analysis_kernel, count=count), in_specs=...  12.2 us
    pallas_call x2, Pallas kernels, turn(): pl.pallas_call(functools.partial(turn_kernel, first), in_specs=[pl.BlockS...  10 us
    all_to_all x1, starting transfers between devices, local(): lax.all_to_all(sent, 'ma', split_axis=0, concat_axis=0, tiled=True)  9.98 us
    pallas_call x1, Pallas kernels, synthesis(): pl.pallas_call(synth_kernel, in_specs=[pl.BlockSpec(memory_space=pltpu.SM...  9.52 us
    all_to_all x1, starting transfers between devices, local(): lax.all_to_all(sent_back, 'ma', split_axis=0, concat_axis=0, tiled=True)  5.67 us
    ppermute x1, starting transfers between devices, local(): lax.ppermute(own, 'row', [((r + 1) % count, r) for r in range(count)])  5.53 us
    all_to_all x1, waiting for transfers between devices, local(): lax.all_to_all(sent, 'ma', split_axis=0, concat_axis=0, tiled=True)  3.37 us
    all_to_all x1, waiting for transfers between devices, local(): lax.all_to_all(sent_back, 'ma', split_axis=0, concat_axis=0, tiled=True)  3.28 us
  transfers between devices with their start and end apart: 4, of which 3 were waited for; matrix products, arithmetic and copies ran while one was open for 0% of the time, Pallas kernels for 25%

profile of v4, /device:TPU:1, one launch (start us, length us, event | category | flops | bytes accessed | tf_op | source)
XLA Modules:
  0.0 65.2 jit_solution(7667254010402604764)
XLA Ops:
  0.6 9.5 %synthesis.1 = (bf16[8,4,24,128]{3,2,1,0:T(8,128)(2,1)}, bf16[17,16,128,128]{3,2,1,0:T(8,128)(2,1)}) custom-call(s32[16]{0:T(128)} %blocks_ref.7, bf16[12,17,2,4096]{3,2,1,0:T(2,128)(2,1)} %bitcast.3, bf16[17,64,2048]{2,1,0:T(8,128)(2,1)} %leg_hbm.1), custom_call_target="tpu_custom_call" | custom-call | tf_op jit(solution)/shard_map/synthesis/pallas_call | solution.py:179
  10.2 10.0 %all-to-all-start = ((bf16[8,4,24,128]{3,2,1,0:T(8,128)(2,1)}), bf16[8,4,24,128]{3,2,1,0:T(8,128)(2,1)S(1)}, u32[]{:S(2)}, u32[]{:S(2)}) async-start(bf16[8,4,24,128]{3,2,1,0:T(8,128)(2,1)} %get-tuple-element.11), calls=%async_computation | async-start | bytes 393216 | tf_op jit(solution)/shard_map/all_to_all | solution.py:508
  20.1 0.0 copy-start
  20.1 0.0 copy-start.1
  20.1 0.0 copy-start.2
  20.1 5.3 %turn.2.refs_1_.refs_3_ = bf16[9,16,64,128]{3,2,1,0:T(8,128)(2,1)} custom-call(bf16[17,16,128,128]{3,2,1,0:T(8,128)(2,1)} %get-tuple-element.16.weights_hbm), custom_call_target="tpu_custom_call" | custom-call | flops 603979776 | bytes 9437184 | tf_op jit(solution)/shard_map/turn/pallas_call | solution.py:357
  25.4 3.4 %all-to-all-done.in_ref = bf16[8,4,24,128]{3,2,1,0:T(8,128)(2,1)S(1)} async-done(((bf16[8,4,24,128]{3,2,1,0:T(8,128)(2,1)}), bf16[8,4,24,128]{3,2,1,0:T(8,128)(2,1)S(1)}, u32[]{:S(2)}, u32[]{:S(2)}) %all-to-all-start) | async-done | bytes 196640 | tf_op jit(solution)/shard_map/all_to_all | solution.py:508
  28.8 0.0 copy-done
  28.8 0.0 copy-done.1
  28.8 0.0 copy-done.2
  28.8 3.0 %azimuth.1 = bf16[8,64,128]{2,1,0:T(8,128)(2,1)} custom-call(s32[16]{0:T(128)S(1)} %copy-done.1, f32[32]{0:T(128)S(1)} %copy-done.2, bf16[8,4,24,128]{3,2,1,0:T(8,128)(2,1)S(1)} %all-to-all-done.in_ref, bf16[2,4,256,768]{3,2,1,0:T(8,128)(2,1)S(1)} %copy-done), custom_call_target="tpu_custom_call" | custom-call | tf_op jit(solution)/shard_map/azimuth/pallas_call | solution.py:294
  31.8 5.7 %all-to-all-start.1 = ((bf16[8,64,128]{2,1,0:T(8,128)(2,1)}), bf16[8,64,128]{2,1,0:T(8,128)(2,1)S(1)}, u32[]{:S(2)}, u32[]{:S(2)}) async-start(bf16[8,64,128]{2,1,0:T(8,128)(2,1)} %azimuth.1), calls=%async_computation.1 | async-start | bytes 262144 | tf_op jit(solution)/shard_map/all_to_all | solution.py:513
  37.5 4.8 %turn.3.refs_2_.refs_4_ = bf16[8,16,64,128]{3,2,1,0:T(8,128)(2,1)} custom-call(bf16[17,16,128,128]{3,2,1,0:T(8,128)(2,1)} %get-tuple-element.16.weights_hbm), custom_call_target="tpu_custom_call" | custom-call | flops 536870912 | bytes 8388608 | tf_op jit(solution)/shard_map/turn/pallas_call | solution.py:357
  42.2 3.3 %all-to-all-done.1.refs_0_ = bf16[8,64,128]{2,1,0:T(8,128)(2,1)S(1)} async-done(((bf16[8,64,128]{2,1,0:T(8,128)(2,1)}), bf16[8,64,128]{2,1,0:T(8,128)(2,1)S(1)}, u32[]{:S(2)}, u32[]{:S(2)}) %all-to-all-start.1) | async-done | bytes 131104 | tf_op jit(solution)/shard_map/all_to_all | solution.py:513
  45.5 5.5 %collective-permute-start.1 = (bf16[8,64,128]{2,1,0:T(8,128)(2,1)S(1)}, bf16[8,64,128]{2,1,0:T(8,128)(2,1)S(1)}, u32[]{:S(2)}, u32[]{:S(2)}) collective-permute-start(bf16[8,64,128]{2,1,0:T(8,128)(2,1)S(1)} %all-to-all-done.1.refs_0_), channel_id=1, source_target_pairs={{8,0},{16,8},{24,16},{32,24},{40,32},{48,40},{56,48},{64,56},{72,6... | collective-permute-start | bytes 393224 | tf_op jit(solution)/shard_map/ppermute | solution.py:517
  51.1 0.0 collective-permute-start
  51.1 6.1 %plain.1 = bf16[2,17,8,4096]{3,2,1,0:T(8,128)(2,1)} custom-call(s32[16]{0:T(128)S(1)} %copy-done.1, bf16[8,64,128]{2,1,0:T(8,128)(2,1)S(1)} %all-to-all-done.1.refs_0_, bf16[9,16,64,128]{3,2,1,0:T(8,128)(2,1)} %turn.2.refs_1_.refs_3_, bf16[8,16,64,128]{3,2,1,0:T(8,128)(2,1)} %turn.3.refs_2_.refs_4_), custom_call_target="tpu_custom_call" | custom-call | flops 285212672 | bytes 12582912 | tf_op jit(solution)/shard_map/plain/pallas_call | solution.py:482
  57.2 0.0 collective-permute-done.1.refs_2_
  57.2 1.9 %collective-permute-done.refs_1_ = bf16[8,64,128]{2,1,0:T(8,128)(2,1)S(1)} collective-permute-done((bf16[8,64,128]{2,1,0:T(8,128)(2,1)S(1)}, bf16[8,64,128]{2,1,0:T(8,128)(2,1)S(1)}, u32[]{:S(2)}, u32[]{:S(2)}) %collective-permute-start) | collective-permute-done | bytes 131104 | tf_op jit(solution)/shard_map/ppermute | solution.py:516
  59.1 6.1 %slope.1 = bf16[2,17,8,4096]{3,2,1,0:T(8,128)(2,1)} custom-call(s32[16]{0:T(128)S(1)} %copy-done.1, bf16[8,64,128]{2,1,0:T(8,128)(2,1)S(1)} %all-to-all-done.1.refs_0_, bf16[8,64,128]{2,1,0:T(8,128)(2,1)S(1)} %collective-permute-done.refs_1_, bf16[8,64,128]{2,1,0:T(8,128)(2,1)S(1)} %collective-permute-done.1.refs_2_, ...), custom_call_target="tpu_custom_call" | custom-call | flops 285212672 | bytes 12582912 | tf_op jit(solution)/shard_map/slope/pallas_call | solution.py:482
Async XLA Ops:
  10.2 18.6 %all-to-all-start = ((bf16[8,4,24,128]{3,2,1,0:T(8,128)(2,1)}), bf16[8,4,24,128]{3,2,1,0:T(8,128)(2,1)S(1)}, u32[]{:S(2)}, u32[]{:S(2)}) async-start(bf16[8,4,24,128]{3,2,1,0:T(8,128)(2,1)} %get-tuple-element.11), calls=%async_computation | async-start | bytes 393216 | tf_op jit(solution)/shard_map/all_to_all | solution.py:508
  20.1 8.7 %copy-start = (bf16[2,4,256,768]{3,2,1,0:T(8,128)(2,1)S(1)}, bf16[2,4,256,768]{3,2,1,0:T(8,128)(2,1)}, u32[]{:S(2)}) copy-start(bf16[2,4,256,768]{3,2,1,0:T(8,128)(2,1)} %constant.2.clone.table) | copy-start | bytes 9437188
  20.1 8.7 %copy-start.1 = (s32[16]{0:T(128)S(1)}, s32[16]{0:T(128)}, u32[]{:S(2)}) copy-start(s32[16]{0:T(128)} %blocks_ref.7) | copy-start | bytes 196
  20.1 8.7 %copy-start.2 = (f32[32]{0:T(128)S(1)}, f32[32]{0:T(128)}, u32[]{:S(2)}) copy-start(f32[32]{0:T(128)} %weights_ref.1) | copy-start | bytes 388
  31.8 13.7 %all-to-all-start.1 = ((bf16[8,64,128]{2,1,0:T(8,128)(2,1)}), bf16[8,64,128]{2,1,0:T(8,128)(2,1)S(1)}, u32[]{:S(2)}, u32[]{:S(2)}) async-start(bf16[8,64,128]{2,1,0:T(8,128)(2,1)} %azimuth.1), calls=%async_computation.1 | async-start | bytes 262144 | tf_op jit(solution)/shard_map/all_to_all | solution.py:513
  45.5 11.7 %collective-permute-start.1 = (bf16[8,64,128]{2,1,0:T(8,128)(2,1)S(1)}, bf16[8,64,128]{2,1,0:T(8,128)(2,1)S(1)}, u32[]{:S(2)}, u32[]{:S(2)}) collective-permute-start(bf16[8,64,128]{2,1,0:T(8,128)(2,1)S(1)} %all-to-all-done.1.refs_0_), channel_id=1, source_target_pairs={{8,0},{16,8},{24,16},{32,24},{40,32},{48,40},{56,48},{64,56},{72,6... | collective-permute-start | bytes 393224 | tf_op jit(solution)/shard_map/ppermute | solution.py:517
  51.1 8.0 %collective-permute-start = (bf16[8,64,128]{2,1,0:T(8,128)(2,1)S(1)}, bf16[8,64,128]{2,1,0:T(8,128)(2,1)S(1)}, u32[]{:S(2)}, u32[]{:S(2)}) collective-permute-start(bf16[8,64,128]{2,1,0:T(8,128)(2,1)S(1)} %all-to-all-done.1.refs_0_), channel_id=1, source_target_pairs={{0,8},{8,16},{16,24},{24,32},{32,40},{40,48},{48,56},{56,64},{64,7... | collective-permute-start | bytes 393224 | tf_op jit(solution)/shard_map/ppermute | solution.py:516

commit v5 on v4

--- a/solution.py
+++ b/solution.py
@@ -15,6 +15,7 @@
 SLOTS = 17
 GROUPS = 16
 SPAN = 16
+BATCHES = ((0, 1), (1, 2), (3, 6), (9, 8))
 
 
 def lane_permutation(back=False):
@@ -82,21 +83,22 @@
 
 
 def synth_kernel(
-    blocks_ref, coef_hbm, leg_hbm, out_ref, weights_hbm,
-    coef, leg, sem_c, sem_l, sem_w, chunks_even, chunks_odd, weights_even, weights_odd, values_even, values_odd, acc, turned,
+    blocks_hbm, coef_hbm, leg_hbm, out_ref, weights_hbm,
+    blocks_ref, sem_b, coef, leg, sem_c, sem_l, sem_w, chunks_even, chunks_odd, weights_even, weights_odd, values_even, values_odd, acc, turned,
 ):
-    def fetch(s):
+    def fetch(n):
+        first, count = BATCHES[n]
+        slots = pl.ds(first, count)
         return (
-            pltpu.make_async_copy(leg_hbm.at[s], leg.at[s], sem_l.at[s]),
-            pltpu.make_async_copy(coef_hbm.at[:, s], coef.at[s], sem_c.at[s]),
+            pltpu.make_async_copy(leg_hbm.at[slots], leg.at[slots], sem_l.at[n]),
+            pltpu.make_async_copy(coef_hbm.at[:, slots], coef.at[:, slots], sem_c.at[n]),
         )
 
-    def start(s, carry):
-        for copy in fetch(s):
+    for n in range(len(BATCHES)):
+        for copy in fetch(n):
             copy.start()
-        return carry
-
-    lax.fori_loop(0, SLOTS, start, 0)
+    order = pltpu.make_async_copy(blocks_hbm, blocks_ref, sem_b)
+    order.start()
     acc[...] = jnp.zeros_like(acc)
     masks = lane_masks()
     perm = lane_permutation()
@@ -107,7 +109,7 @@
         for g in range(GROUPS):
             weights[g] = block_weights(group_rows(chunks, g), masks)
         rows = jnp.concatenate(
-            [coef[s, :, :, g * 256 : (g + 1) * 256].reshape(24, 256) for g in range(GROUPS)], axis=0
+            [coef[:, s, :, g * 256 : (g + 1) * 256].reshape(24, 256) for g in range(GROUPS)], axis=0
         )
         rows = jnp.dot(rows, perm, preferred_element_type=F32)
         for g in range(GROUPS):
@@ -121,8 +123,8 @@
             where = pl.ds(pl.multiple_of(base + g * 24, 8), 24)
             acc[where, :] = acc[where, :] + jnp.where(lower, term[:24], term[24:])
 
-    def arrive(s):
-        for copy in fetch(s):
+    def arrive(n):
+        for copy in fetch(n):
             copy.wait()
 
     def keep_even(t):
@@ -132,12 +134,13 @@
         return pltpu.make_async_copy(weights_odd.at[t], weights_hbm.at[2 * t + 1], sem_w.at[2 * t + 1])
 
     arrive(0)
+    order.wait()
     prepare(0, chunks_even, weights_even.at[0], values_even)
 
     def pair(t, carry):
         keep_even(t).start()
-        arrive(2 * t + 1)
-        arrive(2 * t + 2)
+        for n in range(1, len(BATCHES)):
+            pl.when(2 * t + 1 == BATCHES[n][0])(functools.partial(arrive, n))
         prepare(2 * t + 1, chunks_odd, weights_odd.at[t], values_odd)
         combine(2 * t, weights_even.at[t], values_even)
         prepare(2 * t + 2, chunks_even, weights_even.at[t + 1], values_even)
@@ -178,21 +181,19 @@
 def synthesis(m_blocks, coeffs, legendre):
     return pl.pallas_call(
         synth_kernel,
-        in_specs=[
-            pl.BlockSpec(memory_space=pltpu.SMEM),
-            pl.BlockSpec(memory_space=pltpu.HBM),
-            pl.BlockSpec(memory_space=pltpu.HBM),
-        ],
+        in_specs=[pl.BlockSpec(memory_space=pltpu.HBM)] * 3,
         out_specs=[pl.BlockSpec(memory_space=pltpu.VMEM), pl.BlockSpec(memory_space=pltpu.HBM)],
         out_shape=[
             jax.ShapeDtypeStruct((8, 4, 24, 128), BF16),
             pltpu.HBM((SLOTS, GROUPS, 128, 128), BF16),
         ],
         scratch_shapes=[
-            pltpu.VMEM((SLOTS, 12, 2, 4096), BF16),
+            pltpu.SMEM((16,), jnp.int32),
+            pltpu.SemaphoreType.DMA,
+            pltpu.VMEM((12, SLOTS, 2, 4096), BF16),
             pltpu.VMEM((SLOTS, 64, 2048), BF16),
-            pltpu.SemaphoreType.DMA((SLOTS,)),
-            pltpu.SemaphoreType.DMA((SLOTS,)),
+            pltpu.SemaphoreType.DMA((len(BATCHES),)),
+            pltpu.SemaphoreType.DMA((len(BATCHES),)),
             pltpu.SemaphoreType.DMA((SLOTS,)),
             pltpu.VMEM((16 * 72, 128), F32),
             pltpu.VMEM((16 * 72, 128), F32),
@@ -205,15 +206,10 @@
         ],
         compiler_params=pltpu.CompilerParams(vmem_limit_bytes=60 * 2**20),
         name="synthesis",
-    )(m_blocks, in_hbm(coeffs), in_hbm(legendre))
+    )(in_hbm(m_blocks), in_hbm(coeffs), in_hbm(legendre))
 
 
 def azimuth_kernel(blocks_ref, weights_ref, in_ref, table, out_ref, even_c, odd_c, even_s, odd_s, folded):
-    starts = [pl.multiple_of(blocks_ref[p] * 16, 16) for p in range(16)]
-
-    def basis(part, j):
-        return jnp.concatenate([table[part, j, pl.ds(start, 16), :] for start in starts], axis=0)
-
     lane_group = lax.broadcasted_iota(jnp.int32, (24, 128), 1) // 32
     left = []
     for j in range(4):
@@ -223,6 +219,11 @@
             halves.append(swap_lane_groups(parts, lane_group))
         both = [jnp.concatenate([halves[0][n], halves[1][n]], axis=1) for n in range(4)]
         left.append([jnp.concatenate([both[part * 2], both[part * 2 + 1]], axis=0).astype(BF16) for part in range(2)])
+    starts = [pl.multiple_of(blocks_ref[p] * 16, 16) for p in range(16)]
+
+    def basis(part, j):
+        return jnp.concatenate([table[part, j, pl.ds(start, 16), :] for start in starts], axis=0)
+
     for part, refs in ((0, (even_c, odd_c)), (1, (even_s, odd_s))):
         for parity in range(2):
             refs[parity][...] = jnp.dot(
@@ -293,12 +294,7 @@
     grid_shape = pltpu.VMEM((48, QUARTER), F32)
     return pl.pallas_call(
         azimuth_kernel,
-        in_specs=[
-            pl.BlockSpec(memory_space=pltpu.SMEM),
-            pl.BlockSpec(memory_space=pltpu.SMEM),
-            pl.BlockSpec(memory_space=pltpu.VMEM),
-            pl.BlockSpec(memory_space=pltpu.VMEM),
-        ],
+        in_specs=[pl.BlockSpec(memory_space=pltpu.SMEM)] * 2 + [pl.BlockSpec(memory_space=pltpu.VMEM)] * 2,
         out_specs=pl.BlockSpec(memory_space=pltpu.VMEM),
         out_shape=jax.ShapeDtypeStruct((8, 64, 128), BF16),
         scratch_shapes=[
@@ -373,26 +369,26 @@
     )(in_hbm(weights))
 
 
-def analysis_kernel(
-    blocks_ref, *refs, count,
-):
+def analysis_kernel(blocks_hbm, *refs, count):
     messages = refs[:count]
-    first_hbm, second_hbm, out_hbm, weights, sem_w, placed, turned, terms, out, sem_o = refs[count:]
-    split = first_hbm.shape[0]
-
-    def fetch(s, source):
-        return pltpu.make_async_copy(source, weights.at[s], sem_w.at[s])
-
-    def start_first(s, carry):
-        fetch(s, first_hbm.at[s]).start()
-        return carry
-
-    def start_second(s, carry):
-        fetch(split + s, second_hbm.at[s]).start()
-        return carry
-
-    lax.fori_loop(0, split, start_first, 0)
-    lax.fori_loop(0, SLOTS - split, start_second, 0)
+    if count == 1:
+        first_hbm, second_hbm, out_hbm, weights, blocks_ref, sem_b, sem_w, placed, turned, terms, out, sem_o = refs[1:]
+    else:
+        weights, out_hbm, blocks_ref, sem_b, placed, turned, terms, out, sem_o = refs[count:]
+    order = pltpu.make_async_copy(blocks_hbm, blocks_ref, sem_b)
+    order.start()
+    if count == 1:
+        split = first_hbm.shape[0]
+        batches = ((first_hbm, 0, 0, 2), (first_hbm, 2, 2, split - 2), (second_hbm, 0, split, SLOTS - split))
+    else:
+        batches = ()
+
+    def fetch(n):
+        source, at, first, number = batches[n]
+        return pltpu.make_async_copy(source.at[pl.ds(at, number)], weights.at[pl.ds(first, number)], sem_w.at[n])
+
+    for n in range(len(batches)):
+        fetch(n).start()
     for n, ref in enumerate(messages):
         for d in range(8):
             for j in range(4):
@@ -425,80 +421,84 @@
                 where = ((i * 2 + gh) * 4 + quad) * 40
                 turned[where : where + 32, :] = block[quad * 32 : (quad + 1) * 32]
     lower = lax.broadcasted_iota(jnp.int32, (16, 128), 1) < 64
+    terms[...] = jnp.zeros_like(terms)
     for qg in range(2 * GROUPS):
         both = turned[pl.ds(qg, 16, stride=40), :]
         halves = [jnp.where(lower, both, 0.0), jnp.where(lower, 0.0, both)]
-        terms[qg] = jnp.concatenate(halves, axis=0).astype(BF16)
-
-    def send(s):
-        return [pltpu.make_async_copy(out.at[s, i], out_hbm.at[i, s], sem_o.at[s, i]) for i in range(2)]
+        n = qg % 2
+        terms[qg // 2, n * 32 : (n + 1) * 32, n * 128 : (n + 1) * 128] = jnp.concatenate(halves, axis=0).astype(BF16)
+
+    def send(first, count):
+        slots = pl.ds(first, count)
+        return [pltpu.make_async_copy(out.at[i, slots], out_hbm.at[i, slots], sem_o.at[i]) for i in range(2)]
+
+    def leave(first, count):
+        for copy in send(first, count):
+            copy.start()
 
     group = lax.broadcasted_iota(jnp.int32, (32, 128), 1) // 64
     halves = [(group == j).astype(F32).astype(BF16) for j in range(2)]
 
     def slot(s):
-        base = own_block(blocks_ref, s) * GROUPS
-        for g in range(GROUPS):
-            narrow = weights[s, g]
-            blocks = [narrow[u * 32 : (u + 1) * 32] * halves[j] for u in range(2) for j in range(2)]
-            value = jnp.dot(terms[base + g], jnp.concatenate(blocks, axis=0), preferred_element_type=F32)
-            value = jnp.concatenate([value[:16], value[16:]], axis=1).astype(BF16)
-            for i in range(2):
-                out[s, i, :, g * 256 : (g + 1) * 256] = value[i * 8 : (i + 1) * 8]
-
-    def arrive(s):
-        fetch(s, first_hbm.at[0]).wait()
-
-    def leave(s):
-        for copy in send(s):
-            copy.start()
+        base = own_block(blocks_ref, s) * (GROUPS // 2)
+        for g in range(0, GROUPS, 2):
+            blocks = [
+                weights[s, g + n, u * 32 : (u + 1) * 32] * halves[j]
+                for n in range(2) for u in range(2) for j in range(2)
+            ]
+            value = jnp.dot(terms[base + g // 2], jnp.concatenate(blocks, axis=0), preferred_element_type=F32)
+            for n in range(2):
+                part = [value[(n * 2 + u) * 16 : (n * 2 + u + 1) * 16] for u in range(2)]
+                part = jnp.concatenate(part, axis=1).astype(BF16)
+                for i in range(2):
+                    out[i, s, :, (g + n) * 256 : (g + n + 1) * 256] = part[i * 8 : (i + 1) * 8]
+
+    order.wait()
 
     def pair(t, carry):
-        arrive(2 * t)
-        arrive(2 * t + 1)
+        for n in range(len(batches)):
+            need = batches[n][2] // 2
+            pl.when(t == need)(lambda n=n: fetch(n).wait())
         slot(2 * t)
         slot(2 * t + 1)
-        leave(2 * t)
-        leave(2 * t + 1)
+        leave(2 * t, 2)
         return carry
 
     lax.fori_loop(0, SLOTS // 2, pair, 0)
-    arrive(SLOTS - 1)
     slot(SLOTS - 1)
-    leave(SLOTS - 1)
-
-    def finish(s, carry):
-        for copy in send(s):
-            copy.wait()
-        return carry
-
-    lax.fori_loop(0, SLOTS, finish, 0)
-
-
-def analysis(name, m_blocks, messages, first, second):
+    leave(SLOTS - 1, 1)
+    for copy in send(0, SLOTS):
+        copy.wait()
+
+
+def analysis(name, m_blocks, messages, weights):
     vmem = pl.BlockSpec(memory_space=pltpu.VMEM)
     hbm = pl.BlockSpec(memory_space=pltpu.HBM)
     count = len(messages)
+    plain = count == 1
+    out_shape = pltpu.HBM((2, SLOTS, 8, 4096), BF16)
+    shape = (SLOTS, GROUPS, 64, 128)
     return pl.pallas_call(
         functools.partial(analysis_kernel, count=count),
-        in_specs=[pl.BlockSpec(memory_space=pltpu.SMEM)] + [vmem] * count + [hbm, hbm],
-        out_specs=hbm,
-        out_shape=jax.ShapeDtypeStruct((2, SLOTS, 8, 4096), BF16),
+        in_specs=[hbm] + [vmem] * count + ([hbm, hbm] if plain else [vmem]),
+        out_specs=[hbm, vmem] if plain else hbm,
+        out_shape=[out_shape, pltpu.VMEM(shape, BF16)] if plain else out_shape,
         scratch_shapes=[
-            pltpu.VMEM((SLOTS, GROUPS, 64, 128), BF16),
-            pltpu.SemaphoreType.DMA((SLOTS,)),
+            pltpu.SMEM((16,), jnp.int32),
+            pltpu.SemaphoreType.DMA,
+            *([pltpu.SemaphoreType.DMA((3,))] if plain else []),
             pltpu.VMEM((count, 512, 128), F32),
             pltpu.VMEM((16 * 40, 128), F32),
-            pltpu.VMEM((2 * GROUPS, 32, 128), BF16),
-            pltpu.VMEM((SLOTS, 2, 8, 4096), BF16),
-            pltpu.SemaphoreType.DMA((SLOTS, 2)),
+            pltpu.VMEM((GROUPS, 64, 256), BF16),
+            pltpu.VMEM((2, SLOTS, 8, 4096), BF16),
+            pltpu.SemaphoreType.DMA((2,)),
         ],
         compiler_params=pltpu.CompilerParams(vmem_limit_bytes=24 * 2**20),
         cost_estimate=pl.CostEstimate(
             flops=2 * SLOTS * GROUPS * 32 * 128**2, bytes_accessed=12 * 2**20, transcendentals=0
         ),
         name=name,
-    )(m_blocks, *messages, in_hbm(first), in_hbm(second))
+    )(in_hbm(m_blocks), *messages, *(in_hbm(w) if plain else pltpu.with_memory_space_constraint(w, pltpu.VMEM) for w in weights))
 
 
 def local(coeffs, legendre, lat_weights, m_blocks):
@@ -515,8 +515,8 @@
     count = lax.axis_size("row")
     low = lax.ppermute(own, "row", [(r, (r + 1) % count) for r in range(count)])
     high = lax.ppermute(own, "row", [((r + 1) % count, r) for r in range(count)])
-    plain = analysis("plain", m_blocks, [own], first, second)
-    slope = analysis("slope", m_blocks, [own, low, high], first, second)
+    plain, kept = analysis("plain", m_blocks, [own], [first, second])
+    slope = analysis("slope", m_blocks, [own, low, high], [kept])
     return plain.transpose(0, 2, 1, 3), slope.transpose(0, 2, 1, 3)
 
 

time: 65.5 us -> 62.6 us (0.956)
  Pallas kernels: 34.8 us -> 30.5 us
  waiting for transfers between devices: 8.56 us -> 9.98 us
    pallas_call x2, Pallas kernels: 12.2 us -> 8.77 us  [analysis(): pl.pallas_call(functools.partial(analysis_kernel, count=count), in_specs=...]
    ppermute x1, waiting for transfers between devices: 1.91 us -> 3.32 us  [local(): low = lax.ppermute(own, 'row', [(r, (r + 1) % count) for r in range(count)])]
    pallas_call x1, Pallas kernels: 9.52 us -> 8.67 us  [synthesis(): pl.pallas_call(synth_kernel, in_specs=[pl.BlockSpec(memory_space=pltpu.HB...]
  transfers between devices with their start and end apart: 4 -> 4, of which waited for: 3 -> 3; matrix products, arithmetic and copies ran while one was open for 0% -> 0% of each run, Pallas kernels for 25% -> 24%
where the time goes in v5:
time: 62.6 us; the launch traced here: 62.3 us
  Pallas kernels  30.5 us (49%)
  starting transfers between devices  21.2 us (34%)
  waiting for transfers between devices  9.98 us (16%)
  between operations  0.68 us (1%)
    pallas_call x2, Pallas kernels, turn(): pl.pallas_call(functools.partial(turn_kernel, first), in_specs=[pl.BlockS...  10 us
    all_to_all x1, starting transfers between devices, local(): lax.all_to_all(sent, 'ma', split_axis=0, concat_axis=0, tiled=True)  9.98 us
    pallas_call x2, Pallas kernels, analysis(): pl.pallas_call(functools.partial(analysis_kernel, count=count), in_specs=...  8.77 us
    pallas_call x1, Pallas kernels, synthesis(): pl.pallas_call(synth_kernel, in_specs=[pl.BlockSpec(memory_space=pltpu.HB...  8.67 us
    all_to_all x1, starting transfers between devices, local(): lax.all_to_all(sent_back, 'ma', split_axis=0, concat_axis=0, tiled=True)  5.67 us
    ppermute x1, starting transfers between devices, local(): lax.ppermute(own, 'row', [((r + 1) % count, r) for r in range(count)])  5.53 us
    all_to_all x1, waiting for transfers between devices, local(): lax.all_to_all(sent, 'ma', split_axis=0, concat_axis=0, tiled=True)  3.35 us
    ppermute x1, waiting for transfers between devices, local(): low = lax.ppermute(own, 'row', [(r, (r + 1) % count) for r in range(count)])  3.32 us
  transfers between devices with their start and end apart: 4, of which 3 were waited for; matrix products, arithmetic and copies ran while one was open for 0% of the time, Pallas kernels for 24%

profile of v5, /device:TPU:1, one launch (start us, length us, event | category | flops | bytes accessed | tf_op | source)
XLA Modules:
  0.0 62.3 jit_solution(16161073110412854118)
XLA Ops:
  0.6 8.7 %synthesis.1 = (bf16[8,4,24,128]{3,2,1,0:T(8,128)(2,1)}, bf16[17,16,128,128]{3,2,1,0:T(8,128)(2,1)}) custom-call(s32[16]{0:T(128)} %blocks_hbm.5, bf16[12,17,2,4096]{3,2,1,0:T(2,128)(2,1)} %bitcast.3, bf16[17,64,2048]{2,1,0:T(8,128)(2,1)} %leg_hbm.1), custom_call_target="tpu_custom_call" | custom-call | tf_op jit(solution)/shard_map/synthesis/pallas_call | solution.py:182
  9.3 10.0 %all-to-all-start = ((bf16[8,4,24,128]{3,2,1,0:T(8,128)(2,1)}), bf16[8,4,24,128]{3,2,1,0:T(8,128)(2,1)S(1)}, u32[]{:S(2)}, u32[]{:S(2)}) async-start(bf16[8,4,24,128]{3,2,1,0:T(8,128)(2,1)} %get-tuple-element.13), calls=%async_computation | async-start | bytes 393216 | tf_op jit(solution)/shard_map/all_to_all | solution.py:508
  19.3 0.0 copy-start
  19.3 0.0 copy-start.1
  19.3 0.0 copy-start.2
  19.3 5.3 %turn.2.refs_1_ = bf16[9,16,64,128]{3,2,1,0:T(8,128)(2,1)} custom-call(bf16[17,16,128,128]{3,2,1,0:T(8,128)(2,1)} %get-tuple-element.18.weights_hbm), custom_call_target="tpu_custom_call" | custom-call | flops 603979776 | bytes 9437184 | tf_op jit(solution)/shard_map/turn/pallas_call | solution.py:353
  24.6 3.4 %all-to-all-done.in_ref = bf16[8,4,24,128]{3,2,1,0:T(8,128)(2,1)S(1)} async-done(((bf16[8,4,24,128]{3,2,1,0:T(8,128)(2,1)}), bf16[8,4,24,128]{3,2,1,0:T(8,128)(2,1)S(1)}, u32[]{:S(2)}, u32[]{:S(2)}) %all-to-all-start) | async-done | bytes 196640 | tf_op jit(solution)/shard_map/all_to_all | solution.py:508
  27.9 0.0 copy-done
  27.9 0.0 copy-done.1
  28.0 0.0 copy-done.2
  28.0 3.0 %azimuth.1 = bf16[8,64,128]{2,1,0:T(8,128)(2,1)} custom-call(s32[16]{0:T(128)S(1)} %copy-done.1, f32[32]{0:T(128)S(1)} %copy-done.2, bf16[8,4,24,128]{3,2,1,0:T(8,128)(2,1)S(1)} %all-to-all-done.in_ref, bf16[2,4,256,768]{3,2,1,0:T(8,128)(2,1)S(1)} %copy-done), custom_call_target="tpu_custom_call" | custom-call | tf_op jit(solution)/shard_map/azimuth/pallas_call | solution.py:295
  31.0 5.7 %all-to-all-start.1 = ((bf16[8,64,128]{2,1,0:T(8,128)(2,1)}), bf16[8,64,128]{2,1,0:T(8,128)(2,1)S(1)}, u32[]{:S(2)}, u32[]{:S(2)}) async-start(bf16[8,64,128]{2,1,0:T(8,128)(2,1)} %azimuth.1), calls=%async_computation.1 | async-start | bytes 262144 | tf_op jit(solution)/shard_map/all_to_all | solution.py:513
  36.6 4.7 %turn.3.refs_2_ = bf16[8,16,64,128]{3,2,1,0:T(8,128)(2,1)} custom-call(bf16[17,16,128,128]{3,2,1,0:T(8,128)(2,1)} %get-tuple-element.18.weights_hbm), custom_call_target="tpu_custom_call" | custom-call | flops 536870912 | bytes 8388608 | tf_op jit(solution)/shard_map/turn/pallas_call | solution.py:353
  41.4 3.3 %all-to-all-done.1.refs_0_ = bf16[8,64,128]{2,1,0:T(8,128)(2,1)S(1)} async-done(((bf16[8,64,128]{2,1,0:T(8,128)(2,1)}), bf16[8,64,128]{2,1,0:T(8,128)(2,1)S(1)}, u32[]{:S(2)}, u32[]{:S(2)}) %all-to-all-start.1) | async-done | bytes 131104 | tf_op jit(solution)/shard_map/all_to_all | solution.py:513
  44.7 5.5 %collective-permute-start.1 = (bf16[8,64,128]{2,1,0:T(8,128)(2,1)S(1)}, bf16[8,64,128]{2,1,0:T(8,128)(2,1)S(1)}, u32[]{:S(2)}, u32[]{:S(2)}) collective-permute-start(bf16[8,64,128]{2,1,0:T(8,128)(2,1)S(1)} %all-to-all-done.1.refs_0_), channel_id=1, source_target_pairs={{8,0},{16,8},{24,16},{32,24},{40,32},{48,40},{56,48},{64,56},{72,6... | collective-permute-start | bytes 393224 | tf_op jit(solution)/shard_map/ppermute | solution.py:517
  50.2 0.0 collective-permute-start
  50.2 4.7 %plain.1 = (bf16[2,17,8,4096]{3,2,1,0:T(8,128)(2,1)}, bf16[17,16,64,128]{3,2,1,0:T(8,128)(2,1)S(1)}) custom-call(s32[16]{0:T(128)} %blocks_hbm.5, bf16[8,64,128]{2,1,0:T(8,128)(2,1)S(1)} %all-to-all-done.1.refs_0_, bf16[9,16,64,128]{3,2,1,0:T(8,128)(2,1)} %turn.2.refs_1_, bf16[8,16,64,128]{3,2,1,0:T(8,128)(2,1)} %turn.3.refs_2_), custom_call_target="tpu_custom_call" | custom-call | flops 285212672 | bytes 12582912 | tf_op jit(solution)/shard_map/plain/pallas_call | solution.py:481
  54.9 0.0 collective-permute-done.1.refs_2_
  54.9 3.3 %collective-permute-done.refs_1_ = bf16[8,64,128]{2,1,0:T(8,128)(2,1)S(1)} collective-permute-done((bf16[8,64,128]{2,1,0:T(8,128)(2,1)S(1)}, bf16[8,64,128]{2,1,0:T(8,128)(2,1)S(1)}, u32[]{:S(2)}, u32[]{:S(2)}) %collective-permute-start) | collective-permute-done | bytes 131104 | tf_op jit(solution)/shard_map/ppermute | solution.py:516
  58.2 4.1 %slope.1 = bf16[2,17,8,4096]{3,2,1,0:T(8,128)(2,1)} custom-call(s32[16]{0:T(128)} %blocks_hbm.5, bf16[8,64,128]{2,1,0:T(8,128)(2,1)S(1)} %all-to-all-done.1.refs_0_, bf16[8,64,128]{2,1,0:T(8,128)(2,1)S(1)} %collective-permute-done.refs_1_, bf16[8,64,128]{2,1,0:T(8,128)(2,1)S(1)} %collective-permute-done.1.refs_2_, ...), custom_call_target="tpu_custom_call" | custom-call | flops 285212672 | bytes 12582912 | tf_op jit(solution)/shard_map/slope/pallas_call | solution.py:481
Async XLA Ops:
  9.3 18.6 %all-to-all-start = ((bf16[8,4,24,128]{3,2,1,0:T(8,128)(2,1)}), bf16[8,4,24,128]{3,2,1,0:T(8,128)(2,1)S(1)}, u32[]{:S(2)}, u32[]{:S(2)}) async-start(bf16[8,4,24,128]{3,2,1,0:T(8,128)(2,1)} %get-tuple-element.13), calls=%async_computation | async-start | bytes 393216 | tf_op jit(solution)/shard_map/all_to_all | solution.py:508
  19.3 8.7 %copy-start = (bf16[2,4,256,768]{3,2,1,0:T(8,128)(2,1)S(1)}, bf16[2,4,256,768]{3,2,1,0:T(8,128)(2,1)}, u32[]{:S(2)}) copy-start(bf16[2,4,256,768]{3,2,1,0:T(8,128)(2,1)} %constant.2.clone.table) | copy-start | bytes 9437188
  19.3 8.7 %copy-start.1 = (s32[16]{0:T(128)S(1)}, s32[16]{0:T(128)}, u32[]{:S(2)}) copy-start(s32[16]{0:T(128)} %blocks_hbm.5) | copy-start | bytes 196
  19.3 8.7 %copy-start.2 = (f32[32]{0:T(128)S(1)}, f32[32]{0:T(128)}, u32[]{:S(2)}) copy-start(f32[32]{0:T(128)} %weights_ref.1) | copy-start | bytes 388
  31.0 13.7 %all-to-all-start.1 = ((bf16[8,64,128]{2,1,0:T(8,128)(2,1)}), bf16[8,64,128]{2,1,0:T(8,128)(2,1)S(1)}, u32[]{:S(2)}, u32[]{:S(2)}) async-start(bf16[8,64,128]{2,1,0:T(8,128)(2,1)} %azimuth.1), calls=%async_computation.1 | async-start | bytes 262144 | tf_op jit(solution)/shard_map/all_to_all | solution.py:513
  44.7 10.2 %collective-permute-start.1 = (bf16[8,64,128]{2,1,0:T(8,128)(2,1)S(1)}, bf16[8,64,128]{2,1,0:T(8,128)(2,1)S(1)}, u32[]{:S(2)}, u32[]{:S(2)}) collective-permute-start(bf16[8,64,128]{2,1,0:T(8,128)(2,1)S(1)} %all-to-all-done.1.refs_0_), channel_id=1, source_target_pairs={{8,0},{16,8},{24,16},{32,24},{40,32},{48,40},{56,48},{64,56},{72,6... | collective-permute-start | bytes 393224 | tf_op jit(solution)/shard_map/ppermute | solution.py:517
  50.2 8.0 %collective-permute-start = (bf16[8,64,128]{2,1,0:T(8,128)(2,1)S(1)}, bf16[8,64,128]{2,1,0:T(8,128)(2,1)S(1)}, u32[]{:S(2)}, u32[]{:S(2)}) collective-permute-start(bf16[8,64,128]{2,1,0:T(8,128)(2,1)S(1)} %all-to-all-done.1.refs_0_), channel_id=1, source_target_pairs={{0,8},{8,16},{16,24},{24,32},{32,40},{40,48},{48,56},{56,64},{64,7... | collective-permute-start | bytes 393224 | tf_op jit(solution)/shard_map/ppermute | solution.py:516

commit v6 on v5

--- a/solution.py
+++ b/solution.py
@@ -15,14 +15,19 @@
 SLOTS = 17
 GROUPS = 16
 SPAN = 16
+PITCH = 132
 BATCHES = ((0, 1), (1, 2), (3, 6), (9, 8))
 
 
 def lane_permutation(back=False):
-    natural = lax.broadcasted_iota(jnp.int32, (256, 256), 1 if back else 0)
-    grouped = lax.broadcasted_iota(jnp.int32, (256, 256), 0 if back else 1)
-    target = natural // 64 * 64 + natural % 4 * 16 + natural % 64 // 4
-    return (target == grouped).astype(F32).astype(BF16)
+    natural = lax.broadcasted_iota(jnp.int32, (128, 128), 1 if back else 0)
+    grouped = lax.broadcasted_iota(jnp.int32, (128, 128), 0 if back else 1)
+    c = natural % 64 // 4
+    matrices = []
+    for u in range(2):
+        target = natural // 64 * 64 + (natural + 2 * u) % 4 * 16 + c % 2 * 8 + c // 2
+        matrices.append((target == grouped).astype(F32).astype(BF16))
+    return jnp.concatenate(matrices, axis=1)
 
 
 def lane_masks():
@@ -47,27 +52,39 @@
     return (s >= SPAN - lead).astype(jnp.int32)
 
 
-def spread_rows(table, chunks):
-    for c in range(16):
-        chunks[c * 72 : c * 72 + 64, :] = table[:, c * 128 : (c + 1) * 128].astype(F32)
+def spread(rows, n, scattered):
+    scattered[pl.ds(n // 2 * PITCH + n % 2, 64, stride=2), :] = rows
+
+
+def gather(scattered, row):
+    return [scattered[pl.ds(2 * row + odd, 8, stride=PITCH), :] for odd in range(2)]
 
 
 def group_rows(chunks, g):
-    pieces = [chunks[pl.ds(g * 4 + j, 16, stride=72), :] for j in range(4)]
+    pieces = [piece for j in range(4) for piece in gather(chunks, g * 4 + j)]
     return jnp.concatenate(pieces, axis=0).astype(BF16)
 
 
-def block_weights(rows, masks):
+def order_weights(rows, masks):
     rolled = [rows] + [pltpu.roll(rows, 32 * r, 1) for r in (1, 2, 3)]
     pieces = []
     for j in range(2):
         for a in range(4):
-            first, second = j, 2 + j
             pieces.append(
-                rolled[(first - a) % 4][first * 16 : (first + 1) * 16] * masks[first]
-                + rolled[(second - a) % 4][second * 16 : (second + 1) * 16] * masks[second]
+                rolled[(j - a) % 4][j * 16 : (j + 1) * 16] * masks[j]
+                + rolled[(j + 2 - a) % 4][(j + 2) * 16 : (j + 3) * 16] * masks[j + 2]
             )
     return jnp.concatenate(pieces, axis=0)
+
+
+def block_weights(rows, masks, place):
+    blocks = []
+    for j in range(2):
+        for a in range(4):
+            block = rows[j * 16 : (j + 1) * 16] * masks[a] + rows[(j + 2) * 16 : (j + 3) * 16] * masks[(a + 2) % 4]
+            shift = (place - a) % 4
+            blocks.append(pltpu.roll(block, 32 * shift, 1) if shift else block)
+    return blocks
 
 
 def swap_lane_groups(parts, lane_group):
@@ -83,8 +100,8 @@
 
 
 def synth_kernel(
-    blocks_hbm, coef_hbm, leg_hbm, out_ref, weights_hbm,
-    blocks_ref, sem_b, coef, leg, sem_c, sem_l, sem_w, chunks_even, chunks_odd, weights_even, weights_odd, values_even, values_odd, acc, turned,
+    blocks_hbm, coef_hbm, leg_hbm, out_ref,
+    blocks_ref, sem_b, coef, leg, sem_c, sem_l, chunks_even, chunks_odd, parts_even, parts_odd, weights_even, weights_odd, values_even, values_odd, acc, turned,
 ):
     def fetch(n):
         first, count = BATCHES[n]
@@ -101,78 +118,62 @@
     order.start()
     acc[...] = jnp.zeros_like(acc)
     masks = lane_masks()
-    perm = lane_permutation()
-    lower = lax.broadcasted_iota(jnp.int32, (24, 128), 1) < 64
-
-    def prepare(s, chunks, weights, values):
-        spread_rows(leg.at[s], chunks)
+    perm = lane_permutation()[:, :128]
+    lower = lax.broadcasted_iota(jnp.int32, (32, 128), 1) < 64
+    parts_even[...] = jnp.zeros_like(parts_even)
+    parts_odd[...] = jnp.zeros_like(parts_odd)
+
+    def prepare(s, chunks, parts, weights, values):
+        for c in range(16):
+            spread(leg[s, :, c * 128 : (c + 1) * 128].astype(F32), c, chunks)
         for g in range(GROUPS):
-            weights[g] = block_weights(group_rows(chunks, g), masks)
-        rows = jnp.concatenate(
-            [coef[:, s, :, g * 256 : (g + 1) * 256].reshape(24, 256) for g in range(GROUPS)], axis=0
-        )
-        rows = jnp.dot(rows, perm, preferred_element_type=F32)
+            weights[g] = order_weights(group_rows(chunks, g), masks)
+        rows = jnp.dot(coef[:, s].reshape(12 * 64, 128), perm, preferred_element_type=F32)
+        for k in range(12):
+            spread(rows[k * 64 : (k + 1) * 64], k, parts)
         for g in range(GROUPS):
-            part = rows[g * 24 : (g + 1) * 24]
-            values[g * 48 : (g + 1) * 48, :] = jnp.concatenate([part[:, :128], part[:, 128:]], axis=0).astype(BF16)
+            pieces = [piece for n in range(4) for piece in gather(parts, g * 4 + n)]
+            values[g * 64 : (g + 1) * 64, :] = jnp.concatenate(pieces, axis=0).astype(BF16)
 
     def combine(s, weights, values):
-        base = own_block(blocks_ref, s) * (GROUPS * 24)
+        base = own_block(blocks_ref, s) * (GROUPS * 40)
         for g in range(GROUPS):
-            term = jnp.dot(values[g * 48 : (g + 1) * 48, :], weights[g], preferred_element_type=F32)
-            where = pl.ds(pl.multiple_of(base + g * 24, 8), 24)
-            acc[where, :] = acc[where, :] + jnp.where(lower, term[:24], term[24:])
+            term = jnp.dot(values[g * 64 : (g + 1) * 64, :], weights[g], preferred_element_type=F32)
+            where = pl.ds(pl.multiple_of(base + g * 40, 8), 32)
+            acc[where, :] = acc[where, :] + jnp.where(lower, term[:32], term[32:])
 
     def arrive(n):
         for copy in fetch(n):
             copy.wait()
 
-    def keep_even(t):
-        return pltpu.make_async_copy(weights_even.at[t], weights_hbm.at[2 * t], sem_w.at[2 * t])
-
-    def keep_odd(t):
-        return pltpu.make_async_copy(weights_odd.at[t], weights_hbm.at[2 * t + 1], sem_w.at[2 * t + 1])
-
     arrive(0)
     order.wait()
-    prepare(0, chunks_even, weights_even.at[0], values_even)
+    prepare(0, chunks_even, parts_even, weights_even, values_even)
 
     def pair(t, carry):
-        keep_even(t).start()
         for n in range(1, len(BATCHES)):
             pl.when(2 * t + 1 == BATCHES[n][0])(functools.partial(arrive, n))
-        prepare(2 * t + 1, chunks_odd, weights_odd.at[t], values_odd)
-        combine(2 * t, weights_even.at[t], values_even)
-        prepare(2 * t + 2, chunks_even, weights_even.at[t + 1], values_even)
-        combine(2 * t + 1, weights_odd.at[t], values_odd)
-        keep_odd(t).start()
+        prepare(2 * t + 1, chunks_odd, parts_odd, weights_odd, values_odd)
+        combine(2 * t, weights_even, values_even)
+        prepare(2 * t + 2, chunks_even, parts_even, weights_even, values_even)
+        combine(2 * t + 1, weights_odd, values_odd)
         return carry
 
     lax.fori_loop(0, SLOTS // 2, pair, 0)
-    last = SLOTS // 2
-    keep_even(last).start()
-    combine(SLOTS - 1, weights_even.at[last], values_even)
+    combine(SLOTS - 1, weights_even, values_even)
     for comp in range(3):
         for i in range(2):
             parts = []
             for part in range(2):
                 for vm in range(2):
-                    row = ((vm * 3 + comp) * 2 + part) * 2 + i
-                    parts.append(acc[pl.ds(row, 2 * GROUPS, stride=24), :])
+                    row = i * 16 + part * 8 + vm * 3 + comp
+                    parts.append(acc[pl.ds(row, 2 * GROUPS, stride=40), :])
             turned[comp * 2 + i] = jnp.concatenate(parts, axis=0).T
     for d in range(8):
         for j in range(4):
             pieces = [turned[n, pl.ds(j * 32 + d, 4, stride=8), :] for n in range(6)]
             out_ref[d, j] = jnp.concatenate(pieces, axis=0).astype(BF16)
 
-    def finish(t, carry):
-        keep_even(t).wait()
-        keep_odd(t).wait()
-        return carry
-
-    lax.fori_loop(0, last, finish, 0)
-    keep_even(last).wait()
-
 
 def in_hbm(x):
     return pltpu.with_memory_space_constraint(x, pltpu.HBM)
@@ -182,26 +183,24 @@
     return pl.pallas_call(
         synth_kernel,
         in_specs=[pl.BlockSpec(memory_space=pltpu.HBM)] * 3,
-        out_specs=[pl.BlockSpec(memory_space=pltpu.VMEM), pl.BlockSpec(memory_space=pltpu.HBM)],
-        out_shape=[
-            jax.ShapeDtypeStruct((8, 4, 24, 128), BF16),
-            pltpu.HBM((SLOTS, GROUPS, 128, 128), BF16),
-        ],
+        out_specs=pl.BlockSpec(memory_space=pltpu.VMEM),
+        out_shape=jax.ShapeDtypeStruct((8, 4, 24, 128), BF16),
         scratch_shapes=[
             pltpu.SMEM((16,), jnp.int32),
             pltpu.SemaphoreType.DMA,
-            pltpu.VMEM((12, SLOTS, 2, 4096), BF16),
+            pltpu.VMEM((12, SLOTS, 64, 128), BF16),
             pltpu.VMEM((SLOTS, 64, 2048), BF16),
             pltpu.SemaphoreType.DMA((len(BATCHES),)),
             pltpu.SemaphoreType.DMA((len(BATCHES),)),
-            pltpu.SemaphoreType.DMA((SLOTS,)),
-            pltpu.VMEM((16 * 72, 128), F32),
-            pltpu.VMEM((16 * 72, 128), F32),
-            pltpu.VMEM((SLOTS // 2 + 1, GROUPS, 128, 128), BF16),
-            pltpu.VMEM((SLOTS // 2, GROUPS, 128, 128), BF16),
-            pltpu.VMEM((GROUPS * 48, 128), BF16),
-            pltpu.VMEM((GROUPS * 48, 128), BF16),
-            pltpu.VMEM((2 * GROUPS * 24, 128), F32),
+            pltpu.VMEM((8 * PITCH, 128), F32),
+            pltpu.VMEM((8 * PITCH, 128), F32),
+            pltpu.VMEM((8 * PITCH, 128), F32),
+            pltpu.VMEM((8 * PITCH, 128), F32),
+            pltpu.VMEM((GROUPS, 128, 128), BF16),
+            pltpu.VMEM((GROUPS, 128, 128), BF16),
+            pltpu.VMEM((GROUPS * 64, 128), BF16),
+            pltpu.VMEM((GROUPS * 64, 128), BF16),
+            pltpu.VMEM((2 * GROUPS * 40, 128), F32),
             pltpu.VMEM((6, 128, 128), F32),
         ],
         compiler_params=pltpu.CompilerParams(vmem_limit_bytes=60 * 2**20),
@@ -309,11 +308,11 @@
     )(m_blocks, lat_weights, received, table)
 
 
-def turn_kernel(first, weights_hbm, out_hbm, weights, turned, sem_in, sem_out):
+def turn_kernel(first, leg_hbm, out_hbm, leg, chunks, turned, sem_in, sem_out):
     count = turned.shape[0]
 
     def fetch(s):
-        return pltpu.make_async_copy(weights_hbm.at[first + s], weights.at[s], sem_in.at[s])
+        return pltpu.make_async_copy(leg_hbm.at[first + s], leg.at[s], sem_in.at[s])
 
     def leave(s):
         return pltpu.make_async_copy(turned.at[s], out_hbm.at[s], sem_out.at[s])
@@ -323,18 +322,19 @@
         return carry
 
     lax.fori_loop(0, count, start, 0)
-    perm = lane_permutation(back=True)[:128, :128]
+    perm = lane_permutation(back=True)
+    masks = lane_masks()
 
     def slot(s, carry):
         fetch(s).wait()
+        for c in range(16):
+            spread(leg[s, :, c * 128 : (c + 1) * 128].astype(F32), c, chunks)
         for g in range(0, GROUPS, 2):
-            one, two = weights[s, g], weights[s, g + 1]
-            both = jnp.concatenate(
-                [one[:64] + pltpu.roll(two[:64], 32, 1), pltpu.roll(one[64:], 96, 1) + two[64:]], axis=0
-            )
+            blocks = [block_weights(group_rows(chunks, g + n), masks, n) for n in range(2)]
+            both = jnp.concatenate([one + two for one, two in zip(*blocks)], axis=0)
             both = lax.dot_general(both, perm, (((0,), (0,)), ((), ())), preferred_element_type=F32)
             for n in range(2):
-                rows = [both[(u * 2 + n) * 32 : (u * 2 + n + 1) * 32] for u in range(2)]
+                rows = [both[(u * 2 + n) * 32 : (u * 2 + n + 1) * 32, u * 128 : (u + 1) * 128] for u in range(2)]
                 turned[s, g + n] = jnp.concatenate(rows, axis=0).astype(BF16)
         leave(s).start()
         return carry
@@ -348,7 +348,7 @@
     lax.fori_loop(0, count, finish, 0)
 
 
-def turn(weights, first, count):
+def turn(legendre, first, count):
     shape = (count, GROUPS, 64, 128)
     return pl.pallas_call(
         functools.partial(turn_kernel, first),
@@ -356,17 +356,18 @@
         out_specs=pl.BlockSpec(memory_space=pltpu.HBM),
         out_shape=pltpu.HBM(shape, BF16),
         scratch_shapes=[
-            pltpu.VMEM((count, GROUPS, 128, 128), BF16),
+            pltpu.VMEM((count, 64, 2048), BF16),
+            pltpu.VMEM((8 * PITCH, 128), F32),
             pltpu.VMEM(shape, BF16),
             pltpu.SemaphoreType.DMA((count,)),
             pltpu.SemaphoreType.DMA((count,)),
         ],
-        compiler_params=pltpu.CompilerParams(vmem_limit_bytes=32 * 2**20),
+        compiler_params=pltpu.CompilerParams(vmem_limit_bytes=60 * 2**20),
         cost_estimate=pl.CostEstimate(
             flops=2 * count * GROUPS * 128**3, bytes_accessed=4 * count * GROUPS * 128**2, transcendentals=0
         ),
         name="turn",
-    )(in_hbm(weights))
+    )(in_hbm(legendre))
 
 
 def analysis_kernel(blocks_hbm, *refs, count):
@@ -501,15 +502,21 @@
     )(in_hbm(m_blocks), *messages, *(in_hbm(w) if plain else pltpu.with_memory_space_constraint(w, pltpu.VMEM) for w in weights))
 
 
+def rows_of(coeffs):
+    split = coeffs.reshape(2, 12, SLOTS, 32, 128)
+    return split.transpose(1, 2, 3, 0, 4).reshape(12, SLOTS, 64, 128)
+
+
 def local(coeffs, legendre, lat_weights, m_blocks):
     table = jnp.asarray(quarter_table(), BF16)
-    sent, weights = synthesis(m_blocks, coeffs.transpose(1, 2, 0, 3), legendre)
-    first = turn(weights, 0, 9)
+    sent = synthesis(m_blocks, rows_of(coeffs), legendre)
+    sent, legendre = lax.optimization_barrier((sent, legendre))
+    first = turn(legendre, 0, 9)
     received = lax.all_to_all(sent, "ma", split_axis=0, concat_axis=0, tiled=True)
-    received, first, weights = lax.optimization_barrier((received, first, weights))
+    received, first, legendre = lax.optimization_barrier((received, first, legendre))
     sent_back = azimuth(m_blocks, lat_weights, received, table)
-    sent_back, weights = lax.optimization_barrier((sent_back, weights))
-    second = turn(weights, 9, 8)
+    sent_back, legendre = lax.optimization_barrier((sent_back, legendre))
+    second = turn(legendre, 9, 8)
     own = lax.all_to_all(sent_back, "ma", split_axis=0, concat_axis=0, tiled=True)
     own, second = lax.optimization_barrier((own, second))
     count = lax.axis_size("row")

time: 62.6 us -> 58.5 us (0.935)
  the two profiles are of different devices: /device:TPU:1 before, /device:TPU:6 now
where the time goes in v6:
time: 58.5 us; the launch traced here: 57.7 us
  Pallas kernels  33.1 us (57%)
  starting transfers between devices  16.9 us (29%)
  waiting for transfers between devices  6.95 us (12%)
  between operations  0.7 us (1%)
    pallas_call x2, Pallas kernels, turn(): pl.pallas_call(functools.partial(turn_kernel, first), in_specs=[pl.BlockS...  13.7 us
    pallas_call x2, Pallas kernels, analysis(): pl.pallas_call(functools.partial(analysis_kernel, count=count), in_specs=...  8.78 us
    all_to_all x1, starting transfers between devices, local(): lax.all_to_all(sent, 'ma', split_axis=0, concat_axis=0, tiled=True)  8.48 us
    pallas_call x1, Pallas kernels, synthesis(): pl.pallas_call(synth_kernel, in_specs=[pl.BlockSpec(memory_space=pltpu.HB...  7.63 us
    ppermute x1, starting transfers between devices, local(): lax.ppermute(own, 'row', [((r + 1) % count, r) for r in range(count)])  4.02 us
    all_to_all x1, waiting for transfers between devices, local(): lax.all_to_all(sent, 'ma', split_axis=0, concat_axis=0, tiled=True)  3.81 us
    all_to_all x1, starting transfers between devices, local(): lax.all_to_all(sent_back, 'ma', split_axis=0, concat_axis=0, tiled=True)  3.41 us
    all_to_all x1, waiting for transfers between devices, local(): lax.all_to_all(sent_back, 'ma', split_axis=0, concat_axis=0, tiled=True)  3.14 us
  transfers between devices with their start and end apart: 4, of which 2 were waited for; matrix products, arithmetic and copies ran while one was open for 0% of the time, Pallas kernels for 32%

profile of v6, /device:TPU:6, one launch (start us, length us, event | category | flops | bytes accessed | tf_op | source)
XLA Modules:
  0.0 57.7 jit_solution(6814514126431906343)
XLA Ops:
  0.6 7.6 %synthesis.1 = bf16[8,4,24,128]{3,2,1,0:T(8,128)(2,1)} custom-call(s32[16]{0:T(128)} %blocks_hbm.5, bf16[12,17,64,128]{3,2,1,0:T(8,128)(2,1)} %bitcast.7, bf16[17,64,2048]{2,1,0:T(8,128)(2,1)} %leg_hbm.3), custom_call_target="tpu_custom_call" | custom-call | tf_op jit(solution)/shard_map/synthesis/pallas_call | solution.py:183
  8.3 8.5 %all-to-all-start = ((bf16[8,4,24,128]{3,2,1,0:T(8,128)(2,1)}), bf16[8,4,24,128]{3,2,1,0:T(8,128)(2,1)S(1)}, u32[]{:S(2)}, u32[]{:S(2)}) async-start(bf16[8,4,24,128]{3,2,1,0:T(8,128)(2,1)} %synthesis.1), calls=%async_computation | async-start | bytes 393216 | tf_op jit(solution)/shard_map/all_to_all | solution.py:515
  16.7 0.0 copy-start
  16.7 0.0 copy-start.1
  16.8 0.0 copy-start.2
  16.8 7.2 %turn.2.refs_1_ = bf16[9,16,64,128]{3,2,1,0:T(8,128)(2,1)} custom-call(bf16[17,64,2048]{2,1,0:T(8,128)(2,1)} %leg_hbm.3), custom_call_target="tpu_custom_call" | custom-call | flops 603979776 | bytes 9437184 | tf_op jit(solution)/shard_map/turn/pallas_call | solution.py:353
  24.0 3.8 %all-to-all-done.in_ref = bf16[8,4,24,128]{3,2,1,0:T(8,128)(2,1)S(1)} async-done(((bf16[8,4,24,128]{3,2,1,0:T(8,128)(2,1)}), bf16[8,4,24,128]{3,2,1,0:T(8,128)(2,1)S(1)}, u32[]{:S(2)}, u32[]{:S(2)}) %all-to-all-start) | async-done | bytes 196640 | tf_op jit(solution)/shard_map/all_to_all | solution.py:515
  27.8 0.0 copy-done
  27.8 0.0 copy-done.1
  27.8 0.0 copy-done.2
  27.8 3.0 %azimuth.1 = bf16[8,64,128]{2,1,0:T(8,128)(2,1)} custom-call(s32[16]{0:T(128)S(1)} %copy-done.1, f32[32]{0:T(128)S(1)} %copy-done.2, bf16[8,4,24,128]{3,2,1,0:T(8,128)(2,1)S(1)} %all-to-all-done.in_ref, bf16[2,4,256,768]{3,2,1,0:T(8,128)(2,1)S(1)} %copy-done), custom_call_target="tpu_custom_call" | custom-call | tf_op jit(solution)/shard_map/azimuth/pallas_call | solution.py:294
  30.8 3.4 %all-to-all-start.1 = ((bf16[8,64,128]{2,1,0:T(8,128)(2,1)}), bf16[8,64,128]{2,1,0:T(8,128)(2,1)S(1)}, u32[]{:S(2)}, u32[]{:S(2)}) async-start(bf16[8,64,128]{2,1,0:T(8,128)(2,1)} %azimuth.1), calls=%async_computation.1 | async-start | bytes 262144 | tf_op jit(solution)/shard_map/all_to_all | solution.py:520
  34.2 6.5 %turn.3.refs_2_ = bf16[8,16,64,128]{3,2,1,0:T(8,128)(2,1)} custom-call(bf16[17,64,2048]{2,1,0:T(8,128)(2,1)} %leg_hbm.3), custom_call_target="tpu_custom_call" | custom-call | flops 536870912 | bytes 8388608 | tf_op jit(solution)/shard_map/turn/pallas_call | solution.py:353
  40.7 3.1 %all-to-all-done.1.refs_0_ = bf16[8,64,128]{2,1,0:T(8,128)(2,1)S(1)} async-done(((bf16[8,64,128]{2,1,0:T(8,128)(2,1)}), bf16[8,64,128]{2,1,0:T(8,128)(2,1)S(1)}, u32[]{:S(2)}, u32[]{:S(2)}) %all-to-all-start.1) | async-done | bytes 131104 | tf_op jit(solution)/shard_map/all_to_all | solution.py:520
  43.8 1.0 %collective-permute-start = (bf16[8,64,128]{2,1,0:T(8,128)(2,1)S(1)}, bf16[8,64,128]{2,1,0:T(8,128)(2,1)S(1)}, u32[]{:S(2)}, u32[]{:S(2)}) collective-permute-start(bf16[8,64,128]{2,1,0:T(8,128)(2,1)S(1)} %all-to-all-done.1.refs_0_), channel_id=1, source_target_pairs={{0,8},{8,16},{16,24},{24,32},{32,40},{40,48},{48,56},{56,64},{64,7... | collective-permute-start | bytes 393224 | tf_op jit(solution)/shard_map/ppermute | solution.py:523
  44.8 4.0 %collective-permute-start.1 = (bf16[8,64,128]{2,1,0:T(8,128)(2,1)S(1)}, bf16[8,64,128]{2,1,0:T(8,128)(2,1)S(1)}, u32[]{:S(2)}, u32[]{:S(2)}) collective-permute-start(bf16[8,64,128]{2,1,0:T(8,128)(2,1)S(1)} %all-to-all-done.1.refs_0_), channel_id=1, source_target_pairs={{8,0},{16,8},{24,16},{32,24},{40,32},{48,40},{56,48},{64,56},{72,6... | collective-permute-start | bytes 393224 | tf_op jit(solution)/shard_map/ppermute | solution.py:524
  48.8 4.7 %plain.1 = (bf16[2,17,8,4096]{3,2,1,0:T(8,128)(2,1)}, bf16[17,16,64,128]{3,2,1,0:T(8,128)(2,1)S(1)}) custom-call(s32[16]{0:T(128)} %blocks_hbm.5, bf16[8,64,128]{2,1,0:T(8,128)(2,1)S(1)} %all-to-all-done.1.refs_0_, bf16[9,16,64,128]{3,2,1,0:T(8,128)(2,1)} %turn.2.refs_1_, bf16[8,16,64,128]{3,2,1,0:T(8,128)(2,1)} %turn.3.refs_2_), custom_call_target="tpu_custom_call" | custom-call | flops 285212672 | bytes 12582912 | tf_op jit(solution)/shard_map/plain/pallas_call | solution.py:482
  53.6 0.0 collective-permute-done.refs_1_
  53.6 0.0 collective-permute-done.1.refs_2_
  53.6 4.1 %slope.1 = bf16[2,17,8,4096]{3,2,1,0:T(8,128)(2,1)} custom-call(s32[16]{0:T(128)} %blocks_hbm.5, bf16[8,64,128]{2,1,0:T(8,128)(2,1)S(1)} %all-to-all-done.1.refs_0_, bf16[8,64,128]{2,1,0:T(8,128)(2,1)S(1)} %collective-permute-done.refs_1_, bf16[8,64,128]{2,1,0:T(8,128)(2,1)S(1)} %collective-permute-done.1.refs_2_, ...), custom_call_target="tpu_custom_call" | custom-call | flops 285212672 | bytes 12582912 | tf_op jit(solution)/shard_map/slope/pallas_call | solution.py:482
Async XLA Ops:
  8.3 19.5 %all-to-all-start = ((bf16[8,4,24,128]{3,2,1,0:T(8,128)(2,1)}), bf16[8,4,24,128]{3,2,1,0:T(8,128)(2,1)S(1)}, u32[]{:S(2)}, u32[]{:S(2)}) async-start(bf16[8,4,24,128]{3,2,1,0:T(8,128)(2,1)} %synthesis.1), calls=%async_computation | async-start | bytes 393216 | tf_op jit(solution)/shard_map/all_to_all | solution.py:515
  16.7 11.1 %copy-start = (bf16[2,4,256,768]{3,2,1,0:T(8,128)(2,1)S(1)}, bf16[2,4,256,768]{3,2,1,0:T(8,128)(2,1)}, u32[]{:S(2)}) copy-start(bf16[2,4,256,768]{3,2,1,0:T(8,128)(2,1)} %constant.2.clone.table) | copy-start | bytes 9437188
  16.7 11.0 %copy-start.1 = (s32[16]{0:T(128)S(1)}, s32[16]{0:T(128)}, u32[]{:S(2)}) copy-start(s32[16]{0:T(128)} %blocks_hbm.5) | copy-start | bytes 196
  16.8 11.0 %copy-start.2 = (f32[32]{0:T(128)S(1)}, f32[32]{0:T(128)}, u32[]{:S(2)}) copy-start(f32[32]{0:T(128)} %weights_ref.1) | copy-start | bytes 388
  30.8 13.0 %all-to-all-start.1 = ((bf16[8,64,128]{2,1,0:T(8,128)(2,1)}), bf16[8,64,128]{2,1,0:T(8,128)(2,1)S(1)}, u32[]{:S(2)}, u32[]{:S(2)}) async-start(bf16[8,64,128]{2,1,0:T(8,128)(2,1)} %azimuth.1), calls=%async_computation.1 | async-start | bytes 262144 | tf_op jit(solution)/shard_map/all_to_all | solution.py:520
  43.8 9.7 %collective-permute-start = (bf16[8,64,128]{2,1,0:T(8,128)(2,1)S(1)}, bf16[8,64,128]{2,1,0:T(8,128)(2,1)S(1)}, u32[]{:S(2)}, u32[]{:S(2)}) collective-permute-start(bf16[8,64,128]{2,1,0:T(8,128)(2,1)S(1)} %all-to-all-done.1.refs_0_), channel_id=1, source_target_pairs={{0,8},{8,16},{16,24},{24,32},{32,40},{40,48},{48,56},{56,64},{64,7... | collective-permute-start | bytes 393224 | tf_op jit(solution)/shard_map/ppermute | solution.py:523
  44.8 8.7 %collective-permute-start.1 = (bf16[8,64,128]{2,1,0:T(8,128)(2,1)S(1)}, bf16[8,64,128]{2,1,0:T(8,128)(2,1)S(1)}, u32[]{:S(2)}, u32[]{:S(2)}) collective-permute-start(bf16[8,64,128]{2,1,0:T(8,128)(2,1)S(1)} %all-to-all-done.1.refs_0_), channel_id=1, source_target_pairs={{8,0},{16,8},{24,16},{32,24},{40,32},{48,40},{56,48},{64,56},{72,6... | collective-permute-start | bytes 393224 | tf_op jit(solution)/shard_map/ppermute | solution.py:524

commit v7 on v6

--- a/solution.py
+++ b/solution.py
@@ -12,11 +12,12 @@
 F32, BF16 = jnp.float32, jnp.bfloat16
 POINTS = 3072
 QUARTER = POINTS // 4
+EIGHTH = POINTS // 8
 SLOTS = 17
 GROUPS = 16
 SPAN = 16
 PITCH = 132
-BATCHES = ((0, 1), (1, 2), (3, 6), (9, 8))
+BATCHES = ((0, 1), (1, 2), (3, 2), (5, 4), (9, 8))
 
 
 def lane_permutation(back=False):
@@ -35,16 +36,16 @@
     return [(group == j).astype(F32).astype(BF16) for j in range(4)]
 
 
-def quarter_table():
+def eighth_table():
     j = np.arange(4)[:, None, None, None]
     b = np.arange(16)[None, :, None, None]
     g = np.arange(16)[None, None, :, None]
-    x = np.arange(QUARTER)[None, None, None, :]
+    x = np.arange(EIGHTH)[None, None, None, :]
     order = b * 64 + g * 4 + j
     turns = (order * (2 * x + 1)) % (2 * POINTS)
     angles = turns * (math.pi / POINTS)
     table = np.stack([np.cos(angles), np.sin(angles)])
-    return table.reshape(2, 4, 256, QUARTER)
+    return table.reshape(2, 4, 256, EIGHTH)
 
 
 def own_block(blocks_ref, s):
@@ -223,11 +224,16 @@
     def basis(part, j):
         return jnp.concatenate([table[part, j, pl.ds(start, 16), :] for start in starts], axis=0)
 
-    for part, refs in ((0, (even_c, odd_c)), (1, (even_s, odd_s))):
-        for parity in range(2):
-            refs[parity][...] = jnp.dot(
-                left[parity][part], basis(part, parity), preferred_element_type=F32
-            ) + jnp.dot(left[parity + 2][part], basis(part, parity + 2), preferred_element_type=F32)
+    near, far = slice(0, EIGHTH), slice(EIGHTH, QUARTER)
+    for part, ref in ((0, even_c), (1, even_s)):
+        zero, two = (jnp.dot(left[j][part], basis(part, j), preferred_element_type=F32) for j in (0, 2))
+        ref[:, near] = zero + two
+        ref[:, far] = zero - two if part == 0 else two - zero
+    both = [jnp.concatenate(left[j], axis=0) for j in (1, 3)]
+    for part, here, there in ((0, odd_c, odd_s), (1, odd_s, odd_c)):
+        one, three = (jnp.dot(both[n], basis(part, 2 * n + 1), preferred_element_type=F32) for n in range(2))
+        here[:, near] = (one + three)[part * 48 : (part + 1) * 48]
+        there[:, far] = (one - three)[(1 - part) * 48 : (2 - part) * 48]
     for x in range(QUARTER // 128):
         cols = slice(x * 128, (x + 1) * 128)
         fields = [[], [], [], []]
@@ -261,20 +267,30 @@
             folds[2].append(left_odd + right_odd)
             folds[3].append(left_odd - right_odd)
         for n in range(4):
-            folded[n, :, cols] = jnp.concatenate(folds[n], axis=0).astype(BF16)
+            folded[n, :, cols] = jnp.concatenate(folds[n], axis=0)
     row = lax.broadcasted_iota(jnp.int32, (8, 1), 0) % 4
     own = lax.axis_index("ma")
     weight = jnp.zeros((8, 1), F32)
     for t in range(4):
         weight = jnp.where(row == t, weights_ref[t * 8 + own], weight)
     lane_group = lax.broadcasted_iota(jnp.int32, (8, 128), 1) // 32
+    def back(rows, part, j):
+        return lax.dot_general(
+            rows.astype(BF16), basis(part, j), (((1,), (1,)), ((), ())), preferred_element_type=F32
+        )
+
     for j in range(4):
-        terms = [
-            lax.dot_general(
-                folded[part * 2 + j % 2], basis(part, j), (((1,), (1,)), ((), ())), preferred_element_type=F32
-            )
-            for part in range(2)
-        ]
+        c_near, c_far = folded[j % 2, :, near], folded[j % 2, :, far]
+        s_near, s_far = folded[2 + j % 2, :, near], folded[2 + j % 2, :, far]
+        if j == 0:
+            terms = [back(c_near + c_far, 0, j), back(s_near - s_far, 1, j)]
+        elif j == 2:
+            terms = [back(c_near - c_far, 0, j), back(s_near + s_far, 1, j)]
+        else:
+            sign = 1.0 if j == 1 else -1.0
+            total = back(jnp.concatenate([c_near, sign * s_far], axis=0), 0, j)
+            total = total + back(jnp.concatenate([sign * c_far, s_near], axis=0), 1, j)
+            terms = [total[:32], total[32:]]
         for gh in range(2):
             for h in range(2):
                 parts = []
@@ -301,7 +317,7 @@
             grid_shape,
             grid_shape,
             grid_shape,
-            pltpu.VMEM((4, 32, QUARTER), BF16),
+            pltpu.VMEM((4, 32, QUARTER), F32),
         ],
         compiler_params=pltpu.CompilerParams(vmem_limit_bytes=32 * 2**20),
         name="azimuth",
@@ -508,7 +524,7 @@
 
 
 def local(coeffs, legendre, lat_weights, m_blocks):
-    table = jnp.asarray(quarter_table(), BF16)
+    table = jnp.asarray(eighth_table(), BF16)
     sent = synthesis(m_blocks, rows_of(coeffs), legendre)
     sent, legendre = lax.optimization_barrier((sent, legendre))
     first = turn(legendre, 0, 9)

time: 58.5 us -> 57.7 us (0.986)
  Pallas kernels: 33.1 us -> 32.2 us
where the time goes in v7:
time: 57.7 us; the launch traced here: 56.8 us
  Pallas kernels  32.2 us (56%)
  starting transfers between devices  16.9 us (29%)
  waiting for transfers between devices  6.98 us (12%)
  between operations  0.7 us (1%)
    pallas_call x2, Pallas kernels, turn(): pl.pallas_call(functools.partial(turn_kernel, first), in_specs=[pl.BlockS...  13.6 us
    pallas_call x2, Pallas kernels, analysis(): pl.pallas_call(functools.partial(analysis_kernel, count=count), in_specs=...  8.78 us
    all_to_all x1, starting transfers between devices, local(): lax.all_to_all(sent, 'ma', split_axis=0, concat_axis=0, tiled=True)  8.48 us
    pallas_call x1, Pallas kernels, synthesis(): pl.pallas_call(synth_kernel, in_specs=[pl.BlockSpec(memory_space=pltpu.HB...  7.39 us
    ppermute x1, starting transfers between devices, local(): lax.ppermute(own, 'row', [((r + 1) % count, r) for r in range(count)])  4.02 us
    all_to_all x1, waiting for transfers between devices, local(): lax.all_to_all(sent, 'ma', split_axis=0, concat_axis=0, tiled=True)  3.85 us
    all_to_all x1, starting transfers between devices, local(): lax.all_to_all(sent_back, 'ma', split_axis=0, concat_axis=0, tiled=True)  3.38 us
    all_to_all x1, waiting for transfers between devices, local(): lax.all_to_all(sent_back, 'ma', split_axis=0, concat_axis=0, tiled=True)  3.13 us
  transfers between devices with their start and end apart: 4, of which 2 were waited for; matrix products, arithmetic and copies ran while one was open for 0% of the time, Pallas kernels for 32%

profile of v7, /device:TPU:6, one launch (start us, length us, event | category | flops | bytes accessed | tf_op | source)
XLA Modules:
  0.0 56.8 jit_solution(5064730590167167205)
XLA Ops:
  0.6 7.4 %synthesis.1 = bf16[8,4,24,128]{3,2,1,0:T(8,128)(2,1)} custom-call(s32[16]{0:T(128)} %blocks_hbm.5, bf16[12,17,64,128]{3,2,1,0:T(8,128)(2,1)} %bitcast.7, bf16[17,64,2048]{2,1,0:T(8,128)(2,1)} %leg_hbm.3), custom_call_target="tpu_custom_call" | custom-call | tf_op jit(solution)/shard_map/synthesis/pallas_call | solution.py:184
  8.0 8.5 %all-to-all-start = ((bf16[8,4,24,128]{3,2,1,0:T(8,128)(2,1)}), bf16[8,4,24,128]{3,2,1,0:T(8,128)(2,1)S(1)}, u32[]{:S(2)}, u32[]{:S(2)}) async-start(bf16[8,4,24,128]{3,2,1,0:T(8,128)(2,1)} %synthesis.1), calls=%async_computation | async-start | bytes 393216 | tf_op jit(solution)/shard_map/all_to_all | solution.py:531
  16.5 0.0 copy-start
  16.5 0.0 copy-start.1
  16.5 0.0 copy-start.2
  16.5 7.2 %turn.2.refs_1_ = bf16[9,16,64,128]{3,2,1,0:T(8,128)(2,1)} custom-call(bf16[17,64,2048]{2,1,0:T(8,128)(2,1)} %leg_hbm.3), custom_call_target="tpu_custom_call" | custom-call | flops 603979776 | bytes 9437184 | tf_op jit(solution)/shard_map/turn/pallas_call | solution.py:369
  23.7 3.8 %all-to-all-done.in_ref = bf16[8,4,24,128]{3,2,1,0:T(8,128)(2,1)S(1)} async-done(((bf16[8,4,24,128]{3,2,1,0:T(8,128)(2,1)}), bf16[8,4,24,128]{3,2,1,0:T(8,128)(2,1)S(1)}, u32[]{:S(2)}, u32[]{:S(2)}) %all-to-all-start) | async-done | bytes 196640 | tf_op jit(solution)/shard_map/all_to_all | solution.py:531
  27.6 0.0 copy-done
  27.6 0.0 copy-done.1
  27.6 0.0 copy-done.2
  27.6 2.4 %azimuth.1 = bf16[8,64,128]{2,1,0:T(8,128)(2,1)} custom-call(s32[16]{0:T(128)S(1)} %copy-done.1, f32[32]{0:T(128)S(1)} %copy-done.2, bf16[8,4,24,128]{3,2,1,0:T(8,128)(2,1)S(1)} %all-to-all-done.in_ref, bf16[2,4,256,384]{3,2,1,0:T(8,128)(2,1)S(1)} %copy-done), custom_call_target="tpu_custom_call" | custom-call | tf_op jit(solution)/shard_map/azimuth/pallas_call | solution.py:310
  30.0 3.4 %all-to-all-start.1 = ((bf16[8,64,128]{2,1,0:T(8,128)(2,1)}), bf16[8,64,128]{2,1,0:T(8,128)(2,1)S(1)}, u32[]{:S(2)}, u32[]{:S(2)}) async-start(bf16[8,64,128]{2,1,0:T(8,128)(2,1)} %azimuth.1), calls=%async_computation.1 | async-start | bytes 262144 | tf_op jit(solution)/shard_map/all_to_all | solution.py:536
  33.4 6.5 %turn.3.refs_2_ = bf16[8,16,64,128]{3,2,1,0:T(8,128)(2,1)} custom-call(bf16[17,64,2048]{2,1,0:T(8,128)(2,1)} %leg_hbm.3), custom_call_target="tpu_custom_call" | custom-call | flops 536870912 | bytes 8388608 | tf_op jit(solution)/shard_map/turn/pallas_call | solution.py:369
  39.8 3.1 %all-to-all-done.1.refs_0_ = bf16[8,64,128]{2,1,0:T(8,128)(2,1)S(1)} async-done(((bf16[8,64,128]{2,1,0:T(8,128)(2,1)}), bf16[8,64,128]{2,1,0:T(8,128)(2,1)S(1)}, u32[]{:S(2)}, u32[]{:S(2)}) %all-to-all-start.1) | async-done | bytes 131104 | tf_op jit(solution)/shard_map/all_to_all | solution.py:536
  43.0 1.0 %collective-permute-start = (bf16[8,64,128]{2,1,0:T(8,128)(2,1)S(1)}, bf16[8,64,128]{2,1,0:T(8,128)(2,1)S(1)}, u32[]{:S(2)}, u32[]{:S(2)}) collective-permute-start(bf16[8,64,128]{2,1,0:T(8,128)(2,1)S(1)} %all-to-all-done.1.refs_0_), channel_id=1, source_target_pairs={{0,8},{8,16},{16,24},{24,32},{32,40},{40,48},{48,56},{56,64},{64,7... | collective-permute-start | bytes 393224 | tf_op jit(solution)/shard_map/ppermute | solution.py:539
  44.0 4.0 %collective-permute-start.1 = (bf16[8,64,128]{2,1,0:T(8,128)(2,1)S(1)}, bf16[8,64,128]{2,1,0:T(8,128)(2,1)S(1)}, u32[]{:S(2)}, u32[]{:S(2)}) collective-permute-start(bf16[8,64,128]{2,1,0:T(8,128)(2,1)S(1)} %all-to-all-done.1.refs_0_), channel_id=1, source_target_pairs={{8,0},{16,8},{24,16},{32,24},{40,32},{48,40},{56,48},{64,56},{72,6... | collective-permute-start | bytes 393224 | tf_op jit(solution)/shard_map/ppermute | solution.py:540
  48.0 4.7 %plain.1 = (bf16[2,17,8,4096]{3,2,1,0:T(8,128)(2,1)}, bf16[17,16,64,128]{3,2,1,0:T(8,128)(2,1)S(1)}) custom-call(s32[16]{0:T(128)} %blocks_hbm.5, bf16[8,64,128]{2,1,0:T(8,128)(2,1)S(1)} %all-to-all-done.1.refs_0_, bf16[9,16,64,128]{3,2,1,0:T(8,128)(2,1)} %turn.2.refs_1_, bf16[8,16,64,128]{3,2,1,0:T(8,128)(2,1)} %turn.3.refs_2_), custom_call_target="tpu_custom_call" | custom-call | flops 285212672 | bytes 12582912 | tf_op jit(solution)/shard_map/plain/pallas_call | solution.py:498
  52.7 0.0 collective-permute-done.refs_1_
  52.7 0.0 collective-permute-done.1.refs_2_
  52.7 4.1 %slope.1 = bf16[2,17,8,4096]{3,2,1,0:T(8,128)(2,1)} custom-call(s32[16]{0:T(128)} %blocks_hbm.5, bf16[8,64,128]{2,1,0:T(8,128)(2,1)S(1)} %all-to-all-done.1.refs_0_, bf16[8,64,128]{2,1,0:T(8,128)(2,1)S(1)} %collective-permute-done.refs_1_, bf16[8,64,128]{2,1,0:T(8,128)(2,1)S(1)} %collective-permute-done.1.refs_2_, ...), custom_call_target="tpu_custom_call" | custom-call | flops 285212672 | bytes 12582912 | tf_op jit(solution)/shard_map/slope/pallas_call | solution.py:498
Async XLA Ops:
  8.0 19.5 %all-to-all-start = ((bf16[8,4,24,128]{3,2,1,0:T(8,128)(2,1)}), bf16[8,4,24,128]{3,2,1,0:T(8,128)(2,1)S(1)}, u32[]{:S(2)}, u32[]{:S(2)}) async-start(bf16[8,4,24,128]{3,2,1,0:T(8,128)(2,1)} %synthesis.1), calls=%async_computation | async-start | bytes 393216 | tf_op jit(solution)/shard_map/all_to_all | solution.py:531
  16.5 11.1 %copy-start = (bf16[2,4,256,384]{3,2,1,0:T(8,128)(2,1)S(1)}, bf16[2,4,256,384]{3,2,1,0:T(8,128)(2,1)}, u32[]{:S(2)}) copy-start(bf16[2,4,256,384]{3,2,1,0:T(8,128)(2,1)} %constant.2.clone.table) | copy-start | bytes 4718596
  16.5 11.0 %copy-start.1 = (s32[16]{0:T(128)S(1)}, s32[16]{0:T(128)}, u32[]{:S(2)}) copy-start(s32[16]{0:T(128)} %blocks_hbm.5) | copy-start | bytes 196
  16.5 11.0 %copy-start.2 = (f32[32]{0:T(128)S(1)}, f32[32]{0:T(128)}, u32[]{:S(2)}) copy-start(f32[32]{0:T(128)} %weights_ref.1) | copy-start | bytes 388
  30.0 13.0 %all-to-all-start.1 = ((bf16[8,64,128]{2,1,0:T(8,128)(2,1)}), bf16[8,64,128]{2,1,0:T(8,128)(2,1)S(1)}, u32[]{:S(2)}, u32[]{:S(2)}) async-start(bf16[8,64,128]{2,1,0:T(8,128)(2,1)} %azimuth.1), calls=%async_computation.1 | async-start | bytes 262144 | tf_op jit(solution)/shard_map/all_to_all | solution.py:536
  43.0 9.7 %collective-permute-start = (bf16[8,64,128]{2,1,0:T(8,128)(2,1)S(1)}, bf16[8,64,128]{2,1,0:T(8,128)(2,1)S(1)}, u32[]{:S(2)}, u32[]{:S(2)}) collective-permute-start(bf16[8,64,128]{2,1,0:T(8,128)(2,1)S(1)} %all-to-all-done.1.refs_0_), channel_id=1, source_target_pairs={{0,8},{8,16},{16,24},{24,32},{32,40},{40,48},{48,56},{56,64},{64,7... | collective-permute-start | bytes 393224 | tf_op jit(solution)/shard_map/ppermute | solution.py:539
  44.0 8.7 %collective-permute-start.1 = (bf16[8,64,128]{2,1,0:T(8,128)(2,1)S(1)}, bf16[8,64,128]{2,1,0:T(8,128)(2,1)S(1)}, u32[]{:S(2)}, u32[]{:S(2)}) collective-permute-start(bf16[8,64,128]{2,1,0:T(8,128)(2,1)S(1)} %all-to-all-done.1.refs_0_), channel_id=1, source_target_pairs={{8,0},{16,8},{24,16},{32,24},{40,32},{48,40},{56,48},{64,56},{72,6... | collective-permute-start | bytes 393224 | tf_op jit(solution)/shard_map/ppermute | solution.py:540

commit v8 on v7

--- a/solution.py
+++ b/solution.py
@@ -396,7 +396,7 @@
     order.start()
     if count == 1:
         split = first_hbm.shape[0]
-        batches = ((first_hbm, 0, 0, 2), (first_hbm, 2, 2, split - 2), (second_hbm, 0, split, SLOTS - split))
+        batches = ((first_hbm, 0, 0, 4), (first_hbm, 4, 4, split - 4), (second_hbm, 0, split, SLOTS - split))
     else:
         batches = ()
 
@@ -474,14 +474,16 @@
 
     def pair(t, carry):
         for n in range(len(batches)):
-            need = batches[n][2] // 2
+            need = batches[n][2] // 4
             pl.when(t == need)(lambda n=n: fetch(n).wait())
-        slot(2 * t)
-        slot(2 * t + 1)
-        leave(2 * t, 2)
+        slot(4 * t)
+        slot(4 * t + 1)
+        slot(4 * t + 2)
+        slot(4 * t + 3)
+        leave(4 * t, 4)
         return carry
 
-    lax.fori_loop(0, SLOTS // 2, pair, 0)
+    lax.fori_loop(0, SLOTS // 4, pair, 0)
     slot(SLOTS - 1)
     leave(SLOTS - 1, 1)
     for copy in send(0, SLOTS):

time: 57.7 us -> 56.5 us (0.979)
  Pallas kernels: 32.2 us -> 31 us
    pallas_call x2, Pallas kernels: 8.78 us -> 7.6 us  [analysis(): pl.pallas_call(functools.partial(analysis_kernel, count=count), in_specs=...]
where the time goes in v8:
time: 56.5 us; the launch traced here: 55.6 us
  Pallas kernels  31 us (55%)
  starting transfers between devices  16.9 us (30%)
  waiting for transfers between devices  6.98 us (12%)
  between operations  0.71 us (1%)
    pallas_call x2, Pallas kernels, turn(): pl.pallas_call(functools.partial(turn_kernel, first), in_specs=[pl.BlockS...  13.6 us
    all_to_all x1, starting transfers between devices, local(): lax.all_to_all(sent, 'ma', split_axis=0, concat_axis=0, tiled=True)  8.48 us
    pallas_call x2, Pallas kernels, analysis(): pl.pallas_call(functools.partial(analysis_kernel, count=count), in_specs=...  7.6 us
    pallas_call x1, Pallas kernels, synthesis(): pl.pallas_call(synth_kernel, in_specs=[pl.BlockSpec(memory_space=pltpu.HB...  7.39 us
    ppermute x1, starting transfers between devices, local(): lax.ppermute(own, 'row', [((r + 1) % count, r) for r in range(count)])  4.02 us
    all_to_all x1, waiting for transfers between devices, local(): lax.all_to_all(sent, 'ma', split_axis=0, concat_axis=0, tiled=True)  3.85 us
    all_to_all x1, starting transfers between devices, local(): lax.all_to_all(sent_back, 'ma', split_axis=0, concat_axis=0, tiled=True)  3.38 us
    all_to_all x1, waiting for transfers between devices, local(): lax.all_to_all(sent_back, 'ma', split_axis=0, concat_axis=0, tiled=True)  3.13 us
  transfers between devices with their start and end apart: 4, of which 2 were waited for; matrix products, arithmetic and copies ran while one was open for 0% of the time, Pallas kernels for 32%

profile of v8, /device:TPU:6, one launch (start us, length us, event | category | flops | bytes accessed | tf_op | source)
XLA Modules:
  0.0 55.6 jit_solution(7463540437358718749)
XLA Ops:
  0.6 7.4 %synthesis.1 = bf16[8,4,24,128]{3,2,1,0:T(8,128)(2,1)} custom-call(s32[16]{0:T(128)} %blocks_hbm.5, bf16[12,17,64,128]{3,2,1,0:T(8,128)(2,1)} %bitcast.7, bf16[17,64,2048]{2,1,0:T(8,128)(2,1)} %leg_hbm.3), custom_call_target="tpu_custom_call" | custom-call | tf_op jit(solution)/shard_map/synthesis/pallas_call | solution.py:184
  8.0 8.5 %all-to-all-start = ((bf16[8,4,24,128]{3,2,1,0:T(8,128)(2,1)}), bf16[8,4,24,128]{3,2,1,0:T(8,128)(2,1)S(1)}, u32[]{:S(2)}, u32[]{:S(2)}) async-start(bf16[8,4,24,128]{3,2,1,0:T(8,128)(2,1)} %synthesis.1), calls=%async_computation | async-start | bytes 393216 | tf_op jit(solution)/shard_map/all_to_all | solution.py:533
  16.5 0.0 copy-start
  16.5 0.0 copy-start.1
  16.5 0.0 copy-start.2
  16.5 7.2 %turn.2.refs_1_ = bf16[9,16,64,128]{3,2,1,0:T(8,128)(2,1)} custom-call(bf16[17,64,2048]{2,1,0:T(8,128)(2,1)} %leg_hbm.3), custom_call_target="tpu_custom_call" | custom-call | flops 603979776 | bytes 9437184 | tf_op jit(solution)/shard_map/turn/pallas_call | solution.py:369
  23.7 3.8 %all-to-all-done.in_ref = bf16[8,4,24,128]{3,2,1,0:T(8,128)(2,1)S(1)} async-done(((bf16[8,4,24,128]{3,2,1,0:T(8,128)(2,1)}), bf16[8,4,24,128]{3,2,1,0:T(8,128)(2,1)S(1)}, u32[]{:S(2)}, u32[]{:S(2)}) %all-to-all-start) | async-done | bytes 196640 | tf_op jit(solution)/shard_map/all_to_all | solution.py:533
  27.6 0.0 copy-done
  27.6 0.0 copy-done.1
  27.6 0.0 copy-done.2
  27.6 2.4 %azimuth.1 = bf16[8,64,128]{2,1,0:T(8,128)(2,1)} custom-call(s32[16]{0:T(128)S(1)} %copy-done.1, f32[32]{0:T(128)S(1)} %copy-done.2, bf16[8,4,24,128]{3,2,1,0:T(8,128)(2,1)S(1)} %all-to-all-done.in_ref, bf16[2,4,256,384]{3,2,1,0:T(8,128)(2,1)S(1)} %copy-done), custom_call_target="tpu_custom_call" | custom-call | tf_op jit(solution)/shard_map/azimuth/pallas_call | solution.py:310
  30.0 3.4 %all-to-all-start.1 = ((bf16[8,64,128]{2,1,0:T(8,128)(2,1)}), bf16[8,64,128]{2,1,0:T(8,128)(2,1)S(1)}, u32[]{:S(2)}, u32[]{:S(2)}) async-start(bf16[8,64,128]{2,1,0:T(8,128)(2,1)} %azimuth.1), calls=%async_computation.1 | async-start | bytes 262144 | tf_op jit(solution)/shard_map/all_to_all | solution.py:538
  33.4 6.5 %turn.3.refs_2_ = bf16[8,16,64,128]{3,2,1,0:T(8,128)(2,1)} custom-call(bf16[17,64,2048]{2,1,0:T(8,128)(2,1)} %leg_hbm.3), custom_call_target="tpu_custom_call" | custom-call | flops 536870912 | bytes 8388608 | tf_op jit(solution)/shard_map/turn/pallas_call | solution.py:369
  39.8 3.1 %all-to-all-done.1.refs_0_ = bf16[8,64,128]{2,1,0:T(8,128)(2,1)S(1)} async-done(((bf16[8,64,128]{2,1,0:T(8,128)(2,1)}), bf16[8,64,128]{2,1,0:T(8,128)(2,1)S(1)}, u32[]{:S(2)}, u32[]{:S(2)}) %all-to-all-start.1) | async-done | bytes 131104 | tf_op jit(solution)/shard_map/all_to_all | solution.py:538
  43.0 1.0 %collective-permute-start = (bf16[8,64,128]{2,1,0:T(8,128)(2,1)S(1)}, bf16[8,64,128]{2,1,0:T(8,128)(2,1)S(1)}, u32[]{:S(2)}, u32[]{:S(2)}) collective-permute-start(bf16[8,64,128]{2,1,0:T(8,128)(2,1)S(1)} %all-to-all-done.1.refs_0_), channel_id=1, source_target_pairs={{0,8},{8,16},{16,24},{24,32},{32,40},{40,48},{48,56},{56,64},{64,7... | collective-permute-start | bytes 393224 | tf_op jit(solution)/shard_map/ppermute | solution.py:541
  44.0 4.0 %collective-permute-start.1 = (bf16[8,64,128]{2,1,0:T(8,128)(2,1)S(1)}, bf16[8,64,128]{2,1,0:T(8,128)(2,1)S(1)}, u32[]{:S(2)}, u32[]{:S(2)}) collective-permute-start(bf16[8,64,128]{2,1,0:T(8,128)(2,1)S(1)} %all-to-all-done.1.refs_0_), channel_id=1, source_target_pairs={{8,0},{16,8},{24,16},{32,24},{40,32},{48,40},{56,48},{64,56},{72,6... | collective-permute-start | bytes 393224 | tf_op jit(solution)/shard_map/ppermute | solution.py:542
  48.0 4.1 %plain.1 = (bf16[2,17,8,4096]{3,2,1,0:T(8,128)(2,1)}, bf16[17,16,64,128]{3,2,1,0:T(8,128)(2,1)S(1)}) custom-call(s32[16]{0:T(128)} %blocks_hbm.5, bf16[8,64,128]{2,1,0:T(8,128)(2,1)S(1)} %all-to-all-done.1.refs_0_, bf16[9,16,64,128]{3,2,1,0:T(8,128)(2,1)} %turn.2.refs_1_, bf16[8,16,64,128]{3,2,1,0:T(8,128)(2,1)} %turn.3.refs_2_), custom_call_target="tpu_custom_call" | custom-call | flops 285212672 | bytes 12582912 | tf_op jit(solution)/shard_map/plain/pallas_call | solution.py:500
  52.1 0.0 collective-permute-done.refs_1_
  52.1 0.0 collective-permute-done.1.refs_2_
  52.1 3.5 %slope.1 = bf16[2,17,8,4096]{3,2,1,0:T(8,128)(2,1)} custom-call(s32[16]{0:T(128)} %blocks_hbm.5, bf16[8,64,128]{2,1,0:T(8,128)(2,1)S(1)} %all-to-all-done.1.refs_0_, bf16[8,64,128]{2,1,0:T(8,128)(2,1)S(1)} %collective-permute-done.refs_1_, bf16[8,64,128]{2,1,0:T(8,128)(2,1)S(1)} %collective-permute-done.1.refs_2_, ...), custom_call_target="tpu_custom_call" | custom-call | flops 285212672 | bytes 12582912 | tf_op jit(solution)/shard_map/slope/pallas_call | solution.py:500
Async XLA Ops:
  8.0 19.5 %all-to-all-start = ((bf16[8,4,24,128]{3,2,1,0:T(8,128)(2,1)}), bf16[8,4,24,128]{3,2,1,0:T(8,128)(2,1)S(1)}, u32[]{:S(2)}, u32[]{:S(2)}) async-start(bf16[8,4,24,128]{3,2,1,0:T(8,128)(2,1)} %synthesis.1), calls=%async_computation | async-start | bytes 393216 | tf_op jit(solution)/shard_map/all_to_all | solution.py:533
  16.5 11.1 %copy-start = (bf16[2,4,256,384]{3,2,1,0:T(8,128)(2,1)S(1)}, bf16[2,4,256,384]{3,2,1,0:T(8,128)(2,1)}, u32[]{:S(2)}) copy-start(bf16[2,4,256,384]{3,2,1,0:T(8,128)(2,1)} %constant.2.clone.table) | copy-start | bytes 4718596
  16.5 11.0 %copy-start.1 = (s32[16]{0:T(128)S(1)}, s32[16]{0:T(128)}, u32[]{:S(2)}) copy-start(s32[16]{0:T(128)} %blocks_hbm.5) | copy-start | bytes 196
  16.5 11.0 %copy-start.2 = (f32[32]{0:T(128)S(1)}, f32[32]{0:T(128)}, u32[]{:S(2)}) copy-start(f32[32]{0:T(128)} %weights_ref.1) | copy-start | bytes 388
  30.0 13.0 %all-to-all-start.1 = ((bf16[8,64,128]{2,1,0:T(8,128)(2,1)}), bf16[8,64,128]{2,1,0:T(8,128)(2,1)S(1)}, u32[]{:S(2)}, u32[]{:S(2)}) async-start(bf16[8,64,128]{2,1,0:T(8,128)(2,1)} %azimuth.1), calls=%async_computation.1 | async-start | bytes 262144 | tf_op jit(solution)/shard_map/all_to_all | solution.py:538
  43.0 9.2 %collective-permute-start = (bf16[8,64,128]{2,1,0:T(8,128)(2,1)S(1)}, bf16[8,64,128]{2,1,0:T(8,128)(2,1)S(1)}, u32[]{:S(2)}, u32[]{:S(2)}) collective-permute-start(bf16[8,64,128]{2,1,0:T(8,128)(2,1)S(1)} %all-to-all-done.1.refs_0_), channel_id=1, source_target_pairs={{0,8},{8,16},{16,24},{24,32},{32,40},{40,48},{48,56},{56,64},{64,7... | collective-permute-start | bytes 393224 | tf_op jit(solution)/shard_map/ppermute | solution.py:541
  44.0 8.2 %collective-permute-start.1 = (bf16[8,64,128]{2,1,0:T(8,128)(2,1)S(1)}, bf16[8,64,128]{2,1,0:T(8,128)(2,1)S(1)}, u32[]{:S(2)}, u32[]{:S(2)}) collective-permute-start(bf16[8,64,128]{2,1,0:T(8,128)(2,1)S(1)} %all-to-all-done.1.refs_0_), channel_id=1, source_target_pairs={{8,0},{16,8},{24,16},{32,24},{40,32},{48,40},{56,48},{64,56},{72,6... | collective-permute-start | bytes 393224 | tf_op jit(solution)/shard_map/ppermute | solution.py:542

commit v9 on v8

--- a/solution.py
+++ b/solution.py
@@ -474,16 +474,15 @@
 
     def pair(t, carry):
         for n in range(len(batches)):
-            need = batches[n][2] // 4
+            need = batches[n][2] // 8
             pl.when(t == need)(lambda n=n: fetch(n).wait())
-        slot(4 * t)
-        slot(4 * t + 1)
-        slot(4 * t + 2)
-        slot(4 * t + 3)
-        leave(4 * t, 4)
+        for n in range(8):
+            slot(8 * t + n)
+            if n % 4 == 3:
+                leave(8 * t + n - 3, 4)
         return carry
 
-    lax.fori_loop(0, SLOTS // 4, pair, 0)
+    lax.fori_loop(0, SLOTS // 8, pair, 0)
     slot(SLOTS - 1)
     leave(SLOTS - 1, 1)
     for copy in send(0, SLOTS):

time: 56.5 us -> 56.1 us (level)
  no operation moved by 1% of the time
where the time goes in v9:
time: 56.1 us; the launch traced here: 55.2 us
  Pallas kernels  30.7 us (55%)
  starting transfers between devices  16.9 us (30%)
  waiting for transfers between devices  6.98 us (12%)
  between operations  0.71 us (1%)
    pallas_call x2, Pallas kernels, turn(): pl.pallas_call(functools.partial(turn_kernel, first), in_specs=[pl.BlockS...  13.6 us
    all_to_all x1, starting transfers between devices, local(): lax.all_to_all(sent, 'ma', split_axis=0, concat_axis=0, tiled=True)  8.48 us
    pallas_call x1, Pallas kernels, synthesis(): pl.pallas_call(synth_kernel, in_specs=[pl.BlockSpec(memory_space=pltpu.HB...  7.39 us
    pallas_call x2, Pallas kernels, analysis(): pl.pallas_call(functools.partial(analysis_kernel, count=count), in_specs=...  7.22 us
    ppermute x1, starting transfers between devices, local(): lax.ppermute(own, 'row', [((r + 1) % count, r) for r in range(count)])  4.02 us
    all_to_all x1, waiting for transfers between devices, local(): lax.all_to_all(sent, 'ma', split_axis=0, concat_axis=0, tiled=True)  3.85 us
    all_to_all x1, starting transfers between devices, local(): lax.all_to_all(sent_back, 'ma', split_axis=0, concat_axis=0, tiled=True)  3.38 us
    all_to_all x1, waiting for transfers between devices, local(): lax.all_to_all(sent_back, 'ma', split_axis=0, concat_axis=0, tiled=True)  3.13 us
  transfers between devices with their start and end apart: 4, of which 2 were waited for; matrix products, arithmetic and copies ran while one was open for 0% of the time, Pallas kernels for 32%

profile of v9, /device:TPU:6, one launch (start us, length us, event | category | flops | bytes accessed | tf_op | source)
XLA Modules:
  0.0 55.2 jit_solution(380858767992514041)
XLA Ops:
  0.6 7.4 %synthesis.1 = bf16[8,4,24,128]{3,2,1,0:T(8,128)(2,1)} custom-call(s32[16]{0:T(128)} %blocks_hbm.5, bf16[12,17,64,128]{3,2,1,0:T(8,128)(2,1)} %bitcast.7, bf16[17,64,2048]{2,1,0:T(8,128)(2,1)} %leg_hbm.3), custom_call_target="tpu_custom_call" | custom-call | tf_op jit(solution)/shard_map/synthesis/pallas_call | solution.py:184
  8.0 8.5 %all-to-all-start = ((bf16[8,4,24,128]{3,2,1,0:T(8,128)(2,1)}), bf16[8,4,24,128]{3,2,1,0:T(8,128)(2,1)S(1)}, u32[]{:S(2)}, u32[]{:S(2)}) async-start(bf16[8,4,24,128]{3,2,1,0:T(8,128)(2,1)} %synthesis.1), calls=%async_computation | async-start | bytes 393216 | tf_op jit(solution)/shard_map/all_to_all | solution.py:532
  16.5 0.0 copy-start
  16.5 0.0 copy-start.1
  16.5 0.0 copy-start.2
  16.5 7.2 %turn.2.refs_1_ = bf16[9,16,64,128]{3,2,1,0:T(8,128)(2,1)} custom-call(bf16[17,64,2048]{2,1,0:T(8,128)(2,1)} %leg_hbm.3), custom_call_target="tpu_custom_call" | custom-call | flops 603979776 | bytes 9437184 | tf_op jit(solution)/shard_map/turn/pallas_call | solution.py:369
  23.7 3.8 %all-to-all-done.in_ref = bf16[8,4,24,128]{3,2,1,0:T(8,128)(2,1)S(1)} async-done(((bf16[8,4,24,128]{3,2,1,0:T(8,128)(2,1)}), bf16[8,4,24,128]{3,2,1,0:T(8,128)(2,1)S(1)}, u32[]{:S(2)}, u32[]{:S(2)}) %all-to-all-start) | async-done | bytes 196640 | tf_op jit(solution)/shard_map/all_to_all | solution.py:532
  27.6 0.0 copy-done
  27.6 0.0 copy-done.1
  27.6 0.0 copy-done.2
  27.6 2.4 %azimuth.1 = bf16[8,64,128]{2,1,0:T(8,128)(2,1)} custom-call(s32[16]{0:T(128)S(1)} %copy-done.1, f32[32]{0:T(128)S(1)} %copy-done.2, bf16[8,4,24,128]{3,2,1,0:T(8,128)(2,1)S(1)} %all-to-all-done.in_ref, bf16[2,4,256,384]{3,2,1,0:T(8,128)(2,1)S(1)} %copy-done), custom_call_target="tpu_custom_call" | custom-call | tf_op jit(solution)/shard_map/azimuth/pallas_call | solution.py:310
  30.0 3.4 %all-to-all-start.1 = ((bf16[8,64,128]{2,1,0:T(8,128)(2,1)}), bf16[8,64,128]{2,1,0:T(8,128)(2,1)S(1)}, u32[]{:S(2)}, u32[]{:S(2)}) async-start(bf16[8,64,128]{2,1,0:T(8,128)(2,1)} %azimuth.1), calls=%async_computation.1 | async-start | bytes 262144 | tf_op jit(solution)/shard_map/all_to_all | solution.py:537
  33.4 6.5 %turn.3.refs_2_ = bf16[8,16,64,128]{3,2,1,0:T(8,128)(2,1)} custom-call(bf16[17,64,2048]{2,1,0:T(8,128)(2,1)} %leg_hbm.3), custom_call_target="tpu_custom_call" | custom-call | flops 536870912 | bytes 8388608 | tf_op jit(solution)/shard_map/turn/pallas_call | solution.py:369
  39.8 3.1 %all-to-all-done.1.refs_0_ = bf16[8,64,128]{2,1,0:T(8,128)(2,1)S(1)} async-done(((bf16[8,64,128]{2,1,0:T(8,128)(2,1)}), bf16[8,64,128]{2,1,0:T(8,128)(2,1)S(1)}, u32[]{:S(2)}, u32[]{:S(2)}) %all-to-all-start.1) | async-done | bytes 131104 | tf_op jit(solution)/shard_map/all_to_all | solution.py:537
  43.0 1.0 %collective-permute-start = (bf16[8,64,128]{2,1,0:T(8,128)(2,1)S(1)}, bf16[8,64,128]{2,1,0:T(8,128)(2,1)S(1)}, u32[]{:S(2)}, u32[]{:S(2)}) collective-permute-start(bf16[8,64,128]{2,1,0:T(8,128)(2,1)S(1)} %all-to-all-done.1.refs_0_), channel_id=1, source_target_pairs={{0,8},{8,16},{16,24},{24,32},{32,40},{40,48},{48,56},{56,64},{64,7... | collective-permute-start | bytes 393224 | tf_op jit(solution)/shard_map/ppermute | solution.py:540
  44.0 4.0 %collective-permute-start.1 = (bf16[8,64,128]{2,1,0:T(8,128)(2,1)S(1)}, bf16[8,64,128]{2,1,0:T(8,128)(2,1)S(1)}, u32[]{:S(2)}, u32[]{:S(2)}) collective-permute-start(bf16[8,64,128]{2,1,0:T(8,128)(2,1)S(1)} %all-to-all-done.1.refs_0_), channel_id=1, source_target_pairs={{8,0},{16,8},{24,16},{32,24},{40,32},{48,40},{56,48},{64,56},{72,6... | collective-permute-start | bytes 393224 | tf_op jit(solution)/shard_map/ppermute | solution.py:541
  48.0 4.0 %plain.1 = (bf16[2,17,8,4096]{3,2,1,0:T(8,128)(2,1)}, bf16[17,16,64,128]{3,2,1,0:T(8,128)(2,1)S(1)}) custom-call(s32[16]{0:T(128)} %blocks_hbm.5, bf16[8,64,128]{2,1,0:T(8,128)(2,1)S(1)} %all-to-all-done.1.refs_0_, bf16[9,16,64,128]{3,2,1,0:T(8,128)(2,1)} %turn.2.refs_1_, bf16[8,16,64,128]{3,2,1,0:T(8,128)(2,1)} %turn.3.refs_2_), custom_call_target="tpu_custom_call" | custom-call | flops 285212672 | bytes 12582912 | tf_op jit(solution)/shard_map/plain/pallas_call | solution.py:499
  52.0 0.0 collective-permute-done.refs_1_
  52.1 0.0 collective-permute-done.1.refs_2_
  52.1 3.2 %slope.1 = bf16[2,17,8,4096]{3,2,1,0:T(8,128)(2,1)} custom-call(s32[16]{0:T(128)} %blocks_hbm.5, bf16[8,64,128]{2,1,0:T(8,128)(2,1)S(1)} %all-to-all-done.1.refs_0_, bf16[8,64,128]{2,1,0:T(8,128)(2,1)S(1)} %collective-permute-done.refs_1_, bf16[8,64,128]{2,1,0:T(8,128)(2,1)S(1)} %collective-permute-done.1.refs_2_, ...), custom_call_target="tpu_custom_call" | custom-call | flops 285212672 | bytes 12582912 | tf_op jit(solution)/shard_map/slope/pallas_call | solution.py:499
Async XLA Ops:
  8.0 19.5 %all-to-all-start = ((bf16[8,4,24,128]{3,2,1,0:T(8,128)(2,1)}), bf16[8,4,24,128]{3,2,1,0:T(8,128)(2,1)S(1)}, u32[]{:S(2)}, u32[]{:S(2)}) async-start(bf16[8,4,24,128]{3,2,1,0:T(8,128)(2,1)} %synthesis.1), calls=%async_computation | async-start | bytes 393216 | tf_op jit(solution)/shard_map/all_to_all | solution.py:532
  16.5 11.1 %copy-start = (bf16[2,4,256,384]{3,2,1,0:T(8,128)(2,1)S(1)}, bf16[2,4,256,384]{3,2,1,0:T(8,128)(2,1)}, u32[]{:S(2)}) copy-start(bf16[2,4,256,384]{3,2,1,0:T(8,128)(2,1)} %constant.2.clone.table) | copy-start | bytes 4718596
  16.5 11.0 %copy-start.1 = (s32[16]{0:T(128)S(1)}, s32[16]{0:T(128)}, u32[]{:S(2)}) copy-start(s32[16]{0:T(128)} %blocks_hbm.5) | copy-start | bytes 196
  16.5 11.0 %copy-start.2 = (f32[32]{0:T(128)S(1)}, f32[32]{0:T(128)}, u32[]{:S(2)}) copy-start(f32[32]{0:T(128)} %weights_ref.1) | copy-start | bytes 388
  30.0 13.0 %all-to-all-start.1 = ((bf16[8,64,128]{2,1,0:T(8,128)(2,1)}), bf16[8,64,128]{2,1,0:T(8,128)(2,1)S(1)}, u32[]{:S(2)}, u32[]{:S(2)}) async-start(bf16[8,64,128]{2,1,0:T(8,128)(2,1)} %azimuth.1), calls=%async_computation.1 | async-start | bytes 262144 | tf_op jit(solution)/shard_map/all_to_all | solution.py:537
  43.0 9.1 %collective-permute-start = (bf16[8,64,128]{2,1,0:T(8,128)(2,1)S(1)}, bf16[8,64,128]{2,1,0:T(8,128)(2,1)S(1)}, u32[]{:S(2)}, u32[]{:S(2)}) collective-permute-start(bf16[8,64,128]{2,1,0:T(8,128)(2,1)S(1)} %all-to-all-done.1.refs_0_), channel_id=1, source_target_pairs={{0,8},{8,16},{16,24},{24,32},{32,40},{40,48},{48,56},{56,64},{64,7... | collective-permute-start | bytes 393224 | tf_op jit(solution)/shard_map/ppermute | solution.py:540
  44.0 8.1 %collective-permute-start.1 = (bf16[8,64,128]{2,1,0:T(8,128)(2,1)S(1)}, bf16[8,64,128]{2,1,0:T(8,128)(2,1)S(1)}, u32[]{:S(2)}, u32[]{:S(2)}) collective-permute-start(bf16[8,64,128]{2,1,0:T(8,128)(2,1)S(1)} %all-to-all-done.1.refs_0_), channel_id=1, source_target_pairs={{8,0},{16,8},{24,16},{32,24},{40,32},{48,40},{56,48},{64,56},{72,6... | collective-permute-start | bytes 393224 | tf_op jit(solution)/shard_map/ppermute | solution.py:541
